TPU v7x, 512 devices: a whole 4x8x8 slice. The times are simulated.
512 devices in a mesh: seq: 64 (over z, x, core), head: 8 (over y).
Axes of the slice: x: 4, y: 8, z: 8, core: 2. Of those that a mesh axis runs over, the one named last changes fastest.
Arguments:
- queries: bfloat16 [16384, 2048], P('seq', 'head'), may hold values from -40 to 40
- keys: bfloat16 [16384, 2048], P('seq', 'head'), may hold values from -40 to 40
- values: bfloat16 [16384, 2048], P('seq', 'head'), may hold values from -6 to 6
- text_keys: bfloat16 [256, 2048], P('seq', 'head'), may hold values from -6 to 6
- text_values: bfloat16 [256, 2048], P('seq', 'head'), may hold values from -6 to 6
- text_len: int32 [1], replicated, may hold values from 64 to 256
- radial_width: int32 [64, 5], replicated, may hold values from 32 to 256
- far_blocks: int32 [128, 29], replicated, may hold values from 0 to 127, as said below
- far_count: int32 [128], replicated, may hold values from 0 to 29
- w_out: bfloat16 [2048, 3072], P('head'), may hold values from -0.1875 to 0.1875
Outputs:
- mixed: bfloat16 [16384, 3072], P('seq', 'head')
Inputs may be any that keep to these rules, and one draw needn't show every extreme that they name: `far_blocks`: within the rows of one frame group's query blocks, every listed block comes from a different frame group, and none from a group g with |g - own group| <= 2; so a group asks at most one block of any other group.
All inputs are finite; a program needn't handle non-finite values.
Results may differ from a plain program's by a relative error of at most 0.0057.
Values may be sent and summed in bfloat16 or wider, within the bound.
No kernel may reach another device: no remote copies, remote signals or barrier semaphores. Data moves between devices by JAX's collectives and lax.ppermute only.
A program may use at most 128 MiB of HBM per device.

v0:
```python
import jax
import jax.numpy as jnp
from jax import lax
from jax.sharding import PartitionSpec as P

HD = 128
BLK = 128
NEAR = 2


def from_behind(block, axis, distance):
    devices = range(lax.axis_size(axis))
    route = [(i - distance, i) for i in devices if i - distance in devices]
    return lax.ppermute(block, axis, route)


def head_attention(
    query_head,
    common_key_rows,
    common_value_rows,
    collected_matcher_vectors,
    gathered_value_rows,
    full_mask,
    score_scale,
):
    block_count = collected_matcher_vectors.shape[0]
    clustered_projections = query_head.reshape(block_count, -1, query_head.shape[1])
    shared_scores = jnp.einsum(
        "grh,ch->grc", clustered_projections, common_key_rows, preferred_element_type=jnp.float32
    )
    listed_scores = jnp.einsum(
        "vwp,vtp->vwt",
        clustered_projections,
        collected_matcher_vectors,
        preferred_element_type=jnp.float32,
    )
    logit_matrix = jnp.concatenate((shared_scores, listed_scores), axis=2) * score_scale
    masked = jnp.where(full_mask, logit_matrix, -jnp.inf)
    highest = jnp.max(masked, axis=2, keepdims=True)
    exponent = jnp.where(full_mask, jnp.exp(masked - highest), 0.0)
    softmax_denominators = jnp.sum(exponent, axis=2, keepdims=True)
    attention_weight = exponent.astype(jnp.bfloat16)
    split_position = common_key_rows.shape[0]
    summed = jnp.einsum(
        "clz,zn->cln",
        attention_weight[:, :, :split_position],
        common_value_rows,
        preferred_element_type=jnp.float32,
    )
    summed = summed + jnp.einsum(
        "ley,lyv->lev",
        attention_weight[:, :, split_position:],
        gathered_value_rows,
        preferred_element_type=jnp.float32,
    )
    return (summed / softmax_denominators).astype(jnp.bfloat16).reshape(query_head.shape)


def shards(
    queries,
    keys,
    values,
    text_keys,
    text_values,
    text_len,
    radial_width,
    far_blocks,
    far_count,
    w_out,
):
    own_group = lax.axis_index("seq")
    group_count = lax.axis_size("seq")
    token_rows = queries.shape[0]
    nearby_span = queries.shape[1]
    heads_local = nearby_span // HD
    blocks_local = token_rows // BLK
    far_slots = far_blocks.shape[1]
    score_scale = HD ** (-0.5)
    stacked = jnp.stack((keys, values))
    text_both = lax.all_gather(jnp.stack((text_keys, text_values)), "seq", axis=1, tiled=True)
    below_parts = []
    above_parts = []
    for distance in range(1, NEAR + 1):
        below_parts.append(from_behind(stacked, "seq", distance))
        above_parts.append(from_behind(stacked, "seq", -distance))
    near_both = jnp.concatenate(below_parts[::-1] + [stacked] + above_parts, axis=1)
    offsets = jnp.arange(2 * NEAR + 1, dtype=jnp.int32) - NEAR
    neighbour = own_group + offsets
    present = (neighbour >= 0) & (neighbour < group_count)
    widths = lax.dynamic_index_in_dim(radial_width, own_group, 0, keepdims=False)
    positions = jnp.arange(token_rows, dtype=jnp.int32)
    distant_entries = jnp.abs(positions[:, None, None] - positions[None, None, :])
    band_mask = (distant_entries < widths[None, :, None]) & present[None, :, None]
    text_live = jnp.arange(text_both.shape[1], dtype=jnp.int32) < text_len[0]
    shared_mask = jnp.concatenate(
        (
            jnp.broadcast_to(text_live[None, :], (token_rows, text_live.shape[0])),
            band_mask.reshape(token_rows, -1),
        ),
        axis=1,
    )
    entry_table = far_blocks.reshape(group_count, blocks_local * far_slots)
    count_table = far_count.reshape(group_count, blocks_local)
    place_number = jnp.arange(far_slots, dtype=jnp.int32)
    live_table = (place_number[None, None, :] < count_table[:, :, None]).reshape(
        group_count, blocks_local * far_slots
    )
    source_table = entry_table // blocks_local
    within_table = entry_table % blocks_local
    own_sources = lax.dynamic_index_in_dim(source_table, own_group, 0, keepdims=False)
    own_live = lax.dynamic_index_in_dim(live_table, own_group, 0, keepdims=False)
    wanted = live_table & (source_table == own_group)
    wanted_within = jnp.sum(jnp.where(wanted, within_table, 0), axis=1)
    outgoing = jnp.take(stacked.reshape(2, blocks_local, BLK, nearby_span), wanted_within, axis=1)
    far_both = lax.all_to_all(outgoing, "seq", split_axis=1, concat_axis=1, tiled=True)
    listed_mask = jnp.repeat(own_live.reshape(blocks_local, far_slots), BLK, axis=1)
    full_mask = jnp.concatenate(
        (
            shared_mask.reshape(blocks_local, BLK, -1),
            jnp.broadcast_to(listed_mask[:, None, :], (blocks_local, BLK, listed_mask.shape[1])),
        ),
        axis=2,
    )
    source_grid = own_sources.reshape(blocks_local, far_slots)
    head_outputs = []
    for head_number in range(heads_local):
        columns = slice(head_number * HD, (head_number + 1) * HD)
        common_key_rows = jnp.concatenate(
            (text_both[0][:, columns], near_both[0][:, columns]), axis=0
        )
        common_value_rows = jnp.concatenate(
            (text_both[1][:, columns], near_both[1][:, columns]), axis=0
        )
        collected_matcher_vectors = jnp.take(
            far_both[0][:, :, columns], source_grid, axis=0
        ).reshape(blocks_local, far_slots * BLK, HD)
        gathered_value_rows = jnp.take(far_both[1][:, :, columns], source_grid, axis=0).reshape(
            blocks_local, far_slots * BLK, HD
        )
        head_outputs.append(
            head_attention(
                queries[:, columns],
                common_key_rows,
                common_value_rows,
                collected_matcher_vectors,
                gathered_value_rows,
                full_mask,
                score_scale,
            )
        )
    attention = jnp.concatenate(head_outputs, axis=1)
    partial_terms = jnp.dot(attention, w_out, preferred_element_type=jnp.float32)
    mixed = lax.psum_scatter(partial_terms, "head", scatter_dimension=1, tiled=True)
    return mixed.astype(jnp.bfloat16)


def solution(mesh):
    return jax.shard_map(
        shards,
        mesh=mesh,
        in_specs=(
            P("seq", "head"),
            P("seq", "head"),
            P("seq", "head"),
            P("seq", "head"),
            P("seq", "head"),
            P(),
            P(),
            P(),
            P(),
            P("head", None),
        ),
        out_specs=P("seq", "head"),
        check_vma=False,
    )
```

profile of v0, /device:TPU:1, one launch (start us, length us, event | category | flops | bytes accessed | tf_op | source)
XLA Modules:
  0.0 374.9 jit_solution(11896561036606850969)
XLA Ops:
  9.4 1.0 pad_maximum_fusion.1
  10.4 5.3 %gather_fusion = bf16[64,2,128,256]{3,2,1,0:T(8,128)(2,1)} fusion(bf16[2,2,128,256]{3,2,1,0:T(8,128)(2,1)S(1)} %pad_maximum_fusion.1, s32[1024]{0:T(1024)S(1)} %get-tuple-element.37), kind=kCustom, calls=%fused_computation.4 | custom fusion | bytes 16777472 | tf_op jit(solution)/shard_map/jit(_take)/gather | solution.py:114
  15.7 7.5 %select_bitcast_fusion = bf16[2,64,128,256]{3,2,0,1:T(8,128)(2,1)} fusion(bf16[64,2,128,256]{3,2,1,0:T(8,128)(2,1)} %gather_fusion, pred[64]{0:T(512)(128)(4,1)S(1)} %compare_and_fusion.1), kind=kLoop, calls=%fused_computation.9 | loop fusion | flops 4194304 | bytes 16777280 | tf_op jit(solution)/shard_map/jit(_take)/select_n | solution.py:114
  23.2 15.2 %all-to-all-start = ((bf16[2,64,128,256]{3,2,0,1:T(8,128)(2,1)}), bf16[2,64,128,256]{3,2,0,1:T(8,128)(2,1)}, u32[]{:S(2)}, u32[]{:S(2)}) async-start(bf16[2,64,128,256]{3,2,0,1:T(8,128)(2,1)} %select_bitcast_fusion), calls=%async_computation | async-start | bytes 16777216 | tf_op jit(solution)/shard_map/all_to_all | solution.py:115
  39.2 4.0 %collective-permute-start = (bf16[2,256,256]{2,1,0:T(8,128)(2,1)}, bf16[2,256,256]{2,1,0:T(8,128)(2,1)}, u32[]{:S(2)}, u32[]{:S(2)}) collective-permute-start(bf16[2,256,256]{2,1,0:T(8,128)(2,1)} %pad_maximum_fusion), channel_id=1, source_target_pairs={{0,16},{8,24},{16,32},{24,40},{32,48},{40,56},{48,64},{56,72},{64,... | collective-permute-start | bytes 786440 | tf_op jit(solution)/shard_map/ppermute | solution.py:14
  43.2 2.9 collective-permute-start.1
  46.2 2.1 collective-permute-start.2
  48.3 1.3 collective-permute-start.3
  50.2 1.2 lt.113
  51.4 2.0 lt.114
  54.4 210.8 %all_gather.3 = bf16[2,256,256]{2,0,1:T(2,128)(2,1)S(1)} all-gather(bf16[2,4,256]{2,0,1:T(2,128)(2,1)S(1)} %copy.40), channel_id=1, replica_groups=mesh['seq'=64,'head'=8] {'seq'}, dimensions={1}, use_global_device_ids=true | all-gather | bytes 266240 | tf_op jit(solution)/shard_map/all_gather | solution.py:80
  266.5 1.8 fusion.18
  270.5 1.0 constant_dynamic-update-slice_fusion.3
  271.5 1.0 constant_dynamic-update-slice_fusion.1
  272.5 1.0 constant_dynamic-update-slice_fusion
  273.6 1.1 fusion.60
  274.6 1.5 convolution_bitcast_fusion.3
  276.1 1.5 convolution_bitcast_fusion.2
  277.7 4.0 %slice_bitcast_fusion.1 = (bf16[64,128,256]{2,1,0:T(8,128)(2,1)S(1)}, bf16[64,128,256]{2,1,0:T(8,128)(2,1)S(1)}) fusion(bf16[2,64,128,256]{3,2,0,1:T(8,128)(2,1)} %all-to-all-done), kind=kLoop, calls=%fused_computation.22 | loop fusion | bytes 16777216 | tf_op jit(solution)/shard_map/squeeze | solution.py:135
  281.7 3.2 fusion.59
  284.8 3.2 fusion.58
  288.0 2.6 gather_fusion.2
  290.7 3.8 %gather_fusion.3 = bf16[58,128,128]{2,1,0:T(8,128)(2,1)} fusion(bf16[64,128,128]{2,1,0:T(8,128)(2,1)} %get-tuple-element.13, s32[1024]{0:T(1024)} %get-tuple-element.36), kind=kCustom, calls=%fused_computation.2.clone | custom fusion | bytes 3801320 | tf_op jit(solution)/shard_map/jit(_take)/gather | solution.py:134
  294.5 3.8 %gather_fusion.4 = bf16[58,128,128]{2,1,0:T(8,128)(2,1)} fusion(bf16[64,128,128]{2,1,0:T(8,128)(2,1)} %get-tuple-element.15, s32[1024]{0:T(1024)} %get-tuple-element.36), kind=kCustom, calls=%fused_computation.3.clone | custom fusion | bytes 3801320 | tf_op jit(solution)/shard_map/jit(_take)/gather | solution.py:137
  298.2 3.8 %gather_fusion.1 = bf16[58,128,128]{2,1,0:T(8,128)(2,1)} fusion(bf16[64,128,128]{2,1,0:T(8,128)(2,1)} %get-tuple-element.12, s32[1024]{0:T(1024)} %get-tuple-element.36), kind=kCustom, calls=%fused_computation.clone | custom fusion | bytes 3801320 | tf_op jit(solution)/shard_map/jit(_take)/gather | solution.py:134
  302.0 3.1 broadcast_select_fusion.3
  306.4 3.2 broadcast_in_dim.58
  309.7 3.0 fusion.56
  314.0 3.0 fusion.57
  319.2 2.2 fusion.33
  321.4 44.9 %reduce-scatter.2.cloned.1.call-done = f32[256,384]{1,0:T(8,128)} async-done(((f32[256,3072]{1,0:T(8,128)}), f32[256,384]{1,0:T(8,128)}) %reduce-scatter.2.cloned.1.call-update) | async-done | bytes 393232 | tf_op jit(solution)/shard_map/reduce_scatter | solution.py:153
  366.3 1.7 convert_element_type.19
  (98 shorter events, 13.0 us)
Async XLA Ops:
  6.5 312.6 %copy-start = (bf16[256,3072]{1,0:T(8,128)(2,1)S(1)}, bf16[256,3072]{1,0:T(8,128)(2,1)}, u32[]{:S(2)}) copy-start(bf16[256,3072]{1,0:T(8,128)(2,1)} %param.21) | copy-start | bytes 4718596
  8.7 0.7 copy-start.18
  23.2 15.3 %copy-start.3 = (bf16[256,256]{1,0:T(8,128)(2,1)S(1)}, bf16[256,256]{1,0:T(8,128)(2,1)}, u32[]{:S(2)}) copy-start(bf16[256,256]{1,0:T(8,128)(2,1)} %param.14) | copy-start | bytes 393220
  23.2 15.3 %copy-start.4 = (bf16[256,256]{1,0:T(8,128)(2,1)S(1)}, bf16[256,256]{1,0:T(8,128)(2,1)}, u32[]{:S(2)}) copy-start(bf16[256,256]{1,0:T(8,128)(2,1)} %param.13) | copy-start | bytes 393220
  23.2 26.4 %copy-start.15 = (s32[128]{0:T(128)S(1)}, s32[128]{0:T(128)}, u32[]{:S(2)}) copy-start(s32[128]{0:T(128)} %param.20) | copy-start | bytes 1540
  23.2 26.5 %copy-start.16 = (bf16[4,256]{1,0:T(4,128)(2,1)S(1)}, bf16[4,256]{1,0:T(4,128)(2,1)}, u32[]{:S(2)}) copy-start(bf16[4,256]{1,0:T(4,128)(2,1)} %param.16) | copy-start | bytes 6148
  23.2 26.5 %copy-start.17 = (bf16[4,256]{1,0:T(4,128)(2,1)S(1)}, bf16[4,256]{1,0:T(4,128)(2,1)}, u32[]{:S(2)}) copy-start(bf16[4,256]{1,0:T(4,128)(2,1)} %param.15) | copy-start | bytes 6148
  23.2 26.5 %copy-start.14 = (s32[64,5]{0,1:T(8,128)S(1)}, s32[64,5]{0,1:T(8,128)}, u32[]{:S(2)}) copy-start(s32[64,5]{0,1:T(8,128)} %param.18) | copy-start | bytes 3844
  23.2 254.4 %all-to-all-start = ((bf16[2,64,128,256]{3,2,0,1:T(8,128)(2,1)}), bf16[2,64,128,256]{3,2,0,1:T(8,128)(2,1)}, u32[]{:S(2)}, u32[]{:S(2)}) async-start(bf16[2,64,128,256]{3,2,0,1:T(8,128)(2,1)} %select_bitcast_fusion), calls=%async_computation | async-start | bytes 16777216 | tf_op jit(solution)/shard_map/all_to_all | solution.py:115
  38.4 327.9 %reduce-scatter.2.cloned.1.call-start = ((), (), s32[]{:S(2)}) async-start(), calls=%async_computation.2 | async-start | bytes 3538944 | tf_op jit(solution)/shard_map/reduce_scatter | solution.py:153
  39.2 230.3 %collective-permute-start = (bf16[2,256,256]{2,1,0:T(8,128)(2,1)}, bf16[2,256,256]{2,1,0:T(8,128)(2,1)}, u32[]{:S(2)}, u32[]{:S(2)}) collective-permute-start(bf16[2,256,256]{2,1,0:T(8,128)(2,1)} %pad_maximum_fusion), channel_id=1, source_target_pairs={{0,16},{8,24},{16,32},{24,40},{32,48},{40,56},{48,64},{56,72},{64,... | collective-permute-start | bytes 786440 | tf_op jit(solution)/shard_map/ppermute | solution.py:14
  43.2 227.2 %collective-permute-start.1 = (bf16[2,256,256]{2,1,0:T(8,128)(2,1)}, bf16[2,256,256]{2,1,0:T(8,128)(2,1)}, u32[]{:S(2)}, u32[]{:S(2)}) collective-permute-start(bf16[2,256,256]{2,1,0:T(8,128)(2,1)} %pad_maximum_fusion), channel_id=1, source_target_pairs={{0,8},{8,16},{16,24},{24,32},{32,40},{40,48},{48,56},{56,64},{64,7... | collective-permute-start | bytes 786440 | tf_op jit(solution)/shard_map/ppermute | solution.py:14
  46.2 225.3 %collective-permute-start.2 = (bf16[2,256,256]{2,1,0:T(8,128)(2,1)}, bf16[2,256,256]{2,1,0:T(8,128)(2,1)}, u32[]{:S(2)}, u32[]{:S(2)}) collective-permute-start(bf16[2,256,256]{2,1,0:T(8,128)(2,1)} %pad_maximum_fusion), channel_id=1, source_target_pairs={{8,0},{16,8},{24,16},{32,24},{40,32},{48,40},{56,48},{64,56},{72,6... | collective-permute-start | bytes 786440 | tf_op jit(solution)/shard_map/ppermute | solution.py:14
  48.3 224.2 %collective-permute-start.3 = (bf16[2,256,256]{2,1,0:T(8,128)(2,1)}, bf16[2,256,256]{2,1,0:T(8,128)(2,1)}, u32[]{:S(2)}, u32[]{:S(2)}) collective-permute-start(bf16[2,256,256]{2,1,0:T(8,128)(2,1)} %pad_maximum_fusion), channel_id=1, source_target_pairs={{16,0},{24,8},{32,16},{40,24},{48,32},{56,40},{64,48},{72,56},{80,... | collective-permute-start | bytes 786440 | tf_op jit(solution)/shard_map/ppermute | solution.py:14
  51.4 214.0 %copy-start.10 = (bf16[256,256]{1,0:T(8,128)(2,1)S(1)}, bf16[256,256]{1,0:T(8,128)(2,1)}, u32[]{:S(2)}) copy-start(bf16[256,256]{1,0:T(8,128)(2,1)} %param.12) | copy-start | bytes 393220
  265.4 9.3 %copy-start.5 = (bf16[256,128]{1,0:T(8,128)(2,1)}, bf16[256,128]{1,0:T(8,128)(2,1)S(1)}, u32[]{:S(2)}) copy-start(bf16[256,128]{1,0:T(8,128)(2,1)S(1)} %get-tuple-element.28) | copy-start | bytes 196612
  265.4 3.6 copy-start.19
  302.0 3.1 copy-start.6
  305.8 3.9 %copy-start.2 = (f32[2,128,1536]{1,2,0:T(8,128)S(1)}, f32[2,128,1536]{1,2,0:T(8,128)}, u32[]{:S(2)}) copy-start(f32[2,128,1536]{1,2,0:T(8,128)} %convolution_bitcast_fusion.3) | copy-start | bytes 4718596
  305.8 3.9 %copy-start.9 = (pred[2,128,1280]{1,2,0:T(8,128)(4,1)S(1)}, pred[2,128,1280]{1,2,0:T(8,128)(4,1)}, u32[]{:S(2)}) copy-start(pred[2,128,1280]{1,2,0:T(8,128)(4,1)} %fusion.18) | copy-start | bytes 983044
  305.8 3.9 %copy-start.13 = (pred[5248]{0:T(1024)(128)(4,1)S(1)}, pred[5248]{0:T(1024)(128)(4,1)}, u32[]{:S(2)}) copy-start(pred[5248]{0:T(1024)(128)(4,1)} %pad.22.clone) | copy-start | bytes 15748
  312.6 1.4 copy-start.1
  317.0 1.0 copy-start.8
  317.0 1.0 copy-start.12
  317.7 1.0 copy-start.7
  317.8 1.0 copy-start.11
Sparse Core Ops, SparseCore 0:
  321.5 44.7 reduce-scatter.1
where the time goes:
time: 377 us; the launch traced here: 375 us
  blocking collectives  211 us (56%)
  local copies, waits for them, and re-layouts  46 us (12%)
  waiting for transfers between devices  44.9 us (12%)
  starting transfers between devices  25.5 us (7%)
  other arithmetic  24.1 us (6%)
  between operations  14.5 us (4%)
  matrix products  8.89 us (2%)
    all_gather x1, blocking collectives, shards(): lax.all_gather(jnp.stack((text_keys, text_values)), 'seq', axis=1, tiled=...  211 us
    reduce_scatter x1, waiting for transfers between devices, shards(): lax.psum_scatter(partial_terms, 'head', scatter_dimension=1, tiled=True)  44.9 us
    all_to_all x1, starting transfers between devices, shards(): lax.all_to_all(outgoing, 'seq', split_axis=1, concat_axis=1, tiled=True)  15.2 us
    ppermute x4, starting transfers between devices, from_behind(): return lax.ppermute(block, axis, route)  10.3 us
    gather x2, local copies, waits for them, and re-layouts, shards(): jnp.take(far_both[0][:, :, columns], source_grid, axis=0)  7.55 us
  transfers between devices with their start and end apart: 6, of which 1 were waited for; matrix products, arithmetic and copies ran while one was open for 5% of the time, Pallas kernels for 0%

commit v1 on v0

v1 whole, which is shorter than its diff:
```python
import functools

import jax
import jax.numpy as jnp
from jax import lax
from jax.experimental import pallas as pl
from jax.experimental.pallas import tpu as pltpu
from jax.sharding import PartitionSpec as P

HD = 128
BLK = 128
NEAR = 2
ROW = 8
TPAD = 16
FAR_WIDTH = 1024
NEG = -1e30
FLOOR = -1e9
SCORE_SCALE = HD ** (-0.5) * 1.4426950408889634
EARLY = 5
EARLY_CHUNK = 4
LATE = 3
LATE_CHUNK = 2
STRIDE = 32
EARLY_AT = 2
LATE_AT = 24
HEADER = 2 * ROW * STRIDE


def row_peers():
    return [[z * ROW + r for r in range(ROW)] for z in range(ROW)]


def along_column(block, distance):
    count = ROW * ROW
    return lax.ppermute(block, "seq", [(g, (g + ROW * distance) % count) for g in range(count)])


def list_kernel(far_ref, count_ref, width_ref, len_ref, where_ref, table_ref):
    z = where_ref[0]
    r = where_ref[1]
    table_ref[HEADER] = z
    table_ref[HEADER + 1] = r
    table_ref[HEADER + 2] = len_ref[0]

    def one_group(q, _):
        group = z * ROW + q
        for a in range(2):
            qb = group * 2 + a
            base = (2 * q + a) * STRIDE
            live = count_ref[qb]
            n = jnp.int32(0)
            k = jnp.int32(0)
            for d in range(2 * NEAR + 1):
                h = group + d - NEAR
                inside = (h >= 0) & (h < ROW * ROW) & ((h & (ROW - 1)) == r)
                ahead = ((h >> 3) - z) & (ROW - 1)
                place = jnp.where(ahead == 0, 0, jnp.where(ahead == 1, 4, 2))
                code = width_ref[d, group] * 16 + place
                table_ref[base + EARLY_AT + n] = code
                table_ref[base + EARLY_AT + 1 + n] = code + 1
                n = n + jnp.where(inside, 2, 0)
            for m in range(far_ref.shape[0]):
                block = far_ref[m, qb]
                h = block >> 1
                inside = ((h & (ROW - 1)) == r) & (m < live)
                ahead = ((h >> 3) - z) & (ROW - 1)
                slot = jnp.where(ahead < ROW // 2, 2 * ahead, 2 * (ROW - ahead) - 1)
                slot = jnp.where(ahead == ROW // 2, ROW - 1, slot)
                early = inside & (slot < EARLY)
                late = inside & (slot >= EARLY)
                code = FAR_WIDTH * 16 + slot * 2 + (block & 1)
                table_ref[base + EARLY_AT + n] = code
                table_ref[base + LATE_AT + k] = code - 2 * EARLY
                n = jnp.minimum(n + jnp.where(early, 1, 0), LATE_AT - EARLY_AT - 2)
                k = jnp.minimum(k + jnp.where(late, 1, 0), STRIDE - LATE_AT - 1)
            table_ref[base] = n
            table_ref[base + 1] = k
        return 0

    lax.fori_loop(0, ROW, one_group, 0)


def rounded_top(top):
    high = top.astype(jnp.bfloat16).astype(jnp.float32)
    low = (top - high).astype(jnp.bfloat16).astype(jnp.float32)
    return high, low


def attend(table, late, q_ref, kv, text_bias, text_k, text_v, per_chunk, first_state, finish):
    rows = lax.broadcasted_iota(jnp.int32, (BLK, BLK), 0)
    cols = lax.broadcasted_iota(jnp.int32, (BLK, BLK), 1)
    offset = rows - cols

    def one_group(g, _):
        def chunk(c, states, with_text):
            work = []
            for a in range(2):
                base = (2 * g + a) * STRIDE
                items = []
                for j in range(per_chunk):
                    number = c * per_chunk + j
                    code = table[base + (LATE_AT if late else EARLY_AT) + number]
                    code = jnp.where(number < table[base + late], code, 0)
                    side = code & 1
                    live = jnp.abs(offset + (side - a) * BLK) < (code >> 4)
                    items.append(((code & 15) >> 1, pl.multiple_of(side * BLK, BLK), live))
                for h in range(2):
                    lanes = slice(h * HD, (h + 1) * HD)
                    query = q_ref[g, a * BLK : (a + 1) * BLK, lanes]
                    key_rows = [kv[w, pl.ds(s, BLK), lanes] for w, s, _ in items]
                    value_cols = [kv[w, pl.ds(s + 2 * BLK, BLK), lanes] for w, s, _ in items]
                    if with_text:
                        key_rows.append(text_k[:, lanes])
                        value_cols.append(text_v[h])
                    product = lax.dot_general(
                        jnp.concatenate(key_rows, axis=0),
                        query,
                        (((1,), (1,)), ((), ())),
                        preferred_element_type=jnp.float32,
                    )
                    work.append((product, value_cols, items))
            fresh = []
            for x, (product, value_cols, items) in enumerate(work):
                parts = []
                for j, (_, _, live) in enumerate(items):
                    s = product[j * BLK : (j + 1) * BLK] * SCORE_SCALE
                    parts.append(jnp.where(live, s, NEG))
                if with_text:
                    parts.append(product[per_chunk * BLK :] * SCORE_SCALE + text_bias[...])
                old_top, old_total, old_acc = states[x] if states is not None else (FLOOR, None, None)
                peak = [jnp.max(s, axis=0, keepdims=True) for s in parts]
                top = jnp.maximum(functools.reduce(jnp.maximum, peak), old_top)
                high, low = rounded_top(top)
                top = high + low
                weights = [jnp.exp2(s - top) for s in parts]
                total = functools.reduce(jnp.add, [jnp.sum(p, axis=0, keepdims=True) for p in weights])
                acc = jnp.dot(
                    jnp.concatenate(value_cols, axis=1),
                    jnp.concatenate([p.astype(jnp.bfloat16) for p in weights], axis=0),
                    preferred_element_type=jnp.float32,
                )
                if states is not None:
                    fade = jnp.exp2(old_top - top)
                    total = total + old_total * fade
                    acc = acc + old_acc * fade
                fresh.append((top, total, acc))
            return tuple(fresh)

        states = chunk(0, first_state(g), True)
        most = jnp.maximum(table[2 * g * STRIDE + late], table[(2 * g + 1) * STRIDE + late])
        states = lax.fori_loop(
            1, (most + per_chunk - 1) // per_chunk, lambda c, s: chunk(c, s, False), states
        )
        for a in range(2):
            finish(g, a, states[2 * a], states[2 * a + 1])
        return 0

    lax.fori_loop(0, ROW, one_group, 0)


def set_text(kv, slot_rows, text_len, text_bias, text_k, text_v):
    count = len(slot_rows)
    rows = lax.broadcasted_iota(jnp.int32, (TPAD, BLK), 0)
    for s, first in enumerate(slot_rows):
        alive = (rows < 4) & (first + rows < text_len)
        text_bias[s * TPAD : (s + 1) * TPAD, :] = jnp.where(alive, 0.0, NEG)
    text_k[...] = kv[:, 4 * BLK : 4 * BLK + TPAD, :].reshape(count * TPAD, 2 * HD)
    raw = kv[:, 4 * BLK + TPAD : 4 * BLK + 2 * TPAD, :].reshape(count * TPAD, 2 * HD)
    for h in range(2):
        text_v[h] = raw[:, h * HD : (h + 1) * HD].astype(jnp.float32).T.astype(jnp.bfloat16)


def text_rows(table, steps):
    z = table[HEADER]
    r = table[HEADER + 1]
    return [(((z + d + ROW) % ROW) * ROW + r) * 4 for d in steps]


def early_kernel(
    table, q_ref, own, f1, b1, f2, b2, acc_ref, stat_ref,
    kv, sems, text_bias, text_k, text_v,
):
    copies = [
        pltpu.make_async_copy(src, kv.at[i], sems.at[i]) for i, src in enumerate((own, f1, b1, f2, b2))
    ]
    for copy in copies:
        copy.start()
    for copy in copies:
        copy.wait()
    rows = text_rows(table, (0, -1, 1, -2, 2))
    set_text(kv, rows, table[HEADER + 2], text_bias, text_k, text_v)

    def finish(g, a, *heads):
        lanes = slice(a * BLK, (a + 1) * BLK)
        stats = []
        for h, (top, total, acc) in enumerate(heads):
            acc_ref[g, h * HD : (h + 1) * HD, lanes] = acc
            stats += [top, total]
        stats.append(jnp.zeros((4, BLK), jnp.float32))
        stat_ref[g, :, lanes] = jnp.concatenate(stats, axis=0)

    attend(
        table, 0, q_ref, kv, text_bias, text_k, text_v, EARLY_CHUNK, lambda g: None, finish
    )


def late_kernel(
    table, q_ref, f3, b3, f4, b4, acc_ref, stat_ref, out_ref,
    kv, sems, text_bias, text_k, text_v,
):
    copies = [
        pltpu.make_async_copy(f3, kv.at[0], sems.at[0]),
        pltpu.make_async_copy(b3, kv.at[1], sems.at[1]),
        pltpu.make_async_copy(f4, kv.at[2, : 2 * BLK], sems.at[2]),
        pltpu.make_async_copy(b4, kv.at[2, 2 * BLK :], sems.at[3]),
    ]
    for copy in copies:
        copy.start()
    for copy in copies:
        copy.wait()
    rows = text_rows(table, (-3, 3, 4))
    set_text(kv, rows, table[HEADER + 2], text_bias, text_k, text_v)

    def first_state(g):
        states = []
        for a in range(2):
            lanes = slice(a * BLK, (a + 1) * BLK)
            for h in range(2):
                states.append(
                    (
                        stat_ref[g, 2 * h : 2 * h + 1, lanes],
                        stat_ref[g, 2 * h + 1 : 2 * h + 2, lanes],
                        acc_ref[g, h * HD : (h + 1) * HD, lanes],
                    )
                )
        return states

    def finish(g, a, *heads):
        lanes = slice(a * BLK, (a + 1) * BLK)
        stats = []
        for h, (top, total, acc) in enumerate(heads):
            out_ref[g, h * HD : (h + 1) * HD, lanes] = acc.astype(jnp.bfloat16)
            stats += list(rounded_top(top)) + list(rounded_top(total))
        stats.append(jnp.zeros((TPAD - len(stats), BLK), jnp.float32))
        out_ref[g, 2 * HD : 2 * HD + TPAD, lanes] = jnp.concatenate(stats, axis=0).astype(jnp.bfloat16)

    attend(
        table, 1, q_ref, kv, text_bias, text_k, text_v, LATE_CHUNK, first_state, finish
    )


def merge_kernel(part_ref, out_ref):
    stats = [part_ref[i, 2 * HD : 2 * HD + TPAD, :].astype(jnp.float32) for i in range(ROW)]
    for h in range(2):
        tops = [s[4 * h : 4 * h + 1] + s[4 * h + 1 : 4 * h + 2] for s in stats]
        sums = [s[4 * h + 2 : 4 * h + 3] + s[4 * h + 3 : 4 * h + 4] for s in stats]
        top = functools.reduce(jnp.maximum, tops)
        weights = [jnp.exp2(t - top) for t in tops]
        total = functools.reduce(jnp.add, [w * s for w, s in zip(weights, sums)])
        inverse = 1.0 / total
        rows = slice(h * HD, (h + 1) * HD)
        acc = None
        for i in range(ROW):
            term = part_ref[i, rows, :].astype(jnp.float32) * weights[i]
            acc = term if acc is None else acc + term
        acc = (acc * inverse).astype(jnp.bfloat16)
        for i in range(ROW):
            out_ref[i, rows, :] = acc


def smem():
    return pl.BlockSpec(memory_space=pltpu.SMEM)


def vmem():
    return pl.BlockSpec(memory_space=pltpu.VMEM)


def anywhere():
    return pl.BlockSpec(memory_space=pl.ANY)


def kernel_params():
    return pltpu.CompilerParams(vmem_limit_bytes=32 << 20)


def attend_scratch(slots, copies):
    return [
        pltpu.VMEM((slots, 4 * BLK + 2 * TPAD, 2 * HD), jnp.bfloat16),
        pltpu.SemaphoreType.DMA((copies,)),
        pltpu.VMEM((slots * TPAD, BLK), jnp.float32),
        pltpu.VMEM((slots * TPAD, 2 * HD), jnp.bfloat16),
        pltpu.VMEM((2, HD, slots * TPAD), jnp.bfloat16),
    ]


def shards(
    queries,
    keys,
    values,
    text_keys,
    text_values,
    text_len,
    radial_width,
    far_blocks,
    far_count,
    w_out,
):
    own = lax.axis_index("seq")
    where = jnp.stack((own // ROW, own % ROW)).astype(jnp.int32)
    tokens, width = queries.shape
    heads = lax.axis_size("head")
    columns = w_out.shape[1] // heads

    turned = values.reshape(2, BLK, 2, HD).transpose(0, 3, 2, 1).reshape(tokens, width)
    pad = ((0, TPAD - text_keys.shape[0]), (0, 0))
    kv = jnp.concatenate((keys, turned, jnp.pad(text_keys, pad), jnp.pad(text_values, pad)), axis=0)
    f1 = along_column(kv, 1)
    b1 = along_column(kv, -1)
    q_all = lax.all_to_all(
        jnp.broadcast_to(queries[None], (ROW, tokens, width)), "seq", 0, 0, axis_index_groups=row_peers()
    )
    f2 = along_column(f1, 1)
    b2 = along_column(b1, -1)
    f3 = along_column(f2, 1)
    b3 = along_column(b2, -1)
    f4 = along_column(f2[: 2 * BLK], 2)
    b4 = along_column(b2[2 * BLK :], -2)

    half = lax.dynamic_slice_in_dim(w_out, (own % 2) * HD, HD, 0)
    half = half.reshape(HD, heads, columns).transpose(1, 0, 2)
    half, q_all = lax.optimization_barrier((half, q_all))
    half = lax.all_to_all(half, "head", 0, 0)
    other = lax.ppermute(half, "seq", [(g, g ^ 1) for g in range(ROW * ROW)])

    table = pl.pallas_call(
        list_kernel,
        out_shape=jax.ShapeDtypeStruct((HEADER + 8,), jnp.int32),
        in_specs=[smem()] * 5,
        out_specs=smem(),
        cost_estimate=pl.CostEstimate(flops=2 * 10**9, bytes_accessed=10**5, transcendentals=0),
        name="lists",
    )(far_blocks.T, far_count, radial_width.T, text_len, where)

    acc, stat = pl.pallas_call(
        early_kernel,
        out_shape=(
            jax.ShapeDtypeStruct((ROW, width, tokens), jnp.float32),
            jax.ShapeDtypeStruct((ROW, 8, tokens), jnp.float32),
        ),
        in_specs=[smem(), vmem()] + [anywhere()] * 5,
        out_specs=(vmem(), vmem()),
        scratch_shapes=attend_scratch(EARLY, 5),
        compiler_params=kernel_params(),
        cost_estimate=pl.CostEstimate(flops=8 * 10**9, bytes_accessed=5 * 10**6, transcendentals=0),
        name="attend_early",
    )(table, q_all, kv, f1, b1, f2, b2)
    part = pl.pallas_call(
        late_kernel,
        out_shape=jax.ShapeDtypeStruct((ROW, width + TPAD, tokens), jnp.bfloat16),
        in_specs=[smem(), vmem()] + [anywhere()] * 4 + [vmem()] * 2,
        out_specs=vmem(),
        scratch_shapes=attend_scratch(LATE, 4),
        compiler_params=kernel_params(),
        cost_estimate=pl.CostEstimate(flops=7 * 10**9, bytes_accessed=5 * 10**6, transcendentals=0),
        name="attend_late",
    )(table, q_all, f3, b3, f4, b4, acc, stat)
    part, half = lax.optimization_barrier((part, half))
    part = lax.all_to_all(part, "seq", 0, 0, axis_index_groups=row_peers())
    merged = pl.pallas_call(
        merge_kernel,
        out_shape=jax.ShapeDtypeStruct((ROW, width, tokens), jnp.bfloat16),
        in_specs=[vmem()],
        out_specs=vmem(),
        compiler_params=kernel_params(),
        name="merge",
    )(part)
    attention = lax.all_to_all(merged, "head", 0, 0)
    even = own % 2 == 0
    w_mine = jnp.concatenate((jnp.where(even, half, other), jnp.where(even, other, half)), axis=1)
    mixed = lax.dot_general(
        attention.reshape(heads * width, tokens),
        w_mine.reshape(heads * width, columns),
        (((0,), (0,)), ((), ())),
        preferred_element_type=jnp.float32,
    )
    return mixed.astype(jnp.bfloat16)


def solution(mesh):
    return jax.shard_map(
        shards,
        mesh=mesh,
        in_specs=(
            P("seq", "head"),
            P("seq", "head"),
            P("seq", "head"),
            P("seq", "head"),
            P("seq", "head"),
            P(),
            P(),
            P(),
            P(),
            P("head", None),
        ),
        out_specs=P("seq", "head"),
        check_vma=False,
    )
```

time: 377 us -> 145 us (0.38)
  blocking collectives: 211 us -> 22.7 us
  local copies, waits for them, and re-layouts: 46 us -> 10.4 us
  Pallas kernels: 0 us -> 26.7 us
  starting transfers between devices: 25.5 us -> 50.9 us
  other arithmetic: 24.1 us -> 3.32 us
  waiting for transfers between devices: 44.9 us -> 26.7 us
  between operations: 14.5 us -> 0.97 us
  matrix products: 8.89 us -> 2.79 us
    all_gather x1 -> x0, blocking collectives: 211 us -> none  [shards(): lax.all_gather(jnp.stack((text_keys, text_values)), 'seq', axis=1, tiled=...]
    reduce_scatter x1 -> x0, waiting for transfers between devices: 44.9 us -> none  [shards(): lax.psum_scatter(partial_terms, 'head', scatter_dimension=1, tiled=True)]
    pallas_call x0 -> x4, Pallas kernels: none -> 26.7 us  [the longest x1 9.93 us: shards(): pl.pallas_call(early_kernel, out_shape=(jax.ShapeDtypeStruct((ROW, width,...]
    all_to_all x1 -> x3, waiting for transfers between devices: 0.01 us -> 24.4 us  [the longest x1 21.4 us: shards(): attention = lax.all_to_all(merged, 'head', 0, 0)]
    all_to_all x0 -> x1, blocking collectives: none -> 22.7 us  [shards(): part = lax.all_to_all(part, 'seq', 0, 0, axis_index_groups=row_peers())]
    ppermute x4 -> x9, starting transfers between devices: 10.3 us -> 30.1 us  [the longest x8 27.2 us: along_column(): lax.ppermute(block, 'seq', [(g, (g + ROW * distance) % count) for g in ra...]
    gather x5 -> x0, local copies, waits for them, and re-layouts: 19.3 us -> none  [the longest x2 7.55 us: shards(): jnp.take(far_both[0][:, :, columns], source_grid, axis=0)]
    select_n x5 -> x1, other arithmetic: 10.6 us -> 2.65 us  [shards(): jnp.where(even, half, other)]
  transfers between devices with their start and end apart: 6 -> 12, of which waited for: 1 -> 3; matrix products, arithmetic and copies ran while one was open for 5% -> 7% of each run, Pallas kernels for 0% -> 18%
where the time goes in v1:
time: 145 us; the launch traced here: 144 us
  starting transfers between devices  50.9 us (35%)
  waiting for transfers between devices  26.7 us (18%)
  Pallas kernels  26.7 us (18%)
  blocking collectives  22.7 us (16%)
  local copies, waits for them, and re-layouts  10.4 us (7%)
  other arithmetic  3.32 us (2%)
  matrix products  2.79 us (2%)
    ppermute x8, starting transfers between devices, along_column(): lax.ppermute(block, 'seq', [(g, (g + ROW * distance) % count) for g in ra...  27.2 us
    all_to_all x1, blocking collectives, shards(): part = lax.all_to_all(part, 'seq', 0, 0, axis_index_groups=row_peers())  22.7 us
    all_to_all x1, waiting for transfers between devices, shards(): attention = lax.all_to_all(merged, 'head', 0, 0)  21.4 us
    all_to_all x1, starting transfers between devices, shards(): lax.all_to_all(jnp.broadcast_to(queries[None], (ROW, tokens, width)), 'se...  10.5 us
    pallas_call x1, Pallas kernels, shards(): pl.pallas_call(early_kernel, out_shape=(jax.ShapeDtypeStruct((ROW, width,...  9.93 us
    pallas_call x1, Pallas kernels, shards(): pl.pallas_call(list_kernel, out_shape=jax.ShapeDtypeStruct((HEADER + 8,),...  7.99 us
    pallas_call x1, Pallas kernels, shards(): pl.pallas_call(late_kernel, out_shape=jax.ShapeDtypeStruct((ROW, width +...  7.49 us
    all_to_all x1, starting transfers between devices, shards(): half = lax.all_to_all(half, 'head', 0, 0)  6.83 us
  transfers between devices with their start and end apart: 12, of which 3 were waited for; matrix products, arithmetic and copies ran while one was open for 7% of the time, Pallas kernels for 18%

profile of v1, /device:TPU:1, one launch (start us, length us, event | category | flops | bytes accessed | tf_op | source)
XLA Modules:
  0.0 144.5 jit_solution(8524361561600601816)
XLA Ops:
  0.0 2.1 %broadcast_in_dim.2 = bf16[8,256,256]{2,1,0:T(8,128)(2,1)} broadcast(bf16[256,256]{1,0:T(8,128)(2,1)} %param.10), dimensions={1,2} | broadcast | bytes 1179648 | tf_op jit(solution)/shard_map/broadcast_in_dim | solution.py:321
  2.1 10.5 %all-to-all-start = ((bf16[8,256,256]{2,1,0:T(8,128)(2,1)}), bf16[8,256,256]{2,1,0:T(8,128)(2,1)S(1)}, u32[]{:S(2)}, u32[]{:S(2)}) async-start(bf16[8,256,256]{2,1,0:T(8,128)(2,1)} %broadcast_in_dim.2), calls=%async_computation | async-start | bytes 2097152 | tf_op jit(solution)/shard_map/all_to_all | solution.py:320
  12.6 0.1 copy.15
  12.8 1.9 %collective-permute-start = (bf16[544,256]{1,0:T(8,128)(2,1)S(1)}, bf16[544,256]{1,0:T(8,128)(2,1)}, u32[]{:S(2)}, u32[]{:S(2)}) collective-permute-start(bf16[544,256]{1,0:T(8,128)(2,1)S(1)} %fusion.14.own), channel_id=1, source_target_pairs={{0,64},{8,72},{16,80},{24,88},{32,96},{40,104},{48,112},{56,120},{... | collective-permute-start | bytes 835592 | tf_op jit(solution)/shard_map/ppermute | solution.py:35
  14.8 6.1 %collective-permute-start.3 = (bf16[544,256]{1,0:T(8,128)(2,1)S(1)}, bf16[544,256]{1,0:T(8,128)(2,1)}, u32[]{:S(2)}, u32[]{:S(2)}) collective-permute-start(bf16[544,256]{1,0:T(8,128)(2,1)S(1)} %fusion.14.own), channel_id=1, source_target_pairs={{0,448},{8,456},{16,464},{24,472},{32,480},{40,488},{48,496},{56,5... | collective-permute-start | bytes 835592 | tf_op jit(solution)/shard_map/ppermute | solution.py:35
  20.9 1.0 constant_dynamic-slice_fusion
  21.9 2.3 %copy.18 = bf16[128,3072]{0,1:T(8,128)(2,1)} copy(bf16[128,3072]{1,0:T(8,128)(2,1)} %constant_dynamic-slice_fusion) | data formatting | bytes 1572864
  24.2 2.3 %copy.14 = bf16[128,8,384]{2,0,1:T(8,128)(2,1)} copy(bf16[128,8,384]{0,2,1:T(8,128)(2,1)} %bitcast.18) | data formatting | bytes 1572864 | tf_op jit(solution)/shard_map/reshape | solution.py:331
  27.1 0.0 collective-permute-done.f1
  27.2 1.9 %collective-permute-start.1 = (bf16[544,256]{1,0:T(8,128)(2,1)}, bf16[544,256]{1,0:T(8,128)(2,1)S(1)}, u32[]{:S(2)}, u32[]{:S(2)}) collective-permute-start(bf16[544,256]{1,0:T(8,128)(2,1)} %collective-permute-done.f1), channel_id=1, source_target_pairs={{0,64},{8,72},{16,80},{24,88},{32,96},{40,104},{48,112},{56,120},{... | collective-permute-start | bytes 835592 | tf_op jit(solution)/shard_map/ppermute | solution.py:35
  29.1 4.6 %collective-permute-start.4 = (bf16[544,256]{1,0:T(8,128)(2,1)}, bf16[544,256]{1,0:T(8,128)(2,1)S(1)}, u32[]{:S(2)}, u32[]{:S(2)}) collective-permute-start(bf16[544,256]{1,0:T(8,128)(2,1)} %collective-permute-done.3.b1), channel_id=1, source_target_pairs={{0,448},{8,456},{16,464},{24,472},{32,480},{40,488},{48,496},{56,5... | collective-permute-start | bytes 835592 | tf_op jit(solution)/shard_map/ppermute | solution.py:35
  33.7 0.7 pad_add_fusion.where_ref
  34.3 8.0 %lists.1.table = s32[520]{0:T(1024)} custom-call(s32[29,128]{1,0:T(8,128)} %bitcast.21, s32[128]{0:T(128)} %count_ref.1, s32[5,64]{1,0:T(8,128)} %bitcast.22, s32[1]{0:T(128)S(6)} %copy.22.len_ref, s32[2]{0:T(128)} %pad_add_fusion.where_ref), custom_call_target="tpu_custom_call" | custom-call | flops 2000000000 | bytes 100000 | tf_op jit(solution)/shard_map/lists/pallas_call | solution.py:336
  42.3 0.7 slice.9
  43.0 2.1 %collective-permute-start.7 = (bf16[288,256]{1,0:T(8,128)(2,1)}, bf16[288,256]{1,0:T(8,128)(2,1)}, u32[]{:S(2)}, u32[]{:S(2)}) collective-permute-start(bf16[288,256]{1,0:T(8,128)(2,1)} %slice.9), channel_id=1, source_target_pairs={{0,384},{8,392},{16,400},{24,408},{32,416},{40,424},{48,432},{56,4... | collective-permute-start | bytes 442376 | tf_op jit(solution)/shard_map/ppermute | solution.py:35
  45.2 0.7 slice.8
  45.8 4.0 %collective-permute-start.6 = (bf16[256,256]{1,0:T(8,128)(2,1)}, bf16[256,256]{1,0:T(8,128)(2,1)}, u32[]{:S(2)}, u32[]{:S(2)}) collective-permute-start(bf16[256,256]{1,0:T(8,128)(2,1)} %slice.8), channel_id=1, source_target_pairs={{0,128},{8,136},{16,144},{24,152},{32,160},{40,168},{48,176},{56,1... | collective-permute-start | bytes 393224 | tf_op jit(solution)/shard_map/ppermute | solution.py:35
  49.9 1.9 %collective-permute-start.2 = (bf16[544,256]{1,0:T(8,128)(2,1)S(1)}, bf16[544,256]{1,0:T(8,128)(2,1)}, u32[]{:S(2)}, u32[]{:S(2)}) collective-permute-start(bf16[544,256]{1,0:T(8,128)(2,1)S(1)} %collective-permute-done.1.f2), channel_id=1, source_target_pairs={{0,64},{8,72},{16,80},{24,88},{32,96},{40,104},{48,112},{56,120},{... | collective-permute-start | bytes 835592 | tf_op jit(solution)/shard_map/ppermute | solution.py:35
  51.8 4.6 %collective-permute-start.5 = (bf16[544,256]{1,0:T(8,128)(2,1)S(1)}, bf16[544,256]{1,0:T(8,128)(2,1)}, u32[]{:S(2)}, u32[]{:S(2)}) collective-permute-start(bf16[544,256]{1,0:T(8,128)(2,1)S(1)} %collective-permute-done.4.b2), channel_id=1, source_target_pairs={{0,448},{8,456},{16,464},{24,472},{32,480},{40,488},{48,496},{56,5... | collective-permute-start | bytes 835592 | tf_op jit(solution)/shard_map/ppermute | solution.py:35
  56.4 6.8 %all-to-all-start.1 = ((bf16[8,128,384]{2,1,0:T(8,128)(2,1)}), bf16[8,128,384]{2,1,0:T(8,128)(2,1)}, u32[]{:S(2)}, u32[]{:S(2)}) async-start(bf16[8,128,384]{2,1,0:T(8,128)(2,1)} %bitcast.17), calls=%async_computation.1 | async-start | bytes 1572864 | tf_op jit(solution)/shard_map/all_to_all | solution.py:333
  63.2 9.9 %attend_early.1 = (f32[8,256,256]{2,1,0:T(8,128)S(1)}, f32[8,8,256]{2,1,0:T(8,128)S(1)}) custom-call(s32[520]{0:T(1024)S(1)} %copy-done.3, bf16[8,256,256]{2,1,0:T(8,128)(2,1)S(1)} %all-to-all-done.q_ref, bf16[544,256]{1,0:T(8,128)(2,1)S(1)} %fusion.14.own, bf16[544,256]{1,0:T(8,128)(2,1)} %collective-permute-done.f1, ...), custom_call_target="tpu_custom_call" | custom-call | flops 8000000000 | bytes 5000000 | tf_op jit(solution)/shard_map/attend_early/pallas_call | solution.py:345
  73.2 1.2 copy-done.2
  74.4 7.5 %attend_late.1 = bf16[8,272,256]{2,1,0:T(8,128)(2,1)S(1)} custom-call(s32[520]{0:T(1024)S(1)} %copy-done.3, bf16[8,256,256]{2,1,0:T(8,128)(2,1)S(1)} %copy-done.2, bf16[544,256]{1,0:T(8,128)(2,1)} %collective-permute-done.2.f3, bf16[544,256]{1,0:T(8,128)(2,1)} %collective-permute-done.5.b3, bf16[256,256]{1,0:T(8,128)(2,1)} %collective-permute-done.6.f4, ...), custom_call_target="tpu_custom_call" | custom-call | flops 7000000000 | bytes 5000000 | tf_op jit(solution)/shard_map/attend_late/pallas_call | solution.py:358
  81.9 3.1 %all-to-all-done.1 = bf16[8,128,384]{2,1,0:T(8,128)(2,1)} async-done(((bf16[8,128,384]{2,1,0:T(8,128)(2,1)}), bf16[8,128,384]{2,1,0:T(8,128)(2,1)}, u32[]{:S(2)}, u32[]{:S(2)}) %all-to-all-start.1) | async-done | bytes 786464 | tf_op jit(solution)/shard_map/all_to_all | solution.py:333
  85.0 22.7 %all_to_all.20.part_ref = bf16[8,272,256]{2,1,0:T(8,128)(2,1)S(1)} all-to-all(bf16[8,272,256]{2,1,0:T(8,128)(2,1)S(1)} %attend_late.1), channel_id=1, replica_groups={{0,8,16,24,32,40,48,56},{64,72,80,88,96,104,112,120},{128,136,144,152,1..., dimensions={0} | all-to-all | bytes 2228224 | tf_op jit(solution)/shard_map/all_to_all | solution.py:369
  107.7 1.2 merge.1
  109.0 3.6 %all-to-all-start.3 = ((bf16[8,256,256]{2,1,0:T(8,128)(2,1)}), bf16[8,256,256]{2,1,0:T(8,128)(2,1)S(1)}, u32[]{:S(2)}, u32[]{:S(2)}) async-start(bf16[8,256,256]{2,1,0:T(8,128)(2,1)} %merge.1), calls=%async_computation.3 | async-start | bytes 2097152 | tf_op jit(solution)/shard_map/all_to_all | solution.py:378
  112.5 2.9 %collective-permute-start.8 = (bf16[8,128,384]{2,1,0:T(8,128)(2,1)}, bf16[8,128,384]{2,1,0:T(8,128)(2,1)}, u32[]{:S(2)}, u32[]{:S(2)}) collective-permute-start(bf16[8,128,384]{2,1,0:T(8,128)(2,1)} %all-to-all-done.1), channel_id=1, source_target_pairs={{0,8},{8,0},{16,24},{24,16},{32,40},{40,32},{48,56},{56,48},{64,72... | collective-permute-start | bytes 2359304 | tf_op jit(solution)/shard_map/ppermute | solution.py:334
  115.4 2.2 %collective-permute-done.8 = bf16[8,128,384]{2,1,0:T(8,128)(2,1)} collective-permute-done((bf16[8,128,384]{2,1,0:T(8,128)(2,1)}, bf16[8,128,384]{2,1,0:T(8,128)(2,1)}, u32[]{:S(2)}, u32[]{:S(2)}) %collective-permute-start.8) | collective-permute-done | bytes 786464 | tf_op jit(solution)/shard_map/ppermute | solution.py:334
  117.6 2.7 %broadcast_select_fusion.1 = (bf16[8,128,384]{2,1,0:T(8,128)(2,1)}, bf16[8,128,384]{2,1,0:T(8,128)(2,1)}) fusion(bf16[8,128,384]{2,1,0:T(8,128)(2,1)} %all-to-all-done.1, bf16[8,128,384]{2,1,0:T(8,128)(2,1)} %collective-permute-done.8, pred[]{:T(512)S(6)} %eq.7), kind=kLoop, calls=%fused_computation.9 | loop fusion | flops 786432 | bytes 3145729 | tf_op jit(solution)/shard_map/jit(_where)/select_n | solution.py:380
  120.3 21.4 %all-to-all-done.3 = bf16[8,256,256]{2,1,0:T(8,128)(2,1)S(1)} async-done(((bf16[8,256,256]{2,1,0:T(8,128)(2,1)}), bf16[8,256,256]{2,1,0:T(8,128)(2,1)S(1)}, u32[]{:S(2)}, u32[]{:S(2)}) %all-to-all-start.3) | async-done | bytes 1048608 | tf_op jit(solution)/shard_map/all_to_all | solution.py:378
  141.7 2.8 %fusion.7 = bf16[256,384]{1,0:T(8,128)(2,1)} fusion(bf16[8,256,256]{2,1,0:T(8,128)(2,1)S(1)} %all-to-all-done.3, bf16[8,128,384]{2,1,0:T(8,128)(2,1)} %get-tuple-element.18, bf16[8,128,384]{2,1,0:T(8,128)(2,1)} %get-tuple-element.17), kind=kOutput, calls=%fused_computation.5 | convolution fusion | flops 405897216 | bytes 2818048 | tf_op jit(solution)/shard_map/dot_general | solution.py:381
  (26 shorter events, 0.1 us)
Async XLA Ops:
  0.0 20.9 %copy-start = (bf16[256,3072]{1,0:T(8,128)(2,1)S(1)}, bf16[256,3072]{1,0:T(8,128)(2,1)}, u32[]{:S(2)}) copy-start(bf16[256,3072]{1,0:T(8,128)(2,1)} %param.19) | copy-start | bytes 4718596
  0.0 12.6 %copy-start.4 = (bf16[256,256]{1,0:T(8,128)(2,1)S(1)}, bf16[256,256]{1,0:T(8,128)(2,1)}, u32[]{:S(2)}) copy-start(bf16[256,256]{1,0:T(8,128)(2,1)} %param.12) | copy-start | bytes 393220
  2.1 10.7 %copy-start.5 = (bf16[256,256]{1,0:T(8,128)(2,1)S(1)}, bf16[256,256]{1,0:T(8,128)(2,1)}, u32[]{:S(2)}) copy-start(bf16[256,256]{1,0:T(8,128)(2,1)} %param.11) | copy-start | bytes 393220
  2.1 10.7 %copy-start.6 = (bf16[4,256]{1,0:T(4,128)(2,1)S(1)}, bf16[4,256]{1,0:T(4,128)(2,1)}, u32[]{:S(2)}) copy-start(bf16[4,256]{1,0:T(4,128)(2,1)} %param.14) | copy-start | bytes 6148
  2.1 10.7 %copy-start.7 = (bf16[4,256]{1,0:T(4,128)(2,1)S(1)}, bf16[4,256]{1,0:T(4,128)(2,1)}, u32[]{:S(2)}) copy-start(bf16[4,256]{1,0:T(4,128)(2,1)} %param.13) | copy-start | bytes 6148
  2.1 54.3 %all-to-all-start = ((bf16[8,256,256]{2,1,0:T(8,128)(2,1)}), bf16[8,256,256]{2,1,0:T(8,128)(2,1)S(1)}, u32[]{:S(2)}, u32[]{:S(2)}) async-start(bf16[8,256,256]{2,1,0:T(8,128)(2,1)} %broadcast_in_dim.2), calls=%async_computation | async-start | bytes 2097152 | tf_op jit(solution)/shard_map/all_to_all | solution.py:320
  12.8 14.3 %collective-permute-start = (bf16[544,256]{1,0:T(8,128)(2,1)S(1)}, bf16[544,256]{1,0:T(8,128)(2,1)}, u32[]{:S(2)}, u32[]{:S(2)}) collective-permute-start(bf16[544,256]{1,0:T(8,128)(2,1)S(1)} %fusion.14.own), channel_id=1, source_target_pairs={{0,64},{8,72},{16,80},{24,88},{32,96},{40,104},{48,112},{56,120},{... | collective-permute-start | bytes 835592 | tf_op jit(solution)/shard_map/ppermute | solution.py:35
  14.8 14.3 %collective-permute-start.3 = (bf16[544,256]{1,0:T(8,128)(2,1)S(1)}, bf16[544,256]{1,0:T(8,128)(2,1)}, u32[]{:S(2)}, u32[]{:S(2)}) collective-permute-start(bf16[544,256]{1,0:T(8,128)(2,1)S(1)} %fusion.14.own), channel_id=1, source_target_pairs={{0,448},{8,456},{16,464},{24,472},{32,480},{40,488},{48,496},{56,5... | collective-permute-start | bytes 835592 | tf_op jit(solution)/shard_map/ppermute | solution.py:35
  27.2 18.0 %collective-permute-start.1 = (bf16[544,256]{1,0:T(8,128)(2,1)}, bf16[544,256]{1,0:T(8,128)(2,1)S(1)}, u32[]{:S(2)}, u32[]{:S(2)}) collective-permute-start(bf16[544,256]{1,0:T(8,128)(2,1)} %collective-permute-done.f1), channel_id=1, source_target_pairs={{0,64},{8,72},{16,80},{24,88},{32,96},{40,104},{48,112},{56,120},{... | collective-permute-start | bytes 835592 | tf_op jit(solution)/shard_map/ppermute | solution.py:35
  29.1 13.2 %collective-permute-start.4 = (bf16[544,256]{1,0:T(8,128)(2,1)}, bf16[544,256]{1,0:T(8,128)(2,1)S(1)}, u32[]{:S(2)}, u32[]{:S(2)}) collective-permute-start(bf16[544,256]{1,0:T(8,128)(2,1)} %collective-permute-done.3.b1), channel_id=1, source_target_pairs={{0,448},{8,456},{16,464},{24,472},{32,480},{40,488},{48,496},{56,5... | collective-permute-start | bytes 835592 | tf_op jit(solution)/shard_map/ppermute | solution.py:35
  42.3 20.9 %copy-start.3 = (s32[520]{0:T(1024)S(1)}, s32[520]{0:T(1024)}, u32[]{:S(2)}) copy-start(s32[520]{0:T(1024)} %lists.1.table) | copy-start | bytes 6244
  43.0 30.2 %collective-permute-start.7 = (bf16[288,256]{1,0:T(8,128)(2,1)}, bf16[288,256]{1,0:T(8,128)(2,1)}, u32[]{:S(2)}, u32[]{:S(2)}) collective-permute-start(bf16[288,256]{1,0:T(8,128)(2,1)} %slice.9), channel_id=1, source_target_pairs={{0,384},{8,392},{16,400},{24,408},{32,416},{40,424},{48,432},{56,4... | collective-permute-start | bytes 442376 | tf_op jit(solution)/shard_map/ppermute | solution.py:35
  45.8 27.4 %collective-permute-start.6 = (bf16[256,256]{1,0:T(8,128)(2,1)}, bf16[256,256]{1,0:T(8,128)(2,1)}, u32[]{:S(2)}, u32[]{:S(2)}) collective-permute-start(bf16[256,256]{1,0:T(8,128)(2,1)} %slice.8), channel_id=1, source_target_pairs={{0,128},{8,136},{16,144},{24,152},{32,160},{40,168},{48,176},{56,1... | collective-permute-start | bytes 393224 | tf_op jit(solution)/shard_map/ppermute | solution.py:35
  49.9 23.3 %collective-permute-start.2 = (bf16[544,256]{1,0:T(8,128)(2,1)S(1)}, bf16[544,256]{1,0:T(8,128)(2,1)}, u32[]{:S(2)}, u32[]{:S(2)}) collective-permute-start(bf16[544,256]{1,0:T(8,128)(2,1)S(1)} %collective-permute-done.1.f2), channel_id=1, source_target_pairs={{0,64},{8,72},{16,80},{24,88},{32,96},{40,104},{48,112},{56,120},{... | collective-permute-start | bytes 835592 | tf_op jit(solution)/shard_map/ppermute | solution.py:35
  51.8 21.4 %collective-permute-start.5 = (bf16[544,256]{1,0:T(8,128)(2,1)S(1)}, bf16[544,256]{1,0:T(8,128)(2,1)}, u32[]{:S(2)}, u32[]{:S(2)}) collective-permute-start(bf16[544,256]{1,0:T(8,128)(2,1)S(1)} %collective-permute-done.4.b2), channel_id=1, source_target_pairs={{0,448},{8,456},{16,464},{24,472},{32,480},{40,488},{48,496},{56,5... | collective-permute-start | bytes 835592 | tf_op jit(solution)/shard_map/ppermute | solution.py:35
  56.4 16.8 %copy-start.1 = (bf16[8,256,256]{2,1,0:T(8,128)(2,1)}, bf16[8,256,256]{2,1,0:T(8,128)(2,1)S(1)}, u32[]{:S(2)}) copy-start(bf16[8,256,256]{2,1,0:T(8,128)(2,1)S(1)} %all-to-all-done.q_ref) | copy-start | bytes 3145732
  56.4 28.6 %all-to-all-start.1 = ((bf16[8,128,384]{2,1,0:T(8,128)(2,1)}), bf16[8,128,384]{2,1,0:T(8,128)(2,1)}, u32[]{:S(2)}, u32[]{:S(2)}) async-start(bf16[8,128,384]{2,1,0:T(8,128)(2,1)} %bitcast.17), calls=%async_computation.1 | async-start | bytes 1572864 | tf_op jit(solution)/shard_map/all_to_all | solution.py:333
  73.2 1.2 copy-start.2
  109.0 32.7 %all-to-all-start.3 = ((bf16[8,256,256]{2,1,0:T(8,128)(2,1)}), bf16[8,256,256]{2,1,0:T(8,128)(2,1)S(1)}, u32[]{:S(2)}, u32[]{:S(2)}) async-start(bf16[8,256,256]{2,1,0:T(8,128)(2,1)} %merge.1), calls=%async_computation.3 | async-start | bytes 2097152 | tf_op jit(solution)/shard_map/all_to_all | solution.py:378
  112.5 5.1 %collective-permute-start.8 = (bf16[8,128,384]{2,1,0:T(8,128)(2,1)}, bf16[8,128,384]{2,1,0:T(8,128)(2,1)}, u32[]{:S(2)}, u32[]{:S(2)}) collective-permute-start(bf16[8,128,384]{2,1,0:T(8,128)(2,1)} %all-to-all-done.1), channel_id=1, source_target_pairs={{0,8},{8,0},{16,24},{24,16},{32,40},{40,32},{48,56},{56,48},{64,72... | collective-permute-start | bytes 2359304 | tf_op jit(solution)/shard_map/ppermute | solution.py:334

commit v2 on v0

v2 whole, which is shorter than its diff:
```python
import functools

import jax
import jax.numpy as jnp
from jax import lax
from jax.experimental import pallas as pl
from jax.experimental.pallas import tpu as pltpu
from jax.sharding import PartitionSpec as P

HD = 128
BLK = 128
NEAR = 2
ROW = 8
TPAD = 16
NEG = -1e30
FLOOR = -1e9
SCORE_SCALE = HD ** (-0.5) * 1.4426950408889634
EARLY = (0, -1, 1, -2, 2)
LATE = (-3, 3, 4)
TOGETHER = 4
TEXT_ROWS = 8
GROUPS_AT_ONCE = 4
MESSAGE = 4 * BLK + TPAD
NEAR_AT = ROW
LEN_AT = ROW + 1
WHERE_AT = ROW + 2


def row_peers():
    return [[z * ROW + r for r in range(ROW)] for z in range(ROW)]


def along_column(block, distance):
    count = ROW * ROW
    return lax.ppermute(block, "seq", [(g, (g + ROW * distance) % count) for g in range(count)])


def turned(buf):
    for a in range(2):
        for h in range(2):
            tile = buf[a * BLK : (a + 1) * BLK, h * HD : (h + 1) * HD].astype(jnp.float32)
            yield a, h, tile.T.astype(jnp.bfloat16)


def key_kernel(k_in, v_in, text_in, kv_out, v_buf, sems):
    copies = [
        pltpu.make_async_copy(v_in, v_buf, sems.at[0]),
        pltpu.make_async_copy(k_in, kv_out.at[: 2 * BLK], sems.at[1]),
    ]
    for copy in copies:
        copy.start()
    kv_out[4 * BLK :, :] = text_in[...]
    copies[0].wait()
    for a, h, tile in turned(v_buf):
        kv_out[(2 + a) * BLK : (3 + a) * BLK, h * HD : (h + 1) * HD] = tile
    copies[1].wait()


def query_kernel(q_in, q_out, q_buf, sems):
    copy = pltpu.make_async_copy(q_in, q_buf, sems.at[0])
    copy.start()
    copy.wait()
    for a, h, tile in turned(q_buf):
        for i in range(ROW):
            q_out[i, a * BLK : (a + 1) * BLK, h * HD : (h + 1) * HD] = tile


def weight_kernel(where_ref, w_in, w_out, sems):
    heads, rows, columns = w_out.shape
    start = pl.multiple_of((where_ref[1] & 3) * rows, rows)
    copies = [
        pltpu.make_async_copy(
            w_in.at[pl.ds(start, rows), i * columns : (i + 1) * columns], w_out.at[i], sems.at[i]
        )
        for i in range(heads)
    ]
    for copy in copies:
        copy.start()
    for copy in copies:
        copy.wait()


def list_kernel(where_ref, far_ref, width_ref, table_ref):
    z = where_ref[0]
    r = where_ref[1]
    rows = 2 * ROW
    slots = far_ref.shape[1] - 1
    mine = far_ref[pl.ds(pl.multiple_of(z * rows, rows), rows), :]
    place = lax.broadcasted_iota(jnp.int32, mine.shape, 1)
    count = jnp.sum(jnp.where(place == slots, mine, 0), axis=1, keepdims=True)
    live = place < count
    live = live & (place < slots)
    lane = lax.broadcasted_iota(jnp.int32, (rows, BLK), 1)
    table = jnp.where(lane == LEN_AT, where_ref[2], 0)
    table = jnp.where(lane == WHERE_AT, z, table)
    table = jnp.where(lane == WHERE_AT + 1, r, table)
    for s, step in enumerate(EARLY + LATE):
        group = ((z + step) & (ROW - 1)) * ROW + r
        asked = jnp.where(live & ((mine >> 1) == group), 1 + (mine & 1), 0)
        table = jnp.where(lane == s, jnp.sum(asked, axis=1, keepdims=True), table)
    widths = width_ref[pl.ds(pl.multiple_of(z * ROW, ROW), ROW), :]
    place = lax.broadcasted_iota(jnp.int32, widths.shape, 1)
    query = lax.broadcasted_iota(jnp.int32, widths.shape, 0)
    offset = (r - query + NEAR) & (ROW - 1)
    group = z * ROW + query + offset - NEAR
    valid = (group >= 0) & (group < ROW * ROW) & (place == offset)
    step = (group >> 3) - z
    slot = jnp.where(step == 0, 0, jnp.where(step < 0, 1, 2))
    near = jnp.sum(jnp.where(valid, widths * 16 + slot, 0), axis=1, keepdims=True)
    near = jnp.concatenate((near, jnp.zeros((rows - ROW, 1), jnp.int32)), axis=0)
    table_ref[...] = jnp.where(lane == NEAR_AT, near, table)


def three_parts(x):
    high = x.astype(jnp.bfloat16).astype(jnp.float32)
    rest = x - high
    middle = rest.astype(jnp.bfloat16).astype(jnp.float32)
    return [high, middle, rest - middle]


def two_parts(x):
    high = x.astype(jnp.bfloat16).astype(jnp.float32)
    return [high, x - high]


def list_units(table, first, count, units):
    def one_block(i, n):
        for s in range(count):
            asked = table[i, first + s]
            units[n] = i * 16 + s * 2 + asked - 1
            n = n + jnp.where(asked > 0, 1, 0)
        return n

    return lax.fori_loop(0, 2 * ROW, one_block, jnp.int32(0))


def set_text(kv, table, steps, bias, text_k, text_v):
    z = table[0, WHERE_AT]
    r = table[0, WHERE_AT + 1]
    total = text_k.shape[0]
    row = lax.broadcasted_iota(jnp.int32, (TEXT_ROWS, 2 * BLK), 0)
    keys = []
    vals = []
    for s, step in enumerate(steps):
        first = (((z + step) & (ROW - 1)) * ROW + r) * 4
        alive = (row < 4) & (first + row < table[0, LEN_AT])
        bias[s * TEXT_ROWS : (s + 1) * TEXT_ROWS, :] = jnp.where(alive, 0.0, NEG)
        tile = kv[s, 4 * BLK : 4 * BLK + TPAD, :].astype(jnp.float32)[:TEXT_ROWS]
        keys.append(tile)
        vals.append(pltpu.roll(tile, 4, 0))
    spare = total - len(steps) * TEXT_ROWS
    bias[total - spare :, :] = jnp.full((spare, 2 * BLK), NEG, jnp.float32)
    keys.append(jnp.zeros((spare, 2 * HD), jnp.float32))
    text_k[...] = jnp.concatenate(keys, axis=0).astype(jnp.bfloat16)
    vals.append(jnp.zeros((HD - len(steps) * TEXT_ROWS, 2 * HD), jnp.float32))
    vals = jnp.concatenate(vals, axis=0)
    for h in range(2):
        text_v[h] = vals[:, h * HD : (h + 1) * HD].T.astype(jnp.bfloat16)


def group_queries(q_ref, g, h):
    lanes = slice(h * HD, (h + 1) * HD)
    return jnp.concatenate((q_ref[g, :BLK, lanes], q_ref[g, BLK:, lanes]), axis=1)


def product(left, right):
    return jnp.dot(left, right, preferred_element_type=jnp.float32)


def head_rows(h):
    return slice(h * HD, (h + 1) * HD)


def text_step(q_ref, cases, text_k, text_v, bias):
    spare = HD - text_k.shape[0]
    scores = [
        product(text_k[:, head_rows(h)], group_queries(q_ref, g, h)) * SCORE_SCALE + bias[...] for g, h in cases
    ]
    tops = [jnp.maximum(jnp.max(s, axis=0, keepdims=True), FLOOR) for s in scores]
    weights = [jnp.exp2(s - top) for s, top in zip(scores, tops)]
    totals = [jnp.sum(p, axis=0, keepdims=True) for p in weights]
    filler = jnp.zeros((spare, 2 * BLK), jnp.bfloat16)
    outs = [
        product(text_v[h], jnp.concatenate((p.astype(jnp.bfloat16), filler), axis=0))
        for (_, h), p in zip(cases, weights)
    ]
    return list(zip(tops, totals, outs))


def group_cases(step, groups):
    return [(step * groups + j, h) for j in range(groups) for h in range(2)]


def joined(old, new):
    top = jnp.maximum(old[0], new[0])
    fade = jnp.exp2(old[0] - top)
    rise = jnp.exp2(new[0] - top)
    return top, old[1] * fade + new[1] * rise, old[2] * fade + new[2] * rise


def read_state(acc, stat, g, h):
    return stat[g, 2 * h : 2 * h + 1, :], stat[g, 2 * h + 1 : 2 * h + 2, :], acc[g, head_rows(h), :]


def write_state(acc, stat, g, h, state):
    stat[g, 2 * h : 2 * h + 1, :] = state[0]
    stat[g, 2 * h + 1 : 2 * h + 2, :] = state[1]
    acc[g, head_rows(h), :] = state[2]


def walk_units(units, count, q_ref, kv, acc, stat):
    def step(t, _):
        work = []
        for j in range(TOGETHER):
            number = t * TOGETHER + j
            code = jnp.where(number < count, units[number], 0)
            gone = jnp.where(number < count, 0.0, NEG)
            block = code >> 4
            g = block >> 1
            across = pl.multiple_of((block & 1) * BLK, BLK)
            who = (code & 15) >> 1
            down = pl.multiple_of((code & 1) * BLK, BLK)
            for h in range(2):
                s = product(
                    kv[who, pl.ds(down, BLK), head_rows(h)], q_ref[g, pl.ds(across, BLK), head_rows(h)]
                )
                work.append((g, across, who, down, h, gone, s * SCORE_SCALE))
        done = []
        for g, across, who, down, h, gone, s in work:
            top = jnp.max(s, axis=0, keepdims=True)
            p = jnp.exp2(s - top)
            total = jnp.sum(p, axis=0, keepdims=True)
            out = product(kv[who, pl.ds(down + 2 * BLK, BLK), head_rows(h)], p.astype(jnp.bfloat16))
            done.append((g, across, h, top + gone, total, out))
        for g, across, h, top, total, out in done:
            lanes = pl.ds(across, BLK)
            old_top = stat[g, 2 * h : 2 * h + 1, lanes]
            new_top = jnp.maximum(old_top, top)
            fade = jnp.exp2(old_top - new_top)
            rise = jnp.exp2(top - new_top)
            stat[g, 2 * h : 2 * h + 1, lanes] = new_top
            stat[g, 2 * h + 1 : 2 * h + 2, lanes] = (
                stat[g, 2 * h + 1 : 2 * h + 2, lanes] * fade + total * rise
            )
            acc[g, head_rows(h), lanes] = acc[g, head_rows(h), lanes] * fade + out * rise
        return 0

    lax.fori_loop(0, (count + TOGETHER - 1) // TOGETHER, step, 0)


def wait_all(pairs, sems):
    copies = [pltpu.make_async_copy(src, dst, sems.at[i]) for i, (src, dst) in enumerate(pairs)]
    for copy in copies:
        copy.start()
    for copy in copies:
        copy.wait()


def early_kernel(
    table, q_in, own, f1, b1, f2, b2, acc, stat, q_ref, kv, units, sems, bias, text_k, text_v
):
    wait_all([(x, kv.at[i]) for i, x in enumerate((own, f1, b1, f2, b2))] + [(q_in, q_ref)], sems)
    set_text(kv, table, EARLY, bias, text_k, text_v)
    offset = lax.broadcasted_iota(jnp.int32, (2 * BLK, 2 * BLK), 0) - lax.broadcasted_iota(
        jnp.int32, (2 * BLK, 2 * BLK), 1
    )
    distance = jnp.abs(offset)

    def some_text(step, _):
        cases = group_cases(step, GROUPS_AT_ONCE)
        for (g, h), state in zip(cases, text_step(q_ref, cases, text_k, text_v, bias)):
            write_state(acc, stat, g, h, state)
        for g, h in cases[::2]:
            stat[g, 4:8, :] = jnp.zeros((4, 2 * BLK), jnp.float32)
        return 0

    lax.fori_loop(0, ROW // GROUPS_AT_ONCE, some_text, 0)

    def one_group(g, _):
        near = table[g, NEAR_AT]

        @pl.when(near > 0)
        def _():
            who = near & 15
            scores = []
            for h in range(2):
                s = product(kv[who, : 2 * BLK, head_rows(h)], group_queries(q_ref, g, h)) * SCORE_SCALE
                scores.append(jnp.where(distance < (near >> 4), s, NEG))
            fresh = []
            for h, s in enumerate(scores):
                top = jnp.max(s, axis=0, keepdims=True)
                p = jnp.exp2(s - top)
                values = jnp.concatenate(
                    (kv[who, 2 * BLK : 3 * BLK, head_rows(h)], kv[who, 3 * BLK : 4 * BLK, head_rows(h)]),
                    axis=1,
                )
                fresh.append((top, jnp.sum(p, axis=0, keepdims=True), product(values, p.astype(jnp.bfloat16))))
            for h, new in enumerate(fresh):
                write_state(acc, stat, g, h, joined(read_state(acc, stat, g, h), new))

        return 0

    lax.fori_loop(0, ROW, one_group, 0)
    walk_units(units, list_units(table, 0, len(EARLY), units), q_ref, kv, acc, stat)


def late_kernel(
    table, q_in, f3, b3, far4, acc_in, stat_in, out_ref,
    q_ref, kv, units, sems, bias, text_k, text_v, acc, stat,
):
    wait_all(
        [
            (f3, kv.at[0]),
            (b3, kv.at[1]),
            (far4, kv.at[2]),
            (q_in, q_ref),
            (acc_in, acc),
            (stat_in, stat),
        ],
        sems,
    )
    set_text(kv, table, LATE, bias, text_k, text_v)
    walk_units(units, list_units(table, len(EARLY), len(LATE), units), q_ref, kv, acc, stat)

    def some_groups(step, _):
        cases = group_cases(step, GROUPS_AT_ONCE)
        fresh = text_step(q_ref, cases, text_k, text_v, bias)
        done = [joined(read_state(acc, stat, g, h), new) for (g, h), new in zip(cases, fresh)]
        for x in range(0, len(cases), 2):
            g = cases[x][0]
            rows = []
            for h in range(2):
                top, total, out = done[x + h]
                out_ref[g, head_rows(h), :] = out.astype(jnp.bfloat16)
                rows += three_parts(top) + two_parts(total)
            rows.append(jnp.zeros((TPAD - len(rows), 2 * BLK), jnp.float32))
            out_ref[g, 2 * HD : 2 * HD + TPAD, :] = jnp.concatenate(rows, axis=0).astype(jnp.bfloat16)
        return 0

    lax.fori_loop(0, ROW // GROUPS_AT_ONCE, some_groups, 0)


def merge_kernel(part_ref, out_ref):
    stats = [part_ref[i, 2 * HD : 2 * HD + TPAD, :].astype(jnp.float32) for i in range(ROW)]
    for h in range(2):
        tops = [s[5 * h : 5 * h + 1] + s[5 * h + 1 : 5 * h + 2] + s[5 * h + 2 : 5 * h + 3] for s in stats]
        sums = [s[5 * h + 3 : 5 * h + 4] + s[5 * h + 4 : 5 * h + 5] for s in stats]
        top = functools.reduce(jnp.maximum, tops)
        weights = [jnp.exp2(t - top) for t in tops]
        total = functools.reduce(jnp.add, [w * s for w, s in zip(weights, sums)])
        inverse = 1.0 / total
        rows = slice(h * HD, (h + 1) * HD)
        acc = None
        for i in range(ROW):
            term = part_ref[i, rows, :].astype(jnp.float32) * weights[i]
            acc = term if acc is None else acc + term
        acc = (acc * inverse).astype(jnp.bfloat16)
        for i in range(ROW):
            out_ref[i, rows, :] = acc


def smem():
    return pl.BlockSpec(memory_space=pltpu.SMEM)


def vmem():
    return pl.BlockSpec(memory_space=pltpu.VMEM)


def anywhere():
    return pl.BlockSpec(memory_space=pl.ANY)


def kernel_params():
    return pltpu.CompilerParams(vmem_limit_bytes=32 << 20)


def attend_scratch(slots, copies, text_rows):
    return [
        pltpu.VMEM((ROW, 2 * BLK, 2 * HD), jnp.bfloat16),
        pltpu.VMEM((slots, MESSAGE, 2 * HD), jnp.bfloat16),
        pltpu.SMEM((2 * ROW * slots + 8,), jnp.int32),
        pltpu.SemaphoreType.DMA((copies,)),
        pltpu.VMEM((text_rows, 2 * BLK), jnp.float32),
        pltpu.VMEM((text_rows, 2 * HD), jnp.bfloat16),
        pltpu.VMEM((2, HD, HD), jnp.bfloat16),
    ]


def shards(
    queries,
    keys,
    values,
    text_keys,
    text_values,
    text_len,
    radial_width,
    far_blocks,
    far_count,
    w_out,
):
    own = lax.axis_index("seq")
    where = jnp.stack((own // ROW, own % ROW, text_len[0])).astype(jnp.int32)
    tokens, width = queries.shape
    heads = lax.axis_size("head")
    columns = w_out.shape[1] // heads

    text = jnp.concatenate(
        (text_keys, text_values, jnp.zeros((TPAD - 2 * text_keys.shape[0], width), jnp.bfloat16)), axis=0
    )
    whole = pltpu.CompilerParams(vmem_limit_bytes=60 << 20)
    kv = pl.pallas_call(
        key_kernel,
        out_shape=jax.ShapeDtypeStruct((MESSAGE, width), jnp.bfloat16),
        in_specs=[anywhere(), anywhere(), vmem()],
        out_specs=vmem(),
        scratch_shapes=[pltpu.VMEM((tokens, width), jnp.bfloat16), pltpu.SemaphoreType.DMA((2,))],
        compiler_params=whole,
        name="key_message",
    )(keys, values, text)
    kv, queries = lax.optimization_barrier((kv, queries))
    q_mine = pl.pallas_call(
        query_kernel,
        out_shape=jax.ShapeDtypeStruct((ROW, tokens, width), jnp.bfloat16),
        in_specs=[anywhere()],
        out_specs=vmem(),
        scratch_shapes=[pltpu.VMEM((tokens, width), jnp.bfloat16), pltpu.SemaphoreType.DMA((1,))],
        compiler_params=whole,
        name="query_message",
    )(queries)
    quarter = pl.pallas_call(
        weight_kernel,
        out_shape=jax.ShapeDtypeStruct((heads, width // 4, columns), jnp.bfloat16),
        in_specs=[smem(), anywhere()],
        out_specs=vmem(),
        scratch_shapes=[pltpu.SemaphoreType.DMA((heads,))],
        compiler_params=whole,
        name="weight_message",
    )(where, w_out)
    table = pl.pallas_call(
        list_kernel,
        out_shape=jax.ShapeDtypeStruct((2 * ROW, BLK), jnp.int32),
        in_specs=[smem(), vmem(), vmem()],
        out_specs=vmem(),
        cost_estimate=pl.CostEstimate(flops=10**9, bytes_accessed=10**5, transcendentals=0),
        name="lists",
    )(where, jnp.concatenate((far_blocks, far_count[:, None]), axis=1), radial_width)

    count = ROW * ROW
    f1 = along_column(kv, 1)
    b1 = along_column(kv, -1)
    q_all = lax.all_to_all(q_mine, "seq", 0, 0, axis_index_groups=row_peers())
    f2 = along_column(f1, 1)
    b2 = along_column(b1, -1)
    f2, b2, table, quarter = lax.optimization_barrier((f2, b2, table, quarter))
    f3 = along_column(f2, 1)
    b3 = along_column(b2, -1)
    far4 = lax.ppermute(
        jnp.where(own % 2 == 0, f2, b2),
        "seq",
        [(g, (g + (2 * ROW if g % 2 == 0 else -2 * ROW)) % count) for g in range(count)],
    )
    quarter, q_all = lax.optimization_barrier((quarter, q_all))
    quarter = lax.all_to_all(quarter, "head", 0, 0)

    acc, stat = pl.pallas_call(
        early_kernel,
        out_shape=(
            jax.ShapeDtypeStruct((ROW, width, tokens), jnp.float32),
            jax.ShapeDtypeStruct((ROW, 8, tokens), jnp.float32),
        ),
        in_specs=[smem()] + [anywhere()] * 6,
        out_specs=(vmem(), vmem()),
        scratch_shapes=attend_scratch(len(EARLY), 6, 48),
        compiler_params=kernel_params(),
        cost_estimate=pl.CostEstimate(flops=6 * 10**9, bytes_accessed=5 * 10**6, transcendentals=0),
        name="attend_early",
    )(table, q_all, kv, f1, b1, f2, b2)
    part = pl.pallas_call(
        late_kernel,
        out_shape=jax.ShapeDtypeStruct((ROW, width + TPAD, tokens), jnp.bfloat16),
        in_specs=[smem()] + [anywhere()] * 6,
        out_specs=vmem(),
        scratch_shapes=attend_scratch(len(LATE), 6, 32)
        + [pltpu.VMEM((ROW, width, tokens), jnp.float32), pltpu.VMEM((ROW, 8, tokens), jnp.float32)],
        compiler_params=kernel_params(),
        cost_estimate=pl.CostEstimate(flops=4 * 10**9, bytes_accessed=5 * 10**6, transcendentals=0),
        name="attend_late",
    )(table, q_all, f3, b3, far4, acc, stat)
    part, quarter = lax.optimization_barrier((part, quarter))
    part = lax.all_to_all(part, "seq", 0, 0, axis_index_groups=row_peers())
    part, quarter = lax.optimization_barrier((part, quarter))
    merged = pl.pallas_call(
        merge_kernel,
        out_shape=jax.ShapeDtypeStruct((ROW, width, tokens), jnp.bfloat16),
        in_specs=[vmem()],
        out_specs=vmem(),
        compiler_params=kernel_params(),
        name="merge",
    )(part)
    attention = lax.all_to_all(merged, "head", 0, 0)
    low = (own & 2) == 0
    other = lax.ppermute(quarter, "seq", [(g, g ^ 2) for g in range(count)])
    halves = jnp.stack((jnp.where(low, quarter, other), jnp.where(low, other, quarter)), axis=1)
    theirs = lax.ppermute(halves, "seq", [(g, g ^ 1) for g in range(count)])
    even = (own & 1) == 0
    w_mine = jnp.stack((jnp.where(even, halves, theirs), jnp.where(even, theirs, halves)), axis=2)
    mixed = lax.dot_general(
        attention.reshape(heads * width, tokens),
        w_mine.reshape(heads * width, columns),
        (((0,), (0,)), ((), ())),
        preferred_element_type=jnp.float32,
    )
    return mixed.astype(jnp.bfloat16)


def solution(mesh):
    return jax.shard_map(
        shards,
        mesh=mesh,
        in_specs=(
            P("seq", "head"),
            P("seq", "head"),
            P("seq", "head"),
            P("seq", "head"),
            P("seq", "head"),
            P(),
            P(),
            P(),
            P(),
            P("head", None),
        ),
        out_specs=P("seq", "head"),
        check_vma=False,
    )
```

time: 377 us -> 134 us (0.36)
  blocking collectives: 211 us -> 22.1 us
  local copies, waits for them, and re-layouts: 46 us -> 1.72 us
  starting transfers between devices: 25.5 us -> 51.7 us
  Pallas kernels: 0 us -> 23.3 us
  other arithmetic: 24.1 us -> 3.61 us
  waiting for transfers between devices: 44.9 us -> 28.2 us
  between operations: 14.5 us -> 0.93 us
  matrix products: 8.89 us -> 1.42 us
    all_gather x1 -> x0, blocking collectives: 211 us -> none  [shards(): lax.all_gather(jnp.stack((text_keys, text_values)), 'seq', axis=1, tiled=...]
    reduce_scatter x1 -> x0, waiting for transfers between devices: 44.9 us -> none  [shards(): lax.psum_scatter(partial_terms, 'head', scatter_dimension=1, tiled=True)]
    pallas_call x0 -> x7, Pallas kernels: none -> 23.3 us  [the longest x1 8.55 us: shards(): pl.pallas_call(early_kernel, out_shape=(jax.ShapeDtypeStruct((ROW, width,...]
    all_to_all x0 -> x1, blocking collectives: none -> 22.1 us  [shards(): part = lax.all_to_all(part, 'seq', 0, 0, axis_index_groups=row_peers())]
    gather x5 -> x0, local copies, waits for them, and re-layouts: 19.3 us -> none  [the longest x2 7.55 us: shards(): jnp.take(far_both[0][:, :, columns], source_grid, axis=0)]
    ppermute x4 -> x9, starting transfers between devices: 10.3 us -> 29.2 us  [the longest x6 21 us: along_column(): lax.ppermute(block, 'seq', [(g, (g + ROW * distance) % count) for g in ra...]
    all_to_all x1 -> x3, waiting for transfers between devices: 0.01 us -> 18.8 us  [the longest x1 18.8 us: shards(): attention = lax.all_to_all(merged, 'head', 0, 0)]
    select_n x5 -> x1, other arithmetic: 10.6 us -> 0.04 us  [shards(): jnp.where(own % 2 == 0, f2, b2)]
  transfers between devices with their start and end apart: 6 -> 12, of which waited for: 1 -> 4; matrix products, arithmetic and copies ran while one was open for 5% -> 3% of each run, Pallas kernels for 0% -> 14%
where the time goes in v2:
time: 134 us; the launch traced here: 133 us
  starting transfers between devices  51.7 us (39%)
  waiting for transfers between devices  28.2 us (21%)
  Pallas kernels  23.3 us (17%)
  blocking collectives  22.1 us (16%)
  other arithmetic  3.61 us (3%)
  local copies, waits for them, and re-layouts  1.72 us (1%)
  matrix products  1.42 us (1%)
    all_to_all x1, blocking collectives, shards(): part = lax.all_to_all(part, 'seq', 0, 0, axis_index_groups=row_peers())  22.1 us
    ppermute x6, starting transfers between devices, along_column(): lax.ppermute(block, 'seq', [(g, (g + ROW * distance) % count) for g in ra...  21 us
    all_to_all x1, waiting for transfers between devices, shards(): attention = lax.all_to_all(merged, 'head', 0, 0)  18.8 us
    all_to_all x1, starting transfers between devices, shards(): q_all = lax.all_to_all(q_mine, 'seq', 0, 0, axis_index_groups=row_peers())  10.3 us
    pallas_call x1, Pallas kernels, shards(): pl.pallas_call(early_kernel, out_shape=(jax.ShapeDtypeStruct((ROW, width,...  8.55 us
    all_to_all x1, starting transfers between devices, shards(): quarter = lax.all_to_all(quarter, 'head', 0, 0)  6.83 us
    all_to_all x1, starting transfers between devices, shards(): attention = lax.all_to_all(merged, 'head', 0, 0)  5.32 us
    pallas_call x1, Pallas kernels, shards(): pl.pallas_call(late_kernel, out_shape=jax.ShapeDtypeStruct((ROW, width +...  4.71 us
  transfers between devices with their start and end apart: 12, of which 4 were waited for; matrix products, arithmetic and copies ran while one was open for 3% of the time, Pallas kernels for 14%

profile of v2, /device:TPU:1, one launch (start us, length us, event | category | flops | bytes accessed | tf_op | source)
XLA Modules:
  0.0 132.9 jit_solution(1491196381009739665)
XLA Ops:
  0.1 1.4 %maximum_maximum_fusion.text_in = bf16[16,256]{1,0:T(8,128)(2,1)} fusion(bf16[4,256]{1,0:T(4,128)(2,1)} %param.14, bf16[4,256]{1,0:T(4,128)(2,1)} %param.13, bf16[16]{0:T(256)(128)(2,1)S(1)} %pad.11.clone), kind=kLoop, calls=%fused_computation.9 | loop fusion | flops 24576 | bytes 12320 | tf_op jit(solution)/shard_map/concatenate | solution.py:408
  1.5 2.4 %key_message.1.own = bf16[528,256]{1,0:T(8,128)(2,1)} custom-call(bf16[256,256]{1,0:T(8,128)(2,1)} %k_in.1, bf16[256,256]{1,0:T(8,128)(2,1)} %v_in.1, bf16[16,256]{1,0:T(8,128)(2,1)} %maximum_maximum_fusion.text_in), custom_call_target="tpu_custom_call" | custom-call | tf_op jit(solution)/shard_map/key_message/pallas_call | solution.py:412
  3.9 2.2 %query_message.1 = bf16[8,256,256]{2,1,0:T(8,128)(2,1)} custom-call(bf16[256,256]{1,0:T(8,128)(2,1)} %q_in), custom_call_target="tpu_custom_call" | custom-call | tf_op jit(solution)/shard_map/query_message/pallas_call | solution.py:422
  6.1 10.3 %all-to-all-start = ((bf16[8,256,256]{2,1,0:T(8,128)(2,1)}), bf16[8,256,256]{2,1,0:T(8,128)(2,1)S(1)}, u32[]{:S(2)}, u32[]{:S(2)}) async-start(bf16[8,256,256]{2,1,0:T(8,128)(2,1)} %query_message.1), calls=%async_computation | async-start | bytes 2097152 | tf_op jit(solution)/shard_map/all_to_all | solution.py:452
  16.5 1.9 %collective-permute-start = (bf16[528,256]{1,0:T(8,128)(2,1)S(1)}, bf16[528,256]{1,0:T(8,128)(2,1)S(1)}, u32[]{:S(2)}, u32[]{:S(2)}) collective-permute-start(bf16[528,256]{1,0:T(8,128)(2,1)S(1)} %copy-done), channel_id=1, source_target_pairs={{0,64},{8,72},{16,80},{24,88},{32,96},{40,104},{48,112},{56,120},{... | collective-permute-start | bytes 811016 | tf_op jit(solution)/shard_map/ppermute | solution.py:35
  18.4 6.1 %collective-permute-start.2 = (bf16[528,256]{1,0:T(8,128)(2,1)S(1)}, bf16[528,256]{1,0:T(8,128)(2,1)S(1)}, u32[]{:S(2)}, u32[]{:S(2)}) collective-permute-start(bf16[528,256]{1,0:T(8,128)(2,1)S(1)} %copy-done), channel_id=1, source_target_pairs={{0,448},{8,456},{16,464},{24,472},{32,480},{40,488},{48,496},{56,5... | collective-permute-start | bytes 811016 | tf_op jit(solution)/shard_map/ppermute | solution.py:35
  25.2 4.2 %collective-permute-done.f1 = bf16[528,256]{1,0:T(8,128)(2,1)S(1)} collective-permute-done((bf16[528,256]{1,0:T(8,128)(2,1)S(1)}, bf16[528,256]{1,0:T(8,128)(2,1)S(1)}, u32[]{:S(2)}, u32[]{:S(2)}) %collective-permute-start) | collective-permute-done | bytes 270368 | tf_op jit(solution)/shard_map/ppermute | solution.py:35
  29.4 1.9 %collective-permute-start.1 = (bf16[528,256]{1,0:T(8,128)(2,1)S(1)}, bf16[528,256]{1,0:T(8,128)(2,1)S(1)}, u32[]{:S(2)}, u32[]{:S(2)}) collective-permute-start(bf16[528,256]{1,0:T(8,128)(2,1)S(1)} %collective-permute-done.f1), channel_id=1, source_target_pairs={{0,64},{8,72},{16,80},{24,88},{32,96},{40,104},{48,112},{56,120},{... | collective-permute-start | bytes 811016 | tf_op jit(solution)/shard_map/ppermute | solution.py:35
  31.4 4.6 %collective-permute-start.3 = (bf16[528,256]{1,0:T(8,128)(2,1)S(1)}, bf16[528,256]{1,0:T(8,128)(2,1)S(1)}, u32[]{:S(2)}, u32[]{:S(2)}) collective-permute-start(bf16[528,256]{1,0:T(8,128)(2,1)S(1)} %collective-permute-done.2.b1), channel_id=1, source_target_pairs={{0,448},{8,456},{16,464},{24,472},{32,480},{40,488},{48,496},{56,5... | collective-permute-start | bytes 811016 | tf_op jit(solution)/shard_map/ppermute | solution.py:35
  36.0 0.7 copy.18.far_ref
  36.7 0.7 copy.19.width_ref
  37.4 0.7 pad_add_fusion.1.where_ref
  38.1 2.5 %weight_message.1 = bf16[8,64,384]{2,1,0:T(8,128)(2,1)} custom-call(s32[3]{0:T(128)} %pad_add_fusion.1.where_ref, bf16[256,3072]{1,0:T(8,128)(2,1)} %w_in.1), custom_call_target="tpu_custom_call" | custom-call | tf_op jit(solution)/shard_map/weight_message/pallas_call | solution.py:431
  40.5 1.7 %lists.1.table = s32[16,128]{1,0:T(8,128)} custom-call(s32[3]{0:T(128)} %pad_add_fusion.1.where_ref, s32[128,30]{1,0:T(8,128)} %copy.18.far_ref, s32[64,5]{1,0:T(8,128)} %copy.19.width_ref), custom_call_target="tpu_custom_call" | custom-call | flops 1000000000 | bytes 100000 | tf_op jit(solution)/shard_map/lists/pallas_call | solution.py:440
  42.2 1.9 %collective-permute-start.4 = (bf16[528,256]{1,0:T(8,128)(2,1)S(1)}, bf16[528,256]{1,0:T(8,128)(2,1)S(1)}, u32[]{:S(2)}, u32[]{:S(2)}) collective-permute-start(bf16[528,256]{1,0:T(8,128)(2,1)S(1)} %collective-permute-done.1.f2), channel_id=1, source_target_pairs={{0,64},{8,72},{16,80},{24,88},{32,96},{40,104},{48,112},{56,120},{... | collective-permute-start | bytes 811016 | tf_op jit(solution)/shard_map/ppermute | solution.py:35
  44.1 4.6 %collective-permute-start.5 = (bf16[528,256]{1,0:T(8,128)(2,1)S(1)}, bf16[528,256]{1,0:T(8,128)(2,1)S(1)}, u32[]{:S(2)}, u32[]{:S(2)}) collective-permute-start(bf16[528,256]{1,0:T(8,128)(2,1)S(1)} %collective-permute-done.3.b2), channel_id=1, source_target_pairs={{0,448},{8,456},{16,464},{24,472},{32,480},{40,488},{48,496},{56,5... | collective-permute-start | bytes 811016 | tf_op jit(solution)/shard_map/ppermute | solution.py:35
  48.8 2.4 %collective-permute-start.6 = (bf16[528,256]{1,0:T(8,128)(2,1)S(1)}, bf16[528,256]{1,0:T(8,128)(2,1)S(1)}, u32[]{:S(2)}, u32[]{:S(2)}) collective-permute-start(bf16[528,256]{1,0:T(8,128)(2,1)S(1)} %broadcast_select_fusion), channel_id=1, source_target_pairs={{0,128},{8,392},{16,144},{24,408},{32,160},{40,424},{48,176},{56,4... | collective-permute-start | bytes 811016 | tf_op jit(solution)/shard_map/ppermute | solution.py:458
  51.2 6.8 %all-to-all-start.1 = ((bf16[8,64,384]{2,1,0:T(8,128)(2,1)}), bf16[8,64,384]{2,1,0:T(8,128)(2,1)}, u32[]{:S(2)}, u32[]{:S(2)}) async-start(bf16[8,64,384]{2,1,0:T(8,128)(2,1)} %weight_message.1), calls=%async_computation.1 | async-start | bytes 786432 | tf_op jit(solution)/shard_map/all_to_all | solution.py:464
  58.1 8.5 %attend_early.1 = (f32[8,256,256]{2,1,0:T(8,128)S(1)}, f32[8,8,256]{2,1,0:T(8,128)S(1)}) custom-call(s32[16,128]{1,0:T(8,128)S(1)} %copy-done.1, bf16[8,256,256]{2,1,0:T(8,128)(2,1)S(1)} %all-to-all-done.q_in, bf16[528,256]{1,0:T(8,128)(2,1)S(1)} %copy-done, bf16[528,256]{1,0:T(8,128)(2,1)S(1)} %collective-permute-done.f1, ...), custom_call_target="tpu_custom_call" | custom-call | flops 6000000000 | bytes 5000000 | tf_op jit(solution)/shard_map/attend_early/pallas_call | solution.py:466
  66.6 4.7 %attend_late.1 = bf16[8,272,256]{2,1,0:T(8,128)(2,1)S(1)} custom-call(s32[16,128]{1,0:T(8,128)S(1)} %copy-done.1, bf16[8,256,256]{2,1,0:T(8,128)(2,1)S(1)} %all-to-all-done.q_in, bf16[528,256]{1,0:T(8,128)(2,1)S(1)} %collective-permute-done.4.f3, bf16[528,256]{1,0:T(8,128)(2,1)S(1)} %collective-permute-done.5.b3, ...), custom_call_target="tpu_custom_call" | custom-call | flops 4000000000 | bytes 5000000 | tf_op jit(solution)/shard_map/attend_late/pallas_call | solution.py:479
  71.4 22.1 %all_to_all.20.part_ref = bf16[8,272,256]{2,1,0:T(8,128)(2,1)S(1)} all-to-all(bf16[8,272,256]{2,1,0:T(8,128)(2,1)S(1)} %attend_late.1), channel_id=1, replica_groups={{0,8,16,24,32,40,48,56},{64,72,80,88,96,104,112,120},{128,136,144,152,1..., dimensions={0} | all-to-all | bytes 2228224 | tf_op jit(solution)/shard_map/all_to_all | solution.py:491
  93.5 2.2 %collective-permute-start.7 = (bf16[8,64,384]{2,1,0:T(8,128)(2,1)}, bf16[8,64,384]{2,1,0:T(8,128)(2,1)S(1)}, u32[]{:S(2)}, u32[]{:S(2)}) collective-permute-start(bf16[8,64,384]{2,1,0:T(8,128)(2,1)} %all-to-all-done.1), channel_id=1, source_target_pairs={{0,16},{8,24},{16,0},{24,8},{32,48},{40,56},{48,32},{56,40},{64,80... | collective-permute-start | bytes 1179656 | tf_op jit(solution)/shard_map/ppermute | solution.py:503
  95.7 1.3 merge.1
  97.0 5.3 %all-to-all-start.3 = ((bf16[8,256,256]{2,1,0:T(8,128)(2,1)}), bf16[8,256,256]{2,1,0:T(8,128)(2,1)S(1)}, u32[]{:S(2)}, u32[]{:S(2)}) async-start(bf16[8,256,256]{2,1,0:T(8,128)(2,1)} %merge.1), calls=%async_computation.3 | async-start | bytes 2097152 | tf_op jit(solution)/shard_map/all_to_all | solution.py:501
  102.3 3.2 %collective-permute-done.7 = bf16[8,64,384]{2,1,0:T(8,128)(2,1)S(1)} collective-permute-done((bf16[8,64,384]{2,1,0:T(8,128)(2,1)}, bf16[8,64,384]{2,1,0:T(8,128)(2,1)S(1)}, u32[]{:S(2)}, u32[]{:S(2)}) %collective-permute-start.7) | collective-permute-done | bytes 393248 | tf_op jit(solution)/shard_map/ppermute | solution.py:503
  105.5 1.1 select_bitcast_fusion.3
  106.7 3.5 %collective-permute-start.8 = (bf16[8,2,64,384]{3,2,0,1:T(8,128)(2,1)S(1)}, bf16[8,2,64,384]{3,2,0,1:T(8,128)(2,1)S(1)}, u32[]{:S(2)}, u32[]{:S(2)}) collective-permute-start(bf16[8,2,64,384]{3,2,0,1:T(8,128)(2,1)S(1)} %pad_maximum_fusion.1), channel_id=1, source_target_pairs={{0,8},{8,0},{16,24},{24,16},{32,40},{40,32},{48,56},{56,48},{64,72... | collective-permute-start | bytes 2359304 | tf_op jit(solution)/shard_map/ppermute | solution.py:505
  110.2 1.9 %collective-permute-done.8 = bf16[8,2,64,384]{3,2,0,1:T(8,128)(2,1)S(1)} collective-permute-done((bf16[8,2,64,384]{3,2,0,1:T(8,128)(2,1)S(1)}, bf16[8,2,64,384]{3,2,0,1:T(8,128)(2,1)S(1)}, u32[]{:S(2)}, u32[]{:S(2)}) %collective-permute-start.8) | collective-permute-done | bytes 786464 | tf_op jit(solution)/shard_map/ppermute | solution.py:505
  112.1 0.2 select_bitcast_fusion.1
  112.3 0.2 pad_maximum_fusion
  112.7 18.8 %all-to-all-done.3 = bf16[8,256,256]{2,1,0:T(8,128)(2,1)S(1)} async-done(((bf16[8,256,256]{2,1,0:T(8,128)(2,1)}), bf16[8,256,256]{2,1,0:T(8,128)(2,1)S(1)}, u32[]{:S(2)}, u32[]{:S(2)}) %all-to-all-start.3) | async-done | bytes 1048608 | tf_op jit(solution)/shard_map/all_to_all | solution.py:501
  131.5 1.4 %convolution_convert_fusion = bf16[256,384]{1,0:T(8,128)(2,1)} fusion(bf16[2048,256]{1,0:T(8,128)(2,1)S(1)} %bitcast.16, bf16[2048,384]{1,0:T(8,128)(2,1)S(1)} %bitcast.15), kind=kOutput, calls=%fused_computation.1 | convolution fusion | flops 402751488 | bytes 2818048 | tf_op jit(solution)/shard_map/dot_general | solution.py:508
  (24 shorter events, 0.4 us)
Async XLA Ops:
  3.9 12.6 %copy-start = (bf16[528,256]{1,0:T(8,128)(2,1)S(1)}, bf16[528,256]{1,0:T(8,128)(2,1)}, u32[]{:S(2)}) copy-start(bf16[528,256]{1,0:T(8,128)(2,1)} %key_message.1.own) | copy-start | bytes 811012
  3.9 32.0 %copy-start.2 = (s32[128,29]{0,1:T(8,128)S(1)}, s32[128,29]{0,1:T(8,128)}, u32[]{:S(2)}) copy-start(s32[128,29]{0,1:T(8,128)} %param.17) | copy-start | bytes 44548
  3.9 32.0 %copy-start.4 = (s32[128]{0:T(128)S(1)}, s32[128]{0:T(128)}, u32[]{:S(2)}) copy-start(s32[128]{0:T(128)} %param.18) | copy-start | bytes 1540
  3.9 32.8 %copy-start.3 = (s32[64,5]{0,1:T(8,128)S(1)}, s32[64,5]{0,1:T(8,128)}, u32[]{:S(2)}) copy-start(s32[64,5]{0,1:T(8,128)} %param.16) | copy-start | bytes 3844
  6.1 45.1 %all-to-all-start = ((bf16[8,256,256]{2,1,0:T(8,128)(2,1)}), bf16[8,256,256]{2,1,0:T(8,128)(2,1)S(1)}, u32[]{:S(2)}, u32[]{:S(2)}) async-start(bf16[8,256,256]{2,1,0:T(8,128)(2,1)} %query_message.1), calls=%async_computation | async-start | bytes 2097152 | tf_op jit(solution)/shard_map/all_to_all | solution.py:452
  16.5 13.0 %collective-permute-start = (bf16[528,256]{1,0:T(8,128)(2,1)S(1)}, bf16[528,256]{1,0:T(8,128)(2,1)S(1)}, u32[]{:S(2)}, u32[]{:S(2)}) collective-permute-start(bf16[528,256]{1,0:T(8,128)(2,1)S(1)} %copy-done), channel_id=1, source_target_pairs={{0,64},{8,72},{16,80},{24,88},{32,96},{40,104},{48,112},{56,120},{... | collective-permute-start | bytes 811016 | tf_op jit(solution)/shard_map/ppermute | solution.py:35
  18.4 13.0 %collective-permute-start.2 = (bf16[528,256]{1,0:T(8,128)(2,1)S(1)}, bf16[528,256]{1,0:T(8,128)(2,1)S(1)}, u32[]{:S(2)}, u32[]{:S(2)}) collective-permute-start(bf16[528,256]{1,0:T(8,128)(2,1)S(1)} %copy-done), channel_id=1, source_target_pairs={{0,448},{8,456},{16,464},{24,472},{32,480},{40,488},{48,496},{56,5... | collective-permute-start | bytes 811016 | tf_op jit(solution)/shard_map/ppermute | solution.py:35
  29.4 12.8 %collective-permute-start.1 = (bf16[528,256]{1,0:T(8,128)(2,1)S(1)}, bf16[528,256]{1,0:T(8,128)(2,1)S(1)}, u32[]{:S(2)}, u32[]{:S(2)}) collective-permute-start(bf16[528,256]{1,0:T(8,128)(2,1)S(1)} %collective-permute-done.f1), channel_id=1, source_target_pairs={{0,64},{8,72},{16,80},{24,88},{32,96},{40,104},{48,112},{56,120},{... | collective-permute-start | bytes 811016 | tf_op jit(solution)/shard_map/ppermute | solution.py:35
  31.4 10.9 %collective-permute-start.3 = (bf16[528,256]{1,0:T(8,128)(2,1)S(1)}, bf16[528,256]{1,0:T(8,128)(2,1)S(1)}, u32[]{:S(2)}, u32[]{:S(2)}) collective-permute-start(bf16[528,256]{1,0:T(8,128)(2,1)S(1)} %collective-permute-done.2.b1), channel_id=1, source_target_pairs={{0,448},{8,456},{16,464},{24,472},{32,480},{40,488},{48,496},{56,5... | collective-permute-start | bytes 811016 | tf_op jit(solution)/shard_map/ppermute | solution.py:35
  42.2 15.9 %copy-start.1 = (s32[16,128]{1,0:T(8,128)S(1)}, s32[16,128]{1,0:T(8,128)}, u32[]{:S(2)}) copy-start(s32[16,128]{1,0:T(8,128)} %lists.1.table) | copy-start | bytes 24580
  42.2 24.4 %collective-permute-start.4 = (bf16[528,256]{1,0:T(8,128)(2,1)S(1)}, bf16[528,256]{1,0:T(8,128)(2,1)S(1)}, u32[]{:S(2)}, u32[]{:S(2)}) collective-permute-start(bf16[528,256]{1,0:T(8,128)(2,1)S(1)} %collective-permute-done.1.f2), channel_id=1, source_target_pairs={{0,64},{8,72},{16,80},{24,88},{32,96},{40,104},{48,112},{56,120},{... | collective-permute-start | bytes 811016 | tf_op jit(solution)/shard_map/ppermute | solution.py:35
  44.1 22.5 %collective-permute-start.5 = (bf16[528,256]{1,0:T(8,128)(2,1)S(1)}, bf16[528,256]{1,0:T(8,128)(2,1)S(1)}, u32[]{:S(2)}, u32[]{:S(2)}) collective-permute-start(bf16[528,256]{1,0:T(8,128)(2,1)S(1)} %collective-permute-done.3.b2), channel_id=1, source_target_pairs={{0,448},{8,456},{16,464},{24,472},{32,480},{40,488},{48,496},{56,5... | collective-permute-start | bytes 811016 | tf_op jit(solution)/shard_map/ppermute | solution.py:35
  48.8 17.9 %collective-permute-start.6 = (bf16[528,256]{1,0:T(8,128)(2,1)S(1)}, bf16[528,256]{1,0:T(8,128)(2,1)S(1)}, u32[]{:S(2)}, u32[]{:S(2)}) collective-permute-start(bf16[528,256]{1,0:T(8,128)(2,1)S(1)} %broadcast_select_fusion), channel_id=1, source_target_pairs={{0,128},{8,392},{16,144},{24,408},{32,160},{40,424},{48,176},{56,4... | collective-permute-start | bytes 811016 | tf_op jit(solution)/shard_map/ppermute | solution.py:458
  51.2 20.1 %all-to-all-start.1 = ((bf16[8,64,384]{2,1,0:T(8,128)(2,1)}), bf16[8,64,384]{2,1,0:T(8,128)(2,1)}, u32[]{:S(2)}, u32[]{:S(2)}) async-start(bf16[8,64,384]{2,1,0:T(8,128)(2,1)} %weight_message.1), calls=%async_computation.1 | async-start | bytes 786432 | tf_op jit(solution)/shard_map/all_to_all | solution.py:464
  93.5 12.0 %collective-permute-start.7 = (bf16[8,64,384]{2,1,0:T(8,128)(2,1)}, bf16[8,64,384]{2,1,0:T(8,128)(2,1)S(1)}, u32[]{:S(2)}, u32[]{:S(2)}) collective-permute-start(bf16[8,64,384]{2,1,0:T(8,128)(2,1)} %all-to-all-done.1), channel_id=1, source_target_pairs={{0,16},{8,24},{16,0},{24,8},{32,48},{40,56},{48,32},{56,40},{64,80... | collective-permute-start | bytes 1179656 | tf_op jit(solution)/shard_map/ppermute | solution.py:503
  97.0 34.5 %all-to-all-start.3 = ((bf16[8,256,256]{2,1,0:T(8,128)(2,1)}), bf16[8,256,256]{2,1,0:T(8,128)(2,1)S(1)}, u32[]{:S(2)}, u32[]{:S(2)}) async-start(bf16[8,256,256]{2,1,0:T(8,128)(2,1)} %merge.1), calls=%async_computation.3 | async-start | bytes 2097152 | tf_op jit(solution)/shard_map/all_to_all | solution.py:501
  106.7 5.4 %collective-permute-start.8 = (bf16[8,2,64,384]{3,2,0,1:T(8,128)(2,1)S(1)}, bf16[8,2,64,384]{3,2,0,1:T(8,128)(2,1)S(1)}, u32[]{:S(2)}, u32[]{:S(2)}) collective-permute-start(bf16[8,2,64,384]{3,2,0,1:T(8,128)(2,1)S(1)} %pad_maximum_fusion.1), channel_id=1, source_target_pairs={{0,8},{8,0},{16,24},{24,16},{32,40},{40,32},{48,56},{56,48},{64,72... | collective-permute-start | bytes 2359304 | tf_op jit(solution)/shard_map/ppermute | solution.py:505

commit v3 on v2

--- a/solution.py
+++ b/solution.py
@@ -22,6 +22,8 @@
 GROUPS_AT_ONCE = 4
 MESSAGE = 4 * BLK + TPAD
 NEAR_AT = ROW
+COUNT_AT = 32
+WIDTH_AT = 40
 LEN_AT = ROW + 1
 WHERE_AT = ROW + 2
 
@@ -42,14 +44,16 @@
             yield a, h, tile.T.astype(jnp.bfloat16)
 
 
-def key_kernel(k_in, v_in, text_in, kv_out, v_buf, sems):
+def key_kernel(k_in, v_in, tk_in, tv_in, kv_out, v_buf, sems):
     copies = [
         pltpu.make_async_copy(v_in, v_buf, sems.at[0]),
         pltpu.make_async_copy(k_in, kv_out.at[: 2 * BLK], sems.at[1]),
     ]
     for copy in copies:
         copy.start()
-    kv_out[4 * BLK :, :] = text_in[...]
+    blank = jnp.zeros((TPAD - 2 * tk_in.shape[0], kv_out.shape[1]), jnp.float32)
+    text = (tk_in[...].astype(jnp.float32), tv_in[...].astype(jnp.float32), blank)
+    kv_out[4 * BLK :, :] = jnp.concatenate(text, axis=0).astype(jnp.bfloat16)
     copies[0].wait()
     for a, h, tile in turned(v_buf):
         kv_out[(2 + a) * BLK : (3 + a) * BLK, h * HD : (h + 1) * HD] = tile
@@ -65,31 +69,30 @@
             q_out[i, a * BLK : (a + 1) * BLK, h * HD : (h + 1) * HD] = tile
 
 
-def weight_kernel(where_ref, w_in, w_out, sems):
-    heads, rows, columns = w_out.shape
-    start = pl.multiple_of((where_ref[1] & 3) * rows, rows)
+def list_kernel(where_ref, far_ref, count_ref, width_ref, w_in, table_ref, w_out, wide, tall, sems):
+    z = where_ref[0]
+    r = where_ref[1]
+    heads, quarter, columns = w_out.shape
+    start = pl.multiple_of(((z & 1) * 2 + (r & 1)) * quarter, quarter)
     copies = [
         pltpu.make_async_copy(
-            w_in.at[pl.ds(start, rows), i * columns : (i + 1) * columns], w_out.at[i], sems.at[i]
+            w_in.at[pl.ds(start, quarter), i * columns : (i + 1) * columns], w_out.at[i], sems.at[i]
         )
         for i in range(heads)
     ]
     for copy in copies:
         copy.start()
-    for copy in copies:
-        copy.wait()
-
-
-def list_kernel(where_ref, far_ref, width_ref, table_ref):
-    z = where_ref[0]
-    r = where_ref[1]
     rows = 2 * ROW
-    slots = far_ref.shape[1] - 1
-    mine = far_ref[pl.ds(pl.multiple_of(z * rows, rows), rows), :]
+    slots = far_ref.shape[0]
+    wide[...] = jnp.zeros(wide.shape, jnp.int32)
+    wide[:slots, :] = far_ref[...]
+    wide[COUNT_AT : COUNT_AT + 1, :] = count_ref[...]
+    wide[WIDTH_AT : WIDTH_AT + 2 * NEAR + 1, : ROW * ROW] = width_ref[...]
+    tall[...] = wide[...].T
+    mine = tall[pl.ds(pl.multiple_of(z * rows, rows), rows), :]
     place = lax.broadcasted_iota(jnp.int32, mine.shape, 1)
-    count = jnp.sum(jnp.where(place == slots, mine, 0), axis=1, keepdims=True)
-    live = place < count
-    live = live & (place < slots)
+    count = jnp.sum(jnp.where(place == COUNT_AT, mine, 0), axis=1, keepdims=True)
+    live = (place < count) & (place < slots)
     lane = lax.broadcasted_iota(jnp.int32, (rows, BLK), 1)
     table = jnp.where(lane == LEN_AT, where_ref[2], 0)
     table = jnp.where(lane == WHERE_AT, z, table)
@@ -98,8 +101,8 @@
         group = ((z + step) & (ROW - 1)) * ROW + r
         asked = jnp.where(live & ((mine >> 1) == group), 1 + (mine & 1), 0)
         table = jnp.where(lane == s, jnp.sum(asked, axis=1, keepdims=True), table)
-    widths = width_ref[pl.ds(pl.multiple_of(z * ROW, ROW), ROW), :]
-    place = lax.broadcasted_iota(jnp.int32, widths.shape, 1)
+    widths = tall[pl.ds(pl.multiple_of(z * ROW, ROW), ROW), :]
+    place = lax.broadcasted_iota(jnp.int32, widths.shape, 1) - WIDTH_AT
     query = lax.broadcasted_iota(jnp.int32, widths.shape, 0)
     offset = (r - query + NEAR) & (ROW - 1)
     group = z * ROW + query + offset - NEAR
@@ -109,6 +112,8 @@
     near = jnp.sum(jnp.where(valid, widths * 16 + slot, 0), axis=1, keepdims=True)
     near = jnp.concatenate((near, jnp.zeros((rows - ROW, 1), jnp.int32)), axis=0)
     table_ref[...] = jnp.where(lane == NEAR_AT, near, table)
+    for copy in copies:
+        copy.wait()
 
 
 def three_parts(x):
@@ -134,25 +139,21 @@
     return lax.fori_loop(0, 2 * ROW, one_block, jnp.int32(0))
 
 
-def set_text(kv, table, steps, bias, text_k, text_v):
+def set_text(tiles, table, bias, text_k, text_v):
     z = table[0, WHERE_AT]
     r = table[0, WHERE_AT + 1]
-    total = text_k.shape[0]
     row = lax.broadcasted_iota(jnp.int32, (TEXT_ROWS, 2 * BLK), 0)
     keys = []
     vals = []
-    for s, step in enumerate(steps):
+    for s, step in enumerate(EARLY + LATE):
         first = (((z + step) & (ROW - 1)) * ROW + r) * 4
         alive = (row < 4) & (first + row < table[0, LEN_AT])
         bias[s * TEXT_ROWS : (s + 1) * TEXT_ROWS, :] = jnp.where(alive, 0.0, NEG)
-        tile = kv[s, 4 * BLK : 4 * BLK + TPAD, :].astype(jnp.float32)[:TEXT_ROWS]
+        tile = tiles[s].astype(jnp.float32)[:TEXT_ROWS]
         keys.append(tile)
         vals.append(pltpu.roll(tile, 4, 0))
-    spare = total - len(steps) * TEXT_ROWS
-    bias[total - spare :, :] = jnp.full((spare, 2 * BLK), NEG, jnp.float32)
-    keys.append(jnp.zeros((spare, 2 * HD), jnp.float32))
     text_k[...] = jnp.concatenate(keys, axis=0).astype(jnp.bfloat16)
-    vals.append(jnp.zeros((HD - len(steps) * TEXT_ROWS, 2 * HD), jnp.float32))
+    vals.append(jnp.zeros((HD - ROW * TEXT_ROWS, 2 * HD), jnp.float32))
     vals = jnp.concatenate(vals, axis=0)
     for h in range(2):
         text_v[h] = vals[:, h * HD : (h + 1) * HD].T.astype(jnp.bfloat16)
@@ -248,33 +249,22 @@
     lax.fori_loop(0, (count + TOGETHER - 1) // TOGETHER, step, 0)
 
 
-def wait_all(pairs, sems):
+def start_all(pairs, sems):
     copies = [pltpu.make_async_copy(src, dst, sems.at[i]) for i, (src, dst) in enumerate(pairs)]
     for copy in copies:
         copy.start()
-    for copy in copies:
-        copy.wait()
-
-
-def early_kernel(
-    table, q_in, own, f1, b1, f2, b2, acc, stat, q_ref, kv, units, sems, bias, text_k, text_v
-):
-    wait_all([(x, kv.at[i]) for i, x in enumerate((own, f1, b1, f2, b2))] + [(q_in, q_ref)], sems)
-    set_text(kv, table, EARLY, bias, text_k, text_v)
+    return [copy.wait for copy in copies]
+
+
+def early_kernel(table, q_in, own, f1, b1, f2, b2, acc, stat, q_ref, kv, units, sems):
+    waits = start_all([(x, kv.at[i]) for i, x in enumerate((own, f1, b1, f2, b2))] + [(q_in, q_ref)], sems)
+    count = list_units(table, 0, len(EARLY), units)
+    for wait in waits:
+        wait()
     offset = lax.broadcasted_iota(jnp.int32, (2 * BLK, 2 * BLK), 0) - lax.broadcasted_iota(
         jnp.int32, (2 * BLK, 2 * BLK), 1
     )
     distance = jnp.abs(offset)
-
-    def some_text(step, _):
-        cases = group_cases(step, GROUPS_AT_ONCE)
-        for (g, h), state in zip(cases, text_step(q_ref, cases, text_k, text_v, bias)):
-            write_state(acc, stat, g, h, state)
-        for g, h in cases[::2]:
-            stat[g, 4:8, :] = jnp.zeros((4, 2 * BLK), jnp.float32)
-        return 0
-
-    lax.fori_loop(0, ROW // GROUPS_AT_ONCE, some_text, 0)
 
     def one_group(g, _):
         near = table[g, NEAR_AT]
@@ -288,7 +278,7 @@
                 scores.append(jnp.where(distance < (near >> 4), s, NEG))
             fresh = []
             for h, s in enumerate(scores):
-                top = jnp.max(s, axis=0, keepdims=True)
+                top = jnp.maximum(jnp.max(s, axis=0, keepdims=True), FLOOR)
                 p = jnp.exp2(s - top)
                 values = jnp.concatenate(
                     (kv[who, 2 * BLK : 3 * BLK, head_rows(h)], kv[who, 3 * BLK : 4 * BLK, head_rows(h)]),
@@ -296,31 +286,34 @@
                 )
                 fresh.append((top, jnp.sum(p, axis=0, keepdims=True), product(values, p.astype(jnp.bfloat16))))
             for h, new in enumerate(fresh):
-                write_state(acc, stat, g, h, joined(read_state(acc, stat, g, h), new))
+                write_state(acc, stat, g, h, new)
+            stat[g, 4:8, :] = jnp.zeros((4, 2 * BLK), jnp.float32)
+
+        @pl.when(near == 0)
+        def _():
+            acc[g, :, :] = jnp.zeros((2 * HD, 2 * BLK), jnp.float32)
+            row = lax.broadcasted_iota(jnp.int32, (8, 2 * BLK), 0)
+            stat[g, :, :] = jnp.where((row == 0) | (row == 2), FLOOR, 0.0)
 
         return 0
 
     lax.fori_loop(0, ROW, one_group, 0)
-    walk_units(units, list_units(table, 0, len(EARLY), units), q_ref, kv, acc, stat)
+    walk_units(units, count, q_ref, kv, acc, stat)
 
 
 def late_kernel(
-    table, q_in, f3, b3, far4, acc_in, stat_in, out_ref,
-    q_ref, kv, units, sems, bias, text_k, text_v, acc, stat,
+    table, q_in, own, f1, b1, f2, b2, f3, b3, far4, acc_in, stat_in, out_ref, acc, stat,
+    q_ref, kv, units, sems, tiles, bias, text_k, text_v,
 ):
-    wait_all(
-        [
-            (f3, kv.at[0]),
-            (b3, kv.at[1]),
-            (far4, kv.at[2]),
-            (q_in, q_ref),
-            (acc_in, acc),
-            (stat_in, stat),
-        ],
-        sems,
-    )
-    set_text(kv, table, LATE, bias, text_k, text_v)
-    walk_units(units, list_units(table, len(EARLY), len(LATE), units), q_ref, kv, acc, stat)
+    pairs = [(f3, kv.at[0]), (b3, kv.at[1]), (far4, kv.at[2]), (q_in, q_ref)]
+    for i, x in enumerate((own, f1, b1, f2, b2, f3, b3, far4)):
+        pairs.append((x.at[4 * BLK :], tiles.at[i]))
+    waits = start_all(pairs, sems)
+    count = list_units(table, len(EARLY), len(LATE), units)
+    for wait in waits:
+        wait()
+    set_text(tiles, table, bias, text_k, text_v)
+    walk_units(units, count, q_ref, kv, acc, stat)
 
     def some_groups(step, _):
         cases = group_cases(step, GROUPS_AT_ONCE)
@@ -375,14 +368,20 @@
     return pltpu.CompilerParams(vmem_limit_bytes=32 << 20)
 
 
-def attend_scratch(slots, copies, text_rows):
+def attend_scratch(slots, copies):
     return [
         pltpu.VMEM((ROW, 2 * BLK, 2 * HD), jnp.bfloat16),
         pltpu.VMEM((slots, MESSAGE, 2 * HD), jnp.bfloat16),
         pltpu.SMEM((2 * ROW * slots + 8,), jnp.int32),
         pltpu.SemaphoreType.DMA((copies,)),
-        pltpu.VMEM((text_rows, 2 * BLK), jnp.float32),
-        pltpu.VMEM((text_rows, 2 * HD), jnp.bfloat16),
+    ]
+
+
+def text_scratch():
+    return [
+        pltpu.VMEM((ROW, TPAD, 2 * HD), jnp.bfloat16),
+        pltpu.VMEM((ROW * TEXT_ROWS, 2 * BLK), jnp.float32),
+        pltpu.VMEM((ROW * TEXT_ROWS, 2 * HD), jnp.bfloat16),
         pltpu.VMEM((2, HD, HD), jnp.bfloat16),
     ]
 
@@ -405,19 +404,16 @@
     heads = lax.axis_size("head")
     columns = w_out.shape[1] // heads
 
-    text = jnp.concatenate(
-        (text_keys, text_values, jnp.zeros((TPAD - 2 * text_keys.shape[0], width), jnp.bfloat16)), axis=0
-    )
     whole = pltpu.CompilerParams(vmem_limit_bytes=60 << 20)
     kv = pl.pallas_call(
         key_kernel,
         out_shape=jax.ShapeDtypeStruct((MESSAGE, width), jnp.bfloat16),
-        in_specs=[anywhere(), anywhere(), vmem()],
+        in_specs=[anywhere(), anywhere(), vmem(), vmem()],
         out_specs=vmem(),
         scratch_shapes=[pltpu.VMEM((tokens, width), jnp.bfloat16), pltpu.SemaphoreType.DMA((2,))],
         compiler_params=whole,
         name="key_message",
-    )(keys, values, text)
+    )(keys, values, text_keys, text_values)
     kv, queries = lax.optimization_barrier((kv, queries))
     q_mine = pl.pallas_call(
         query_kernel,
@@ -428,30 +424,30 @@
         compiler_params=whole,
         name="query_message",
     )(queries)
-    quarter = pl.pallas_call(
-        weight_kernel,
-        out_shape=jax.ShapeDtypeStruct((heads, width // 4, columns), jnp.bfloat16),
-        in_specs=[smem(), anywhere()],
-        out_specs=vmem(),
-        scratch_shapes=[pltpu.SemaphoreType.DMA((heads,))],
+    table, quarter = pl.pallas_call(
+        list_kernel,
+        out_shape=(
+            jax.ShapeDtypeStruct((2 * ROW, BLK), jnp.int32),
+            jax.ShapeDtypeStruct((heads, width // 4, columns), jnp.bfloat16),
+        ),
+        in_specs=[smem(), vmem(), vmem(), vmem(), anywhere()],
+        out_specs=(vmem(), vmem()),
+        scratch_shapes=[
+            pltpu.VMEM((BLK, BLK), jnp.int32),
+            pltpu.VMEM((BLK, BLK), jnp.int32),
+            pltpu.SemaphoreType.DMA((heads,)),
+        ],
         compiler_params=whole,
-        name="weight_message",
-    )(where, w_out)
-    table = pl.pallas_call(
-        list_kernel,
-        out_shape=jax.ShapeDtypeStruct((2 * ROW, BLK), jnp.int32),
-        in_specs=[smem(), vmem(), vmem()],
-        out_specs=vmem(),
-        cost_estimate=pl.CostEstimate(flops=10**9, bytes_accessed=10**5, transcendentals=0),
+        cost_estimate=pl.CostEstimate(flops=40 * 10**9, bytes_accessed=10**5, transcendentals=0),
         name="lists",
-    )(where, jnp.concatenate((far_blocks, far_count[:, None]), axis=1), radial_width)
+    )(where, far_blocks.T, far_count[None, :], radial_width.T, w_out)
 
     count = ROW * ROW
     f1 = along_column(kv, 1)
     b1 = along_column(kv, -1)
     q_all = lax.all_to_all(q_mine, "seq", 0, 0, axis_index_groups=row_peers())
-    f2 = along_column(f1, 1)
-    b2 = along_column(b1, -1)
+    f2 = along_column(kv, 2)
+    b2 = along_column(kv, -2)
     f2, b2, table, quarter = lax.optimization_barrier((f2, b2, table, quarter))
     f3 = along_column(f2, 1)
     b3 = along_column(b2, -1)
@@ -471,25 +467,34 @@
         ),
         in_specs=[smem()] + [anywhere()] * 6,
         out_specs=(vmem(), vmem()),
-        scratch_shapes=attend_scratch(len(EARLY), 6, 48),
+        scratch_shapes=attend_scratch(len(EARLY), 6),
         compiler_params=kernel_params(),
         cost_estimate=pl.CostEstimate(flops=6 * 10**9, bytes_accessed=5 * 10**6, transcendentals=0),
         name="attend_early",
     )(table, q_all, kv, f1, b1, f2, b2)
-    part = pl.pallas_call(
+    part, _, _ = pl.pallas_call(
         late_kernel,
-        out_shape=jax.ShapeDtypeStruct((ROW, width + TPAD, tokens), jnp.bfloat16),
-        in_specs=[smem()] + [anywhere()] * 6,
-        out_specs=vmem(),
-        scratch_shapes=attend_scratch(len(LATE), 6, 32)
-        + [pltpu.VMEM((ROW, width, tokens), jnp.float32), pltpu.VMEM((ROW, 8, tokens), jnp.float32)],
+        out_shape=(
+            jax.ShapeDtypeStruct((ROW, width + TPAD, tokens), jnp.bfloat16),
+            jax.ShapeDtypeStruct(acc.shape, acc.dtype),
+            jax.ShapeDtypeStruct(stat.shape, stat.dtype),
+        ),
+        in_specs=[smem()] + [anywhere()] * 9 + [vmem()] * 2,
+        out_specs=(vmem(),) * 3,
+        scratch_shapes=attend_scratch(len(LATE), 4 + ROW) + text_scratch(),
+        input_output_aliases={10: 1, 11: 2},
         compiler_params=kernel_params(),
         cost_estimate=pl.CostEstimate(flops=4 * 10**9, bytes_accessed=5 * 10**6, transcendentals=0),
         name="attend_late",
-    )(table, q_all, f3, b3, far4, acc, stat)
+    )(table, q_all, kv, f1, b1, f2, b2, f3, b3, far4, acc, stat)
     part, quarter = lax.optimization_barrier((part, quarter))
     part = lax.all_to_all(part, "seq", 0, 0, axis_index_groups=row_peers())
-    part, quarter = lax.optimization_barrier((part, quarter))
+    low = (own & ROW) == 0
+    other = lax.ppermute(quarter, "seq", [(g, g ^ ROW) for g in range(count)])
+    halves = jnp.stack((jnp.where(low, quarter, other), jnp.where(low, other, quarter)), axis=1)
+    theirs = lax.ppermute(halves, "seq", [(g, g ^ 1) for g in range(count)])
+    even = (own & 1) == 0
+    w_mine = jnp.stack((jnp.where(even, halves, theirs), jnp.where(even, theirs, halves)), axis=2)
     merged = pl.pallas_call(
         merge_kernel,
         out_shape=jax.ShapeDtypeStruct((ROW, width, tokens), jnp.bfloat16),
@@ -499,12 +504,6 @@
         name="merge",
     )(part)
     attention = lax.all_to_all(merged, "head", 0, 0)
-    low = (own & 2) == 0
-    other = lax.ppermute(quarter, "seq", [(g, g ^ 2) for g in range(count)])
-    halves = jnp.stack((jnp.where(low, quarter, other), jnp.where(low, other, quarter)), axis=1)
-    theirs = lax.ppermute(halves, "seq", [(g, g ^ 1) for g in range(count)])
-    even = (own & 1) == 0
-    w_mine = jnp.stack((jnp.where(even, halves, theirs), jnp.where(even, theirs, halves)), axis=2)
     mixed = lax.dot_general(
         attention.reshape(heads * width, tokens),
         w_mine.reshape(heads * width, columns),

time: 134 us -> 125 us (0.933)
  blocking collectives: 22.1 us -> 0 us
  waiting for transfers between devices: 28.2 us -> 41.1 us
  starting transfers between devices: 51.7 us -> 56.6 us
  Pallas kernels: 23.3 us -> 20.4 us
  local copies, waits for them, and re-layouts: 1.72 us -> 0.18 us
    all_to_all x1 -> x0, blocking collectives: 22.1 us -> none  [shards(): part = lax.all_to_all(part, 'seq', 0, 0, axis_index_groups=row_peers())]
    all_to_all x0 -> x1, waiting for transfers between devices: none -> 13.9 us  [shards(): part = lax.all_to_all(part, 'seq', 0, 0, axis_index_groups=row_peers())]
    all_to_all x0 -> x1, starting transfers between devices: none -> 5.57 us  [shards(): part = lax.all_to_all(part, 'seq', 0, 0, axis_index_groups=row_peers())]
    ppermute x6, starting transfers between devices: 21 us -> 26.5 us  [along_column(): lax.ppermute(block, 'seq', [(g, (g + ROW * distance) % count) for g in ra...]
    all_to_all x1, starting transfers between devices: 10.3 us -> 5.82 us  [shards(): q_all = lax.all_to_all(q_mine, 'seq', 0, 0, axis_index_groups=row_peers())]
    ppermute x6, waiting for transfers between devices: 4.24 us -> 0.02 us  [along_column(): lax.ppermute(block, 'seq', [(g, (g + ROW * distance) % count) for g in ra...]
    ppermute x1, waiting for transfers between devices: 3.21 us -> 0.01 us  [shards(): other = lax.ppermute(quarter, 'seq', [(g, g ^ ROW) for g in range(count)])]
    all_to_all x1, waiting for transfers between devices: 18.8 us -> 21.2 us  [shards(): attention = lax.all_to_all(merged, 'head', 0, 0)]
  transfers between devices with their start and end apart: 12 -> 13, of which waited for: 4 -> 5; matrix products, arithmetic and copies ran while one was open for 3% -> 3% of each run, Pallas kernels for 14% -> 15%
where the time goes in v3:
time: 125 us; the launch traced here: 124 us
  starting transfers between devices  56.6 us (45%)
  waiting for transfers between devices  41.1 us (33%)
  Pallas kernels  20.4 us (16%)
  other arithmetic  3.31 us (3%)
  matrix products  1.42 us (1%)
    ppermute x6, starting transfers between devices, along_column(): lax.ppermute(block, 'seq', [(g, (g + ROW * distance) % count) for g in ra...  26.5 us
    all_to_all x1, waiting for transfers between devices, shards(): attention = lax.all_to_all(merged, 'head', 0, 0)  21.2 us
    all_to_all x1, waiting for transfers between devices, shards(): part = lax.all_to_all(part, 'seq', 0, 0, axis_index_groups=row_peers())  13.9 us
    pallas_call x1, Pallas kernels, shards(): pl.pallas_call(early_kernel, out_shape=(jax.ShapeDtypeStruct((ROW, width,...  6.95 us
    all_to_all x1, starting transfers between devices, shards(): quarter = lax.all_to_all(quarter, 'head', 0, 0)  6.82 us
    all_to_all x1, starting transfers between devices, shards(): q_all = lax.all_to_all(q_mine, 'seq', 0, 0, axis_index_groups=row_peers())  5.82 us
    all_to_all x1, starting transfers between devices, shards(): part = lax.all_to_all(part, 'seq', 0, 0, axis_index_groups=row_peers())  5.57 us
    pallas_call x1, Pallas kernels, shards(): pl.pallas_call(late_kernel, out_shape=(jax.ShapeDtypeStruct((ROW, width +...  4.92 us
  transfers between devices with their start and end apart: 13, of which 5 were waited for; matrix products, arithmetic and copies ran while one was open for 3% of the time, Pallas kernels for 15%

profile of v3, /device:TPU:1, one launch (start us, length us, event | category | flops | bytes accessed | tf_op | source)
XLA Modules:
  0.0 123.9 jit_solution(7021609654474741868)
XLA Ops:
  0.0 2.4 %key_message.1.own = bf16[528,256]{1,0:T(8,128)(2,1)} custom-call(bf16[256,256]{1,0:T(8,128)(2,1)} %k_in.1, bf16[256,256]{1,0:T(8,128)(2,1)} %v_in.1, bf16[4,256]{1,0:T(4,128)(2,1)} %tk_in.1, bf16[4,256]{1,0:T(4,128)(2,1)} %tv_in.1), custom_call_target="tpu_custom_call" | custom-call | tf_op jit(solution)/shard_map/key_message/pallas_call | solution.py:408
  2.4 6.6 %collective-permute-start = (bf16[528,256]{1,0:T(8,128)(2,1)}, bf16[528,256]{1,0:T(8,128)(2,1)S(1)}, u32[]{:S(2)}, u32[]{:S(2)}) collective-permute-start(bf16[528,256]{1,0:T(8,128)(2,1)} %key_message.1.own), channel_id=1, source_target_pairs={{0,128},{8,136},{16,144},{24,152},{32,160},{40,168},{48,176},{56,1... | collective-permute-start | bytes 811016 | tf_op jit(solution)/shard_map/ppermute | solution.py:37
  9.1 6.8 %collective-permute-start.1 = (bf16[528,256]{1,0:T(8,128)(2,1)}, bf16[528,256]{1,0:T(8,128)(2,1)S(1)}, u32[]{:S(2)}, u32[]{:S(2)}) collective-permute-start(bf16[528,256]{1,0:T(8,128)(2,1)} %key_message.1.own), channel_id=1, source_target_pairs={{0,384},{8,392},{16,400},{24,408},{32,416},{40,424},{48,432},{56,4... | collective-permute-start | bytes 811016 | tf_op jit(solution)/shard_map/ppermute | solution.py:37
  15.9 3.1 %collective-permute-start.2 = (bf16[528,256]{1,0:T(8,128)(2,1)}, bf16[528,256]{1,0:T(8,128)(2,1)S(1)}, u32[]{:S(2)}, u32[]{:S(2)}) collective-permute-start(bf16[528,256]{1,0:T(8,128)(2,1)} %key_message.1.own), channel_id=1, source_target_pairs={{0,64},{8,72},{16,80},{24,88},{32,96},{40,104},{48,112},{56,120},{... | collective-permute-start | bytes 811016 | tf_op jit(solution)/shard_map/ppermute | solution.py:37
  19.0 3.4 %collective-permute-start.3 = (bf16[528,256]{1,0:T(8,128)(2,1)}, bf16[528,256]{1,0:T(8,128)(2,1)S(1)}, u32[]{:S(2)}, u32[]{:S(2)}) collective-permute-start(bf16[528,256]{1,0:T(8,128)(2,1)} %key_message.1.own), channel_id=1, source_target_pairs={{0,448},{8,456},{16,464},{24,472},{32,480},{40,488},{48,496},{56,5... | collective-permute-start | bytes 811016 | tf_op jit(solution)/shard_map/ppermute | solution.py:37
  22.4 2.1 %query_message.1 = bf16[8,256,256]{2,1,0:T(8,128)(2,1)} custom-call(bf16[256,256]{1,0:T(8,128)(2,1)} %q_in), custom_call_target="tpu_custom_call" | custom-call | tf_op jit(solution)/shard_map/query_message/pallas_call | solution.py:418
  24.5 5.8 %all-to-all-start = ((bf16[8,256,256]{2,1,0:T(8,128)(2,1)}), bf16[8,256,256]{2,1,0:T(8,128)(2,1)S(1)}, u32[]{:S(2)}, u32[]{:S(2)}) async-start(bf16[8,256,256]{2,1,0:T(8,128)(2,1)} %query_message.1), calls=%async_computation | async-start | bytes 2097152 | tf_op jit(solution)/shard_map/all_to_all | solution.py:448
  31.0 0.6 pad_add_fusion.where_ref
  31.6 2.7 %lists.1 = (s32[16,128]{1,0:T(8,128)}, bf16[8,64,384]{2,1,0:T(8,128)(2,1)}) custom-call(s32[3]{0:T(128)} %pad_add_fusion.where_ref, s32[29,128]{1,0:T(8,128)} %bitcast.19, s32[1,128]{1,0:T(1,128)} %bitcast.21, s32[5,64]{1,0:T(8,128)} %bitcast.20, bf16[256,3072]{1,0:T(8,128)(2,1)} %w_in.1), custom_call_target="tpu_custom_call" | custom-call | flops 40000000000 | bytes 100000 | tf_op jit(solution)/shard_map/lists/pallas_call | solution.py:427
  34.3 0.0 copy-start.1
  34.4 2.1 %collective-permute-start.4 = (bf16[528,256]{1,0:T(8,128)(2,1)S(1)}, bf16[528,256]{1,0:T(8,128)(2,1)S(1)}, u32[]{:S(2)}, u32[]{:S(2)}) collective-permute-start(bf16[528,256]{1,0:T(8,128)(2,1)S(1)} %collective-permute-done.f2), channel_id=1, source_target_pairs={{0,64},{8,72},{16,80},{24,88},{32,96},{40,104},{48,112},{56,120},{... | collective-permute-start | bytes 811016 | tf_op jit(solution)/shard_map/ppermute | solution.py:37
  36.4 4.6 %collective-permute-start.5 = (bf16[528,256]{1,0:T(8,128)(2,1)S(1)}, bf16[528,256]{1,0:T(8,128)(2,1)S(1)}, u32[]{:S(2)}, u32[]{:S(2)}) collective-permute-start(bf16[528,256]{1,0:T(8,128)(2,1)S(1)} %collective-permute-done.1.b2), channel_id=1, source_target_pairs={{0,448},{8,456},{16,464},{24,472},{32,480},{40,488},{48,496},{56,5... | collective-permute-start | bytes 811016 | tf_op jit(solution)/shard_map/ppermute | solution.py:37
  41.1 2.1 %collective-permute-start.6 = (bf16[528,256]{1,0:T(8,128)(2,1)S(1)}, bf16[528,256]{1,0:T(8,128)(2,1)S(1)}, u32[]{:S(2)}, u32[]{:S(2)}) collective-permute-start(bf16[528,256]{1,0:T(8,128)(2,1)S(1)} %broadcast_select_fusion), channel_id=1, source_target_pairs={{0,128},{8,392},{16,144},{24,408},{32,160},{40,424},{48,176},{56,4... | collective-permute-start | bytes 811016 | tf_op jit(solution)/shard_map/ppermute | solution.py:454
  43.2 2.2 %all-to-all-done.q_in = bf16[8,256,256]{2,1,0:T(8,128)(2,1)S(1)} async-done(((bf16[8,256,256]{2,1,0:T(8,128)(2,1)}), bf16[8,256,256]{2,1,0:T(8,128)(2,1)S(1)}, u32[]{:S(2)}, u32[]{:S(2)}) %all-to-all-start) | async-done | bytes 1048608 | tf_op jit(solution)/shard_map/all_to_all | solution.py:448
  45.4 6.8 %all-to-all-start.1 = ((bf16[8,64,384]{2,1,0:T(8,128)(2,1)}), bf16[8,64,384]{2,1,0:T(8,128)(2,1)}, u32[]{:S(2)}, u32[]{:S(2)}) async-start(bf16[8,64,384]{2,1,0:T(8,128)(2,1)} %get-tuple-element.32), calls=%async_computation.1 | async-start | bytes 786432 | tf_op jit(solution)/shard_map/all_to_all | solution.py:460
  52.3 6.9 %attend_early.1 = (f32[8,256,256]{2,1,0:T(8,128)S(1)}, f32[8,8,256]{2,1,0:T(8,128)S(1)}) custom-call(s32[16,128]{1,0:T(8,128)S(1)} %copy-done.1, bf16[8,256,256]{2,1,0:T(8,128)(2,1)S(1)} %all-to-all-done.q_in, bf16[528,256]{1,0:T(8,128)(2,1)S(1)} %copy-done, bf16[528,256]{1,0:T(8,128)(2,1)S(1)} %collective-permute-done.2.f1, ...), custom_call_target="tpu_custom_call" | custom-call | flops 6000000000 | bytes 5000000 | tf_op jit(solution)/shard_map/attend_early/pallas_call | solution.py:462
  59.3 4.9 %attend_late.1 = (bf16[8,272,256]{2,1,0:T(8,128)(2,1)}, f32[8,256,256]{2,1,0:T(8,128)S(1)}, f32[8,8,256]{2,1,0:T(8,128)S(1)}) custom-call(s32[16,128]{1,0:T(8,128)S(1)} %copy-done.1, bf16[8,256,256]{2,1,0:T(8,128)(2,1)S(1)} %all-to-all-done.q_in, bf16[528,256]{1,0:T(8,128)(2,1)S(1)} %copy-done, ...), custom_call_target="tpu_custom_call", output_to_operand_aliasing={{1}: (10, {}), {2}: (11, {})} | custom-call | flops 4000000000 | bytes 5000000 | tf_op jit(solution)/shard_map/attend_late/pallas_call | solution.py:475
  64.2 1.7 %all-to-all-done.1 = bf16[8,64,384]{2,1,0:T(8,128)(2,1)} async-done(((bf16[8,64,384]{2,1,0:T(8,128)(2,1)}), bf16[8,64,384]{2,1,0:T(8,128)(2,1)}, u32[]{:S(2)}, u32[]{:S(2)}) %all-to-all-start.1) | async-done | bytes 393248 | tf_op jit(solution)/shard_map/all_to_all | solution.py:460
  65.9 5.6 %all-to-all-start.2 = ((bf16[8,272,256]{2,1,0:T(8,128)(2,1)}), bf16[8,272,256]{2,1,0:T(8,128)(2,1)S(1)}, u32[]{:S(2)}, u32[]{:S(2)}) async-start(bf16[8,272,256]{2,1,0:T(8,128)(2,1)} %get-tuple-element.33), calls=%async_computation.2 | async-start | bytes 2228224 | tf_op jit(solution)/shard_map/all_to_all | solution.py:491
  71.5 1.9 %collective-permute-start.7 = (bf16[8,64,384]{2,1,0:T(8,128)(2,1)}, bf16[8,64,384]{2,1,0:T(8,128)(2,1)S(1)}, u32[]{:S(2)}, u32[]{:S(2)}) collective-permute-start(bf16[8,64,384]{2,1,0:T(8,128)(2,1)} %all-to-all-done.1), channel_id=1, source_target_pairs={{0,64},{8,72},{16,80},{24,88},{32,96},{40,104},{48,112},{56,120},{... | collective-permute-start | bytes 1179656 | tf_op jit(solution)/shard_map/ppermute | solution.py:493
  73.4 13.9 %all-to-all-done.2.part_ref = bf16[8,272,256]{2,1,0:T(8,128)(2,1)S(1)} async-done(((bf16[8,272,256]{2,1,0:T(8,128)(2,1)}), bf16[8,272,256]{2,1,0:T(8,128)(2,1)S(1)}, u32[]{:S(2)}, u32[]{:S(2)}) %all-to-all-start.2) | async-done | bytes 1114144 | tf_op jit(solution)/shard_map/all_to_all | solution.py:491
  87.3 1.3 %merge.1 = bf16[8,256,256]{2,1,0:T(8,128)(2,1)} custom-call(bf16[8,272,256]{2,1,0:T(8,128)(2,1)S(1)} %all-to-all-done.2.part_ref), custom_call_target="tpu_custom_call" | custom-call | tf_op jit(solution)/shard_map/merge/pallas_call | solution.py:498
  88.5 4.8 %all-to-all-start.3 = ((bf16[8,256,256]{2,1,0:T(8,128)(2,1)}), bf16[8,256,256]{2,1,0:T(8,128)(2,1)S(1)}, u32[]{:S(2)}, u32[]{:S(2)}) async-start(bf16[8,256,256]{2,1,0:T(8,128)(2,1)} %merge.1), calls=%async_computation.3 | async-start | bytes 2097152 | tf_op jit(solution)/shard_map/all_to_all | solution.py:506
  93.3 1.1 select_bitcast_fusion.3
  94.4 0.1 pad_maximum_fusion.1
  94.5 3.1 %collective-permute-start.8 = (bf16[8,2,64,384]{3,2,0,1:T(8,128)(2,1)S(1)}, bf16[8,2,64,384]{3,2,0,1:T(8,128)(2,1)}, u32[]{:S(2)}, u32[]{:S(2)}) collective-permute-start(bf16[8,2,64,384]{3,2,0,1:T(8,128)(2,1)S(1)} %pad_maximum_fusion.1), channel_id=1, source_target_pairs={{0,8},{8,0},{16,24},{24,16},{32,40},{40,32},{48,56},{56,48},{64,72... | collective-permute-start | bytes 2359304 | tf_op jit(solution)/shard_map/ppermute | solution.py:495
  97.6 2.0 %collective-permute-done.8 = bf16[8,2,64,384]{3,2,0,1:T(8,128)(2,1)} collective-permute-done((bf16[8,2,64,384]{3,2,0,1:T(8,128)(2,1)S(1)}, bf16[8,2,64,384]{3,2,0,1:T(8,128)(2,1)}, u32[]{:S(2)}, u32[]{:S(2)}) %collective-permute-start.8) | collective-permute-done | bytes 786464 | tf_op jit(solution)/shard_map/ppermute | solution.py:495
  99.6 1.3 %select_bitcast_fusion.1 = (bf16[8,2,1,64,384]{4,3,0,1,2:T(8,128)(2,1)S(1)}, bf16[8,2,1,64,384]{4,3,0,1,2:T(8,128)(2,1)S(1)}) fusion(bf16[8,2,64,384]{3,2,0,1:T(8,128)(2,1)} %collective-permute-done.8, pred[]{:T(512)S(6)} %eq.13, bf16[8,1,64,384]{3,2,0,1:T(8,128)(2,1)S(1)} %get-tuple-element.38, bf16[8,1,64,384]{3,2,0,1:T(8,128)(2,1)S(1)} %get-tuple-element.37), kind=kLoop, calls=%fused_computation.4 | loop fusion | flops 1179648 | bytes 3145729 | tf_op jit(solution)/shard_map/stack | solution.py:497
  100.9 0.2 pad_maximum_fusion
  101.1 0.2 copy.13
  101.3 21.2 %all-to-all-done.3 = bf16[8,256,256]{2,1,0:T(8,128)(2,1)S(1)} async-done(((bf16[8,256,256]{2,1,0:T(8,128)(2,1)}), bf16[8,256,256]{2,1,0:T(8,128)(2,1)S(1)}, u32[]{:S(2)}, u32[]{:S(2)}) %all-to-all-start.3) | async-done | bytes 1048608 | tf_op jit(solution)/shard_map/all_to_all | solution.py:506
  122.5 1.4 %convolution_convert_fusion = bf16[256,384]{1,0:T(8,128)(2,1)} fusion(bf16[2048,256]{1,0:T(8,128)(2,1)S(1)} %bitcast.18, bf16[2048,384]{1,0:T(8,128)(2,1)S(1)} %bitcast.17), kind=kOutput, calls=%fused_computation.1 | convolution fusion | flops 402751488 | bytes 2818048 | tf_op jit(solution)/shard_map/dot_general | solution.py:507
  (12 shorter events, 0.1 us)
Async XLA Ops:
  2.4 31.9 %collective-permute-start = (bf16[528,256]{1,0:T(8,128)(2,1)}, bf16[528,256]{1,0:T(8,128)(2,1)S(1)}, u32[]{:S(2)}, u32[]{:S(2)}) collective-permute-start(bf16[528,256]{1,0:T(8,128)(2,1)} %key_message.1.own), channel_id=1, source_target_pairs={{0,128},{8,136},{16,144},{24,152},{32,160},{40,168},{48,176},{56,1... | collective-permute-start | bytes 811016 | tf_op jit(solution)/shard_map/ppermute | solution.py:37
  9.1 25.3 %collective-permute-start.1 = (bf16[528,256]{1,0:T(8,128)(2,1)}, bf16[528,256]{1,0:T(8,128)(2,1)S(1)}, u32[]{:S(2)}, u32[]{:S(2)}) collective-permute-start(bf16[528,256]{1,0:T(8,128)(2,1)} %key_message.1.own), channel_id=1, source_target_pairs={{0,384},{8,392},{16,400},{24,408},{32,416},{40,424},{48,432},{56,4... | collective-permute-start | bytes 811016 | tf_op jit(solution)/shard_map/ppermute | solution.py:37
  15.9 36.4 %collective-permute-start.2 = (bf16[528,256]{1,0:T(8,128)(2,1)}, bf16[528,256]{1,0:T(8,128)(2,1)S(1)}, u32[]{:S(2)}, u32[]{:S(2)}) collective-permute-start(bf16[528,256]{1,0:T(8,128)(2,1)} %key_message.1.own), channel_id=1, source_target_pairs={{0,64},{8,72},{16,80},{24,88},{32,96},{40,104},{48,112},{56,120},{... | collective-permute-start | bytes 811016 | tf_op jit(solution)/shard_map/ppermute | solution.py:37
  19.0 33.3 %collective-permute-start.3 = (bf16[528,256]{1,0:T(8,128)(2,1)}, bf16[528,256]{1,0:T(8,128)(2,1)S(1)}, u32[]{:S(2)}, u32[]{:S(2)}) collective-permute-start(bf16[528,256]{1,0:T(8,128)(2,1)} %key_message.1.own), channel_id=1, source_target_pairs={{0,448},{8,456},{16,464},{24,472},{32,480},{40,488},{48,496},{56,5... | collective-permute-start | bytes 811016 | tf_op jit(solution)/shard_map/ppermute | solution.py:37
  24.5 20.9 %all-to-all-start = ((bf16[8,256,256]{2,1,0:T(8,128)(2,1)}), bf16[8,256,256]{2,1,0:T(8,128)(2,1)S(1)}, u32[]{:S(2)}, u32[]{:S(2)}) async-start(bf16[8,256,256]{2,1,0:T(8,128)(2,1)} %query_message.1), calls=%async_computation | async-start | bytes 2097152 | tf_op jit(solution)/shard_map/all_to_all | solution.py:448
  34.3 18.0 %copy-start = (bf16[528,256]{1,0:T(8,128)(2,1)S(1)}, bf16[528,256]{1,0:T(8,128)(2,1)}, u32[]{:S(2)}) copy-start(bf16[528,256]{1,0:T(8,128)(2,1)} %key_message.1.own) | copy-start | bytes 811012
  34.3 18.0 %copy-start.1 = (s32[16,128]{1,0:T(8,128)S(1)}, s32[16,128]{1,0:T(8,128)}, u32[]{:S(2)}) copy-start(s32[16,128]{1,0:T(8,128)} %get-tuple-element.23.table) | copy-start | bytes 24580
  34.4 24.9 %collective-permute-start.4 = (bf16[528,256]{1,0:T(8,128)(2,1)S(1)}, bf16[528,256]{1,0:T(8,128)(2,1)S(1)}, u32[]{:S(2)}, u32[]{:S(2)}) collective-permute-start(bf16[528,256]{1,0:T(8,128)(2,1)S(1)} %collective-permute-done.f2), channel_id=1, source_target_pairs={{0,64},{8,72},{16,80},{24,88},{32,96},{40,104},{48,112},{56,120},{... | collective-permute-start | bytes 811016 | tf_op jit(solution)/shard_map/ppermute | solution.py:37
  36.4 22.8 %collective-permute-start.5 = (bf16[528,256]{1,0:T(8,128)(2,1)S(1)}, bf16[528,256]{1,0:T(8,128)(2,1)S(1)}, u32[]{:S(2)}, u32[]{:S(2)}) collective-permute-start(bf16[528,256]{1,0:T(8,128)(2,1)S(1)} %collective-permute-done.1.b2), channel_id=1, source_target_pairs={{0,448},{8,456},{16,464},{24,472},{32,480},{40,488},{48,496},{56,5... | collective-permute-start | bytes 811016 | tf_op jit(solution)/shard_map/ppermute | solution.py:37
  41.1 18.2 %collective-permute-start.6 = (bf16[528,256]{1,0:T(8,128)(2,1)S(1)}, bf16[528,256]{1,0:T(8,128)(2,1)S(1)}, u32[]{:S(2)}, u32[]{:S(2)}) collective-permute-start(bf16[528,256]{1,0:T(8,128)(2,1)S(1)} %broadcast_select_fusion), channel_id=1, source_target_pairs={{0,128},{8,392},{16,144},{24,408},{32,160},{40,424},{48,176},{56,4... | collective-permute-start | bytes 811016 | tf_op jit(solution)/shard_map/ppermute | solution.py:454
  45.4 20.5 %all-to-all-start.1 = ((bf16[8,64,384]{2,1,0:T(8,128)(2,1)}), bf16[8,64,384]{2,1,0:T(8,128)(2,1)}, u32[]{:S(2)}, u32[]{:S(2)}) async-start(bf16[8,64,384]{2,1,0:T(8,128)(2,1)} %get-tuple-element.32), calls=%async_computation.1 | async-start | bytes 786432 | tf_op jit(solution)/shard_map/all_to_all | solution.py:460
  65.9 21.4 %all-to-all-start.2 = ((bf16[8,272,256]{2,1,0:T(8,128)(2,1)}), bf16[8,272,256]{2,1,0:T(8,128)(2,1)S(1)}, u32[]{:S(2)}, u32[]{:S(2)}) async-start(bf16[8,272,256]{2,1,0:T(8,128)(2,1)} %get-tuple-element.33), calls=%async_computation.2 | async-start | bytes 2228224 | tf_op jit(solution)/shard_map/all_to_all | solution.py:491
  71.5 21.8 %collective-permute-start.7 = (bf16[8,64,384]{2,1,0:T(8,128)(2,1)}, bf16[8,64,384]{2,1,0:T(8,128)(2,1)S(1)}, u32[]{:S(2)}, u32[]{:S(2)}) collective-permute-start(bf16[8,64,384]{2,1,0:T(8,128)(2,1)} %all-to-all-done.1), channel_id=1, source_target_pairs={{0,64},{8,72},{16,80},{24,88},{32,96},{40,104},{48,112},{56,120},{... | collective-permute-start | bytes 1179656 | tf_op jit(solution)/shard_map/ppermute | solution.py:493
  88.5 34.0 %all-to-all-start.3 = ((bf16[8,256,256]{2,1,0:T(8,128)(2,1)}), bf16[8,256,256]{2,1,0:T(8,128)(2,1)S(1)}, u32[]{:S(2)}, u32[]{:S(2)}) async-start(bf16[8,256,256]{2,1,0:T(8,128)(2,1)} %merge.1), calls=%async_computation.3 | async-start | bytes 2097152 | tf_op jit(solution)/shard_map/all_to_all | solution.py:506
  94.5 5.1 %collective-permute-start.8 = (bf16[8,2,64,384]{3,2,0,1:T(8,128)(2,1)S(1)}, bf16[8,2,64,384]{3,2,0,1:T(8,128)(2,1)}, u32[]{:S(2)}, u32[]{:S(2)}) collective-permute-start(bf16[8,2,64,384]{3,2,0,1:T(8,128)(2,1)S(1)} %pad_maximum_fusion.1), channel_id=1, source_target_pairs={{0,8},{8,0},{16,24},{24,16},{32,40},{40,32},{48,56},{56,48},{64,72... | collective-permute-start | bytes 2359304 | tf_op jit(solution)/shard_map/ppermute | solution.py:495

commit v4 on v3

--- a/solution.py
+++ b/solution.py
@@ -17,9 +17,9 @@
 SCORE_SCALE = HD ** (-0.5) * 1.4426950408889634
 EARLY = (0, -1, 1, -2, 2)
 LATE = (-3, 3, 4)
-TOGETHER = 4
+TOGETHER = 8
 TEXT_ROWS = 8
-GROUPS_AT_ONCE = 4
+GROUPS_AT_ONCE = 8
 MESSAGE = 4 * BLK + TPAD
 NEAR_AT = ROW
 COUNT_AT = 32
@@ -44,10 +44,11 @@
             yield a, h, tile.T.astype(jnp.bfloat16)
 
 
-def key_kernel(k_in, v_in, tk_in, tv_in, kv_out, v_buf, sems):
+def message_kernel(k_in, v_in, q_in, tk_in, tv_in, kv_out, q_out, v_buf, q_buf, sems):
     copies = [
         pltpu.make_async_copy(v_in, v_buf, sems.at[0]),
-        pltpu.make_async_copy(k_in, kv_out.at[: 2 * BLK], sems.at[1]),
+        pltpu.make_async_copy(q_in, q_buf, sems.at[1]),
+        pltpu.make_async_copy(k_in, kv_out.at[: 2 * BLK], sems.at[2]),
     ]
     for copy in copies:
         copy.start()
@@ -58,15 +59,10 @@
     for a, h, tile in turned(v_buf):
         kv_out[(2 + a) * BLK : (3 + a) * BLK, h * HD : (h + 1) * HD] = tile
     copies[1].wait()
-
-
-def query_kernel(q_in, q_out, q_buf, sems):
-    copy = pltpu.make_async_copy(q_in, q_buf, sems.at[0])
-    copy.start()
-    copy.wait()
     for a, h, tile in turned(q_buf):
         for i in range(ROW):
             q_out[i, a * BLK : (a + 1) * BLK, h * HD : (h + 1) * HD] = tile
+    copies[2].wait()
 
 
 def list_kernel(where_ref, far_ref, count_ref, width_ref, w_in, table_ref, w_out, wide, tall, sems):
@@ -153,10 +149,11 @@
         keys.append(tile)
         vals.append(pltpu.roll(tile, 4, 0))
     text_k[...] = jnp.concatenate(keys, axis=0).astype(jnp.bfloat16)
-    vals.append(jnp.zeros((HD - ROW * TEXT_ROWS, 2 * HD), jnp.float32))
+    spare = HD - ROW * TEXT_ROWS
+    vals.append(jnp.zeros((spare, 2 * HD), jnp.float32))
     vals = jnp.concatenate(vals, axis=0)
     for h in range(2):
-        text_v[h] = vals[:, h * HD : (h + 1) * HD].T.astype(jnp.bfloat16)
+        text_v[h] = vals[:, h * HD : (h + 1) * HD].T.astype(jnp.bfloat16)[:, : HD - spare]
 
 
 def group_queries(q_ref, g, h):
@@ -173,18 +170,13 @@
 
 
 def text_step(q_ref, cases, text_k, text_v, bias):
-    spare = HD - text_k.shape[0]
     scores = [
         product(text_k[:, head_rows(h)], group_queries(q_ref, g, h)) * SCORE_SCALE + bias[...] for g, h in cases
     ]
     tops = [jnp.maximum(jnp.max(s, axis=0, keepdims=True), FLOOR) for s in scores]
     weights = [jnp.exp2(s - top) for s, top in zip(scores, tops)]
     totals = [jnp.sum(p, axis=0, keepdims=True) for p in weights]
-    filler = jnp.zeros((spare, 2 * BLK), jnp.bfloat16)
-    outs = [
-        product(text_v[h], jnp.concatenate((p.astype(jnp.bfloat16), filler), axis=0))
-        for (_, h), p in zip(cases, weights)
-    ]
+    outs = [product(text_v[h], p.astype(jnp.bfloat16)) for (_, h), p in zip(cases, weights)]
     return list(zip(tops, totals, outs))
 
 
@@ -256,8 +248,8 @@
     return [copy.wait for copy in copies]
 
 
-def early_kernel(table, q_in, own, f1, b1, f2, b2, acc, stat, q_ref, kv, units, sems):
-    waits = start_all([(x, kv.at[i]) for i, x in enumerate((own, f1, b1, f2, b2))] + [(q_in, q_ref)], sems)
+def early_kernel(table, q_ref, own, f1, b1, f2, b2, acc, stat, kv, units, sems):
+    waits = start_all([(x, kv.at[i]) for i, x in enumerate((own, f1, b1, f2, b2))], sems)
     count = list_units(table, 0, len(EARLY), units)
     for wait in waits:
         wait()
@@ -266,46 +258,41 @@
     )
     distance = jnp.abs(offset)
 
-    def one_group(g, _):
-        near = table[g, NEAR_AT]
-
-        @pl.when(near > 0)
-        def _():
+    r = table[0, WHERE_AT + 1]
+    for steps in ((0, 1), (2, 3), (4,)):
+        cases = []
+        for step in steps:
+            g = (r + NEAR - step) & (ROW - 1)
+            near = table[g, NEAR_AT]
             who = near & 15
-            scores = []
             for h in range(2):
                 s = product(kv[who, : 2 * BLK, head_rows(h)], group_queries(q_ref, g, h)) * SCORE_SCALE
-                scores.append(jnp.where(distance < (near >> 4), s, NEG))
-            fresh = []
-            for h, s in enumerate(scores):
-                top = jnp.maximum(jnp.max(s, axis=0, keepdims=True), FLOOR)
-                p = jnp.exp2(s - top)
-                values = jnp.concatenate(
-                    (kv[who, 2 * BLK : 3 * BLK, head_rows(h)], kv[who, 3 * BLK : 4 * BLK, head_rows(h)]),
-                    axis=1,
-                )
-                fresh.append((top, jnp.sum(p, axis=0, keepdims=True), product(values, p.astype(jnp.bfloat16))))
-            for h, new in enumerate(fresh):
-                write_state(acc, stat, g, h, new)
+                cases.append((g, h, who, jnp.where(distance < (near >> 4), s, NEG)))
+        fresh = []
+        for g, h, who, s in cases:
+            top = jnp.maximum(jnp.max(s, axis=0, keepdims=True), FLOOR)
+            p = jnp.exp2(s - top)
+            values = jnp.concatenate(
+                (kv[who, 2 * BLK : 3 * BLK, head_rows(h)], kv[who, 3 * BLK : 4 * BLK, head_rows(h)]), axis=1
+            )
+            out = product(values, p.astype(jnp.bfloat16))
+            fresh.append((g, h, (top, jnp.sum(p, axis=0, keepdims=True), out)))
+        for g, h, state in fresh:
+            write_state(acc, stat, g, h, state)
             stat[g, 4:8, :] = jnp.zeros((4, 2 * BLK), jnp.float32)
-
-        @pl.when(near == 0)
-        def _():
-            acc[g, :, :] = jnp.zeros((2 * HD, 2 * BLK), jnp.float32)
-            row = lax.broadcasted_iota(jnp.int32, (8, 2 * BLK), 0)
-            stat[g, :, :] = jnp.where((row == 0) | (row == 2), FLOOR, 0.0)
-
-        return 0
-
-    lax.fori_loop(0, ROW, one_group, 0)
+    row = lax.broadcasted_iota(jnp.int32, (8, 2 * BLK), 0)
+    for step in range(2 * NEAR + 1, ROW):
+        g = (r + NEAR - step) & (ROW - 1)
+        acc[g, :, :] = jnp.zeros((2 * HD, 2 * BLK), jnp.float32)
+        stat[g, :, :] = jnp.where((row == 0) | (row == 2), FLOOR, 0.0)
     walk_units(units, count, q_ref, kv, acc, stat)
 
 
 def late_kernel(
-    table, q_in, own, f1, b1, f2, b2, f3, b3, far4, acc_in, stat_in, out_ref, acc, stat,
-    q_ref, kv, units, sems, tiles, bias, text_k, text_v,
+    table, q_ref, own, f1, b1, f2, b2, f3, b3, far4, acc_in, stat_in, out_ref, acc, stat,
+    kv, units, sems, tiles, bias, text_k, text_v,
 ):
-    pairs = [(f3, kv.at[0]), (b3, kv.at[1]), (far4, kv.at[2]), (q_in, q_ref)]
+    pairs = [(f3, kv.at[0]), (b3, kv.at[1]), (far4, kv.at[2])]
     for i, x in enumerate((own, f1, b1, f2, b2, f3, b3, far4)):
         pairs.append((x.at[4 * BLK :], tiles.at[i]))
     waits = start_all(pairs, sems)
@@ -370,7 +357,6 @@
 
 def attend_scratch(slots, copies):
     return [
-        pltpu.VMEM((ROW, 2 * BLK, 2 * HD), jnp.bfloat16),
         pltpu.VMEM((slots, MESSAGE, 2 * HD), jnp.bfloat16),
         pltpu.SMEM((2 * ROW * slots + 8,), jnp.int32),
         pltpu.SemaphoreType.DMA((copies,)),
@@ -382,7 +368,7 @@
         pltpu.VMEM((ROW, TPAD, 2 * HD), jnp.bfloat16),
         pltpu.VMEM((ROW * TEXT_ROWS, 2 * BLK), jnp.float32),
         pltpu.VMEM((ROW * TEXT_ROWS, 2 * HD), jnp.bfloat16),
-        pltpu.VMEM((2, HD, HD), jnp.bfloat16),
+        pltpu.VMEM((2, HD, ROW * TEXT_ROWS), jnp.bfloat16),
     ]
 
 
@@ -405,25 +391,22 @@
     columns = w_out.shape[1] // heads
 
     whole = pltpu.CompilerParams(vmem_limit_bytes=60 << 20)
-    kv = pl.pallas_call(
-        key_kernel,
-        out_shape=jax.ShapeDtypeStruct((MESSAGE, width), jnp.bfloat16),
-        in_specs=[anywhere(), anywhere(), vmem(), vmem()],
-        out_specs=vmem(),
-        scratch_shapes=[pltpu.VMEM((tokens, width), jnp.bfloat16), pltpu.SemaphoreType.DMA((2,))],
+    kv, q_mine = pl.pallas_call(
+        message_kernel,
+        out_shape=(
+            jax.ShapeDtypeStruct((MESSAGE, width), jnp.bfloat16),
+            jax.ShapeDtypeStruct((ROW, tokens, width), jnp.bfloat16),
+        ),
+        in_specs=[anywhere()] * 3 + [vmem()] * 2,
+        out_specs=(vmem(), vmem()),
+        scratch_shapes=[
+            pltpu.VMEM((tokens, width), jnp.bfloat16),
+            pltpu.VMEM((tokens, width), jnp.bfloat16),
+            pltpu.SemaphoreType.DMA((3,)),
+        ],
         compiler_params=whole,
-        name="key_message",
-    )(keys, values, text_keys, text_values)
-    kv, queries = lax.optimization_barrier((kv, queries))
-    q_mine = pl.pallas_call(
-        query_kernel,
-        out_shape=jax.ShapeDtypeStruct((ROW, tokens, width), jnp.bfloat16),
-        in_specs=[anywhere()],
-        out_specs=vmem(),
-        scratch_shapes=[pltpu.VMEM((tokens, width), jnp.bfloat16), pltpu.SemaphoreType.DMA((1,))],
-        compiler_params=whole,
-        name="query_message",
-    )(queries)
+        name="messages",
+    )(keys, values, queries, text_keys, text_values)
     table, quarter = pl.pallas_call(
         list_kernel,
         out_shape=(
@@ -465,9 +448,9 @@
             jax.ShapeDtypeStruct((ROW, width, tokens), jnp.float32),
             jax.ShapeDtypeStruct((ROW, 8, tokens), jnp.float32),
         ),
-        in_specs=[smem()] + [anywhere()] * 6,
+        in_specs=[smem(), vmem()] + [anywhere()] * 5,
         out_specs=(vmem(), vmem()),
-        scratch_shapes=attend_scratch(len(EARLY), 6),
+        scratch_shapes=attend_scratch(len(EARLY), 5),
         compiler_params=kernel_params(),
         cost_estimate=pl.CostEstimate(flops=6 * 10**9, bytes_accessed=5 * 10**6, transcendentals=0),
         name="attend_early",
@@ -479,9 +462,9 @@
             jax.ShapeDtypeStruct(acc.shape, acc.dtype),
             jax.ShapeDtypeStruct(stat.shape, stat.dtype),
         ),
-        in_specs=[smem()] + [anywhere()] * 9 + [vmem()] * 2,
+        in_specs=[smem(), vmem()] + [anywhere()] * 8 + [vmem()] * 2,
         out_specs=(vmem(),) * 3,
-        scratch_shapes=attend_scratch(len(LATE), 4 + ROW) + text_scratch(),
+        scratch_shapes=attend_scratch(len(LATE), 3 + ROW) + text_scratch(),
         input_output_aliases={10: 1, 11: 2},
         compiler_params=kernel_params(),
         cost_estimate=pl.CostEstimate(flops=4 * 10**9, bytes_accessed=5 * 10**6, transcendentals=0),

time: 125 us -> 120 us (0.960)
  Pallas kernels: 20.4 us -> 15.8 us
  waiting for transfers between devices: 41.1 us -> 43.3 us
  starting transfers between devices: 56.6 us -> 55.1 us
    all_to_all x1, waiting for transfers between devices: 1.69 us -> 4.78 us  [shards(): quarter = lax.all_to_all(quarter, 'head', 0, 0)]
    pallas_call x1, Pallas kernels: 6.95 us -> 4.07 us  [shards(): pl.pallas_call(early_kernel, out_shape=(jax.ShapeDtypeStruct((ROW, width,...]
    pallas_call x2 -> x1, Pallas kernels: 4.57 us -> 3.06 us  [shards(): pl.pallas_call(message_kernel, out_shape=(jax.ShapeDtypeStruct((MESSAGE,...]
  transfers between devices with their start and end apart: 13 -> 13, of which waited for: 5 -> 5; matrix products, arithmetic and copies ran while one was open for 3% -> 2% of each run, Pallas kernels for 15% -> 11%
where the time goes in v4:
time: 120 us; the launch traced here: 119 us
  starting transfers between devices  55.1 us (46%)
  waiting for transfers between devices  43.3 us (36%)
  Pallas kernels  15.8 us (13%)
  other arithmetic  2.22 us (2%)
  matrix products  1.42 us (1%)
    ppermute x6, starting transfers between devices, along_column(): lax.ppermute(block, 'seq', [(g, (g + ROW * distance) % count) for g in ra...  26.5 us
    all_to_all x1, waiting for transfers between devices, shards(): attention = lax.all_to_all(merged, 'head', 0, 0)  20.6 us
    all_to_all x1, waiting for transfers between devices, shards(): part = lax.all_to_all(part, 'seq', 0, 0, axis_index_groups=row_peers())  13.9 us
    all_to_all x1, starting transfers between devices, shards(): quarter = lax.all_to_all(quarter, 'head', 0, 0)  6.82 us
    all_to_all x1, starting transfers between devices, shards(): q_all = lax.all_to_all(q_mine, 'seq', 0, 0, axis_index_groups=row_peers())  5.82 us
    all_to_all x1, starting transfers between devices, shards(): part = lax.all_to_all(part, 'seq', 0, 0, axis_index_groups=row_peers())  5.57 us
    all_to_all x1, waiting for transfers between devices, shards(): quarter = lax.all_to_all(quarter, 'head', 0, 0)  4.78 us
    pallas_call x1, Pallas kernels, shards(): pl.pallas_call(late_kernel, out_shape=(jax.ShapeDtypeStruct((ROW, width +...  4.7 us
  transfers between devices with their start and end apart: 13, of which 5 were waited for; matrix products, arithmetic and copies ran while one was open for 2% of the time, Pallas kernels for 11%

profile of v4, /device:TPU:1, one launch (start us, length us, event | category | flops | bytes accessed | tf_op | source)
XLA Modules:
  0.0 119.0 jit_solution(2391520426950054830)
XLA Ops:
  0.0 3.1 %messages.1 = (bf16[528,256]{1,0:T(8,128)(2,1)}, bf16[8,256,256]{2,1,0:T(8,128)(2,1)}) custom-call(bf16[256,256]{1,0:T(8,128)(2,1)} %k_in.1, bf16[256,256]{1,0:T(8,128)(2,1)} %v_in.1, bf16[256,256]{1,0:T(8,128)(2,1)} %q_in.1, bf16[4,256]{1,0:T(4,128)(2,1)} %tk_in.1, bf16[4,256]{1,0:T(4,128)(2,1)} %tv_in.1), custom_call_target="tpu_custom_call" | custom-call | tf_op jit(solution)/shard_map/messages/pallas_call | solution.py:394
  3.1 6.6 %collective-permute-start = (bf16[528,256]{1,0:T(8,128)(2,1)}, bf16[528,256]{1,0:T(8,128)(2,1)S(1)}, u32[]{:S(2)}, u32[]{:S(2)}) collective-permute-start(bf16[528,256]{1,0:T(8,128)(2,1)} %get-tuple-element.20.own), channel_id=1, source_target_pairs={{0,128},{8,136},{16,144},{24,152},{32,160},{40,168},{48,176},{56,1... | collective-permute-start | bytes 811016 | tf_op jit(solution)/shard_map/ppermute | solution.py:37
  9.7 6.8 %collective-permute-start.1 = (bf16[528,256]{1,0:T(8,128)(2,1)}, bf16[528,256]{1,0:T(8,128)(2,1)S(1)}, u32[]{:S(2)}, u32[]{:S(2)}) collective-permute-start(bf16[528,256]{1,0:T(8,128)(2,1)} %get-tuple-element.20.own), channel_id=1, source_target_pairs={{0,384},{8,392},{16,400},{24,408},{32,416},{40,424},{48,432},{56,4... | collective-permute-start | bytes 811016 | tf_op jit(solution)/shard_map/ppermute | solution.py:37
  16.5 3.1 %collective-permute-start.2 = (bf16[528,256]{1,0:T(8,128)(2,1)}, bf16[528,256]{1,0:T(8,128)(2,1)S(1)}, u32[]{:S(2)}, u32[]{:S(2)}) collective-permute-start(bf16[528,256]{1,0:T(8,128)(2,1)} %get-tuple-element.20.own), channel_id=1, source_target_pairs={{0,64},{8,72},{16,80},{24,88},{32,96},{40,104},{48,112},{56,120},{... | collective-permute-start | bytes 811016 | tf_op jit(solution)/shard_map/ppermute | solution.py:37
  19.6 3.4 %collective-permute-start.3 = (bf16[528,256]{1,0:T(8,128)(2,1)}, bf16[528,256]{1,0:T(8,128)(2,1)S(1)}, u32[]{:S(2)}, u32[]{:S(2)}) collective-permute-start(bf16[528,256]{1,0:T(8,128)(2,1)} %get-tuple-element.20.own), channel_id=1, source_target_pairs={{0,448},{8,456},{16,464},{24,472},{32,480},{40,488},{48,496},{56,5... | collective-permute-start | bytes 811016 | tf_op jit(solution)/shard_map/ppermute | solution.py:37
  23.0 5.8 %all-to-all-start = ((bf16[8,256,256]{2,1,0:T(8,128)(2,1)}), bf16[8,256,256]{2,1,0:T(8,128)(2,1)S(1)}, u32[]{:S(2)}, u32[]{:S(2)}) async-start(bf16[8,256,256]{2,1,0:T(8,128)(2,1)} %get-tuple-element.25), calls=%async_computation | async-start | bytes 2097152 | tf_op jit(solution)/shard_map/all_to_all | solution.py:431
  29.5 0.7 pad_add_fusion.where_ref
  30.1 2.7 %lists.1 = (s32[16,128]{1,0:T(8,128)}, bf16[8,64,384]{2,1,0:T(8,128)(2,1)}) custom-call(s32[3]{0:T(128)} %pad_add_fusion.where_ref, s32[29,128]{1,0:T(8,128)} %bitcast.19, s32[1,128]{1,0:T(1,128)} %bitcast.21, s32[5,64]{1,0:T(8,128)} %bitcast.20, bf16[256,3072]{1,0:T(8,128)(2,1)} %w_in.1), custom_call_target="tpu_custom_call" | custom-call | flops 40000000000 | bytes 100000 | tf_op jit(solution)/shard_map/lists/pallas_call | solution.py:410
  32.9 0.0 copy-start.1
  32.9 0.0 collective-permute-done.f2
  32.9 2.1 %collective-permute-start.4 = (bf16[528,256]{1,0:T(8,128)(2,1)S(1)}, bf16[528,256]{1,0:T(8,128)(2,1)S(1)}, u32[]{:S(2)}, u32[]{:S(2)}) collective-permute-start(bf16[528,256]{1,0:T(8,128)(2,1)S(1)} %collective-permute-done.f2), channel_id=1, source_target_pairs={{0,64},{8,72},{16,80},{24,88},{32,96},{40,104},{48,112},{56,120},{... | collective-permute-start | bytes 811016 | tf_op jit(solution)/shard_map/ppermute | solution.py:37
  35.0 4.6 %collective-permute-start.5 = (bf16[528,256]{1,0:T(8,128)(2,1)S(1)}, bf16[528,256]{1,0:T(8,128)(2,1)S(1)}, u32[]{:S(2)}, u32[]{:S(2)}) collective-permute-start(bf16[528,256]{1,0:T(8,128)(2,1)S(1)} %collective-permute-done.1.b2), channel_id=1, source_target_pairs={{0,448},{8,456},{16,464},{24,472},{32,480},{40,488},{48,496},{56,5... | collective-permute-start | bytes 811016 | tf_op jit(solution)/shard_map/ppermute | solution.py:37
  39.6 2.1 %collective-permute-start.6 = (bf16[528,256]{1,0:T(8,128)(2,1)S(1)}, bf16[528,256]{1,0:T(8,128)(2,1)S(1)}, u32[]{:S(2)}, u32[]{:S(2)}) collective-permute-start(bf16[528,256]{1,0:T(8,128)(2,1)S(1)} %broadcast_select_fusion), channel_id=1, source_target_pairs={{0,128},{8,392},{16,144},{24,408},{32,160},{40,424},{48,176},{56,4... | collective-permute-start | bytes 811016 | tf_op jit(solution)/shard_map/ppermute | solution.py:437
  41.8 2.2 %all-to-all-done.q_ref = bf16[8,256,256]{2,1,0:T(8,128)(2,1)S(1)} async-done(((bf16[8,256,256]{2,1,0:T(8,128)(2,1)}), bf16[8,256,256]{2,1,0:T(8,128)(2,1)S(1)}, u32[]{:S(2)}, u32[]{:S(2)}) %all-to-all-start) | async-done | bytes 1048608 | tf_op jit(solution)/shard_map/all_to_all | solution.py:431
  43.9 6.8 %all-to-all-start.1 = ((bf16[8,64,384]{2,1,0:T(8,128)(2,1)}), bf16[8,64,384]{2,1,0:T(8,128)(2,1)}, u32[]{:S(2)}, u32[]{:S(2)}) async-start(bf16[8,64,384]{2,1,0:T(8,128)(2,1)} %get-tuple-element.32), calls=%async_computation.1 | async-start | bytes 786432 | tf_op jit(solution)/shard_map/all_to_all | solution.py:443
  50.8 4.1 %attend_early.1 = (f32[8,256,256]{2,1,0:T(8,128)S(1)}, f32[8,8,256]{2,1,0:T(8,128)S(1)}) custom-call(s32[16,128]{1,0:T(8,128)S(1)} %copy-done.1, bf16[8,256,256]{2,1,0:T(8,128)(2,1)S(1)} %all-to-all-done.q_ref, bf16[528,256]{1,0:T(8,128)(2,1)S(1)} %copy-done, bf16[528,256]{1,0:T(8,128)(2,1)S(1)} %collective-permute-done.2.f1, ...), custom_call_target="tpu_custom_call" | custom-call | flops 6000000000 | bytes 5000000 | tf_op jit(solution)/shard_map/attend_early/pallas_call | solution.py:445
  54.9 4.7 %attend_late.1 = (bf16[8,272,256]{2,1,0:T(8,128)(2,1)}, f32[8,256,256]{2,1,0:T(8,128)S(1)}, f32[8,8,256]{2,1,0:T(8,128)S(1)}) custom-call(s32[16,128]{1,0:T(8,128)S(1)} %copy-done.1, bf16[8,256,256]{2,1,0:T(8,128)(2,1)S(1)} %all-to-all-done.q_ref, bf16[528,256]{1,0:T(8,128)(2,1)S(1)} %copy-done, ...), custom_call_target="tpu_custom_call", output_to_operand_aliasing={{1}: (10, {}), {2}: (11, {})} | custom-call | flops 4000000000 | bytes 5000000 | tf_op jit(solution)/shard_map/attend_late/pallas_call | solution.py:458
  59.6 4.8 %all-to-all-done.1 = bf16[8,64,384]{2,1,0:T(8,128)(2,1)} async-done(((bf16[8,64,384]{2,1,0:T(8,128)(2,1)}), bf16[8,64,384]{2,1,0:T(8,128)(2,1)}, u32[]{:S(2)}, u32[]{:S(2)}) %all-to-all-start.1) | async-done | bytes 393248 | tf_op jit(solution)/shard_map/all_to_all | solution.py:443
  64.4 5.6 %all-to-all-start.2 = ((bf16[8,272,256]{2,1,0:T(8,128)(2,1)}), bf16[8,272,256]{2,1,0:T(8,128)(2,1)S(1)}, u32[]{:S(2)}, u32[]{:S(2)}) async-start(bf16[8,272,256]{2,1,0:T(8,128)(2,1)} %get-tuple-element.33), calls=%async_computation.2 | async-start | bytes 2228224 | tf_op jit(solution)/shard_map/all_to_all | solution.py:474
  69.9 1.9 %collective-permute-start.7 = (bf16[8,64,384]{2,1,0:T(8,128)(2,1)}, bf16[8,64,384]{2,1,0:T(8,128)(2,1)S(1)}, u32[]{:S(2)}, u32[]{:S(2)}) collective-permute-start(bf16[8,64,384]{2,1,0:T(8,128)(2,1)} %all-to-all-done.1), channel_id=1, source_target_pairs={{0,64},{8,72},{16,80},{24,88},{32,96},{40,104},{48,112},{56,120},{... | collective-permute-start | bytes 1179656 | tf_op jit(solution)/shard_map/ppermute | solution.py:476
  71.9 13.9 %all-to-all-done.2.part_ref = bf16[8,272,256]{2,1,0:T(8,128)(2,1)S(1)} async-done(((bf16[8,272,256]{2,1,0:T(8,128)(2,1)}), bf16[8,272,256]{2,1,0:T(8,128)(2,1)S(1)}, u32[]{:S(2)}, u32[]{:S(2)}) %all-to-all-start.2) | async-done | bytes 1114144 | tf_op jit(solution)/shard_map/all_to_all | solution.py:474
  85.8 1.2 %merge.1 = bf16[8,256,256]{2,1,0:T(8,128)(2,1)} custom-call(bf16[8,272,256]{2,1,0:T(8,128)(2,1)S(1)} %all-to-all-done.2.part_ref), custom_call_target="tpu_custom_call" | custom-call | tf_op jit(solution)/shard_map/merge/pallas_call | solution.py:481
  87.0 3.6 %all-to-all-start.3 = ((bf16[8,256,256]{2,1,0:T(8,128)(2,1)}), bf16[8,256,256]{2,1,0:T(8,128)(2,1)S(1)}, u32[]{:S(2)}, u32[]{:S(2)}) async-start(bf16[8,256,256]{2,1,0:T(8,128)(2,1)} %merge.1), calls=%async_computation.3 | async-start | bytes 2097152 | tf_op jit(solution)/shard_map/all_to_all | solution.py:489
  90.6 1.1 select_bitcast_fusion.3
  91.7 0.1 pad_maximum_fusion.1
  91.8 2.8 %collective-permute-start.8 = (bf16[8,2,64,384]{3,2,0,1:T(8,128)(2,1)S(1)}, bf16[8,2,64,384]{3,2,0,1:T(8,128)(2,1)S(1)}, u32[]{:S(2)}, u32[]{:S(2)}) collective-permute-start(bf16[8,2,64,384]{3,2,0,1:T(8,128)(2,1)S(1)} %pad_maximum_fusion.1), channel_id=1, source_target_pairs={{0,8},{8,0},{16,24},{24,16},{32,40},{40,32},{48,56},{56,48},{64,72... | collective-permute-start | bytes 2359304 | tf_op jit(solution)/shard_map/ppermute | solution.py:478
  94.6 1.9 %collective-permute-done.8 = bf16[8,2,64,384]{3,2,0,1:T(8,128)(2,1)S(1)} collective-permute-done((bf16[8,2,64,384]{3,2,0,1:T(8,128)(2,1)S(1)}, bf16[8,2,64,384]{3,2,0,1:T(8,128)(2,1)S(1)}, u32[]{:S(2)}, u32[]{:S(2)}) %collective-permute-start.8) | collective-permute-done | bytes 786464 | tf_op jit(solution)/shard_map/ppermute | solution.py:478
  96.5 0.2 select_bitcast_fusion.1
  96.6 0.2 pad_maximum_fusion
  96.8 0.2 copy.13
  97.0 20.6 %all-to-all-done.3 = bf16[8,256,256]{2,1,0:T(8,128)(2,1)S(1)} async-done(((bf16[8,256,256]{2,1,0:T(8,128)(2,1)}), bf16[8,256,256]{2,1,0:T(8,128)(2,1)S(1)}, u32[]{:S(2)}, u32[]{:S(2)}) %all-to-all-start.3) | async-done | bytes 1048608 | tf_op jit(solution)/shard_map/all_to_all | solution.py:489
  117.6 1.4 %convolution_convert_fusion = bf16[256,384]{1,0:T(8,128)(2,1)} fusion(bf16[2048,256]{1,0:T(8,128)(2,1)S(1)} %bitcast.18, bf16[2048,384]{1,0:T(8,128)(2,1)S(1)} %bitcast.17), kind=kOutput, calls=%fused_computation.1 | convolution fusion | flops 402751488 | bytes 2818048 | tf_op jit(solution)/shard_map/dot_general | solution.py:490
  (11 shorter events, 0.1 us)
Async XLA Ops:
  3.1 29.8 %collective-permute-start = (bf16[528,256]{1,0:T(8,128)(2,1)}, bf16[528,256]{1,0:T(8,128)(2,1)S(1)}, u32[]{:S(2)}, u32[]{:S(2)}) collective-permute-start(bf16[528,256]{1,0:T(8,128)(2,1)} %get-tuple-element.20.own), channel_id=1, source_target_pairs={{0,128},{8,136},{16,144},{24,152},{32,160},{40,168},{48,176},{56,1... | collective-permute-start | bytes 811016 | tf_op jit(solution)/shard_map/ppermute | solution.py:37
  9.7 23.2 %collective-permute-start.1 = (bf16[528,256]{1,0:T(8,128)(2,1)}, bf16[528,256]{1,0:T(8,128)(2,1)S(1)}, u32[]{:S(2)}, u32[]{:S(2)}) collective-permute-start(bf16[528,256]{1,0:T(8,128)(2,1)} %get-tuple-element.20.own), channel_id=1, source_target_pairs={{0,384},{8,392},{16,400},{24,408},{32,416},{40,424},{48,432},{56,4... | collective-permute-start | bytes 811016 | tf_op jit(solution)/shard_map/ppermute | solution.py:37
  16.5 34.3 %collective-permute-start.2 = (bf16[528,256]{1,0:T(8,128)(2,1)}, bf16[528,256]{1,0:T(8,128)(2,1)S(1)}, u32[]{:S(2)}, u32[]{:S(2)}) collective-permute-start(bf16[528,256]{1,0:T(8,128)(2,1)} %get-tuple-element.20.own), channel_id=1, source_target_pairs={{0,64},{8,72},{16,80},{24,88},{32,96},{40,104},{48,112},{56,120},{... | collective-permute-start | bytes 811016 | tf_op jit(solution)/shard_map/ppermute | solution.py:37
  19.6 31.2 %collective-permute-start.3 = (bf16[528,256]{1,0:T(8,128)(2,1)}, bf16[528,256]{1,0:T(8,128)(2,1)S(1)}, u32[]{:S(2)}, u32[]{:S(2)}) collective-permute-start(bf16[528,256]{1,0:T(8,128)(2,1)} %get-tuple-element.20.own), channel_id=1, source_target_pairs={{0,448},{8,456},{16,464},{24,472},{32,480},{40,488},{48,496},{56,5... | collective-permute-start | bytes 811016 | tf_op jit(solution)/shard_map/ppermute | solution.py:37
  23.0 20.9 %all-to-all-start = ((bf16[8,256,256]{2,1,0:T(8,128)(2,1)}), bf16[8,256,256]{2,1,0:T(8,128)(2,1)S(1)}, u32[]{:S(2)}, u32[]{:S(2)}) async-start(bf16[8,256,256]{2,1,0:T(8,128)(2,1)} %get-tuple-element.25), calls=%async_computation | async-start | bytes 2097152 | tf_op jit(solution)/shard_map/all_to_all | solution.py:431
  32.9 17.9 %copy-start = (bf16[528,256]{1,0:T(8,128)(2,1)S(1)}, bf16[528,256]{1,0:T(8,128)(2,1)}, u32[]{:S(2)}) copy-start(bf16[528,256]{1,0:T(8,128)(2,1)} %get-tuple-element.20.own) | copy-start | bytes 811012
  32.9 17.9 %copy-start.1 = (s32[16,128]{1,0:T(8,128)S(1)}, s32[16,128]{1,0:T(8,128)}, u32[]{:S(2)}) copy-start(s32[16,128]{1,0:T(8,128)} %get-tuple-element.23.table) | copy-start | bytes 24580
  32.9 21.9 %collective-permute-start.4 = (bf16[528,256]{1,0:T(8,128)(2,1)S(1)}, bf16[528,256]{1,0:T(8,128)(2,1)S(1)}, u32[]{:S(2)}, u32[]{:S(2)}) collective-permute-start(bf16[528,256]{1,0:T(8,128)(2,1)S(1)} %collective-permute-done.f2), channel_id=1, source_target_pairs={{0,64},{8,72},{16,80},{24,88},{32,96},{40,104},{48,112},{56,120},{... | collective-permute-start | bytes 811016 | tf_op jit(solution)/shard_map/ppermute | solution.py:37
  35.0 19.9 %collective-permute-start.5 = (bf16[528,256]{1,0:T(8,128)(2,1)S(1)}, bf16[528,256]{1,0:T(8,128)(2,1)S(1)}, u32[]{:S(2)}, u32[]{:S(2)}) collective-permute-start(bf16[528,256]{1,0:T(8,128)(2,1)S(1)} %collective-permute-done.1.b2), channel_id=1, source_target_pairs={{0,448},{8,456},{16,464},{24,472},{32,480},{40,488},{48,496},{56,5... | collective-permute-start | bytes 811016 | tf_op jit(solution)/shard_map/ppermute | solution.py:37
  39.6 15.3 %collective-permute-start.6 = (bf16[528,256]{1,0:T(8,128)(2,1)S(1)}, bf16[528,256]{1,0:T(8,128)(2,1)S(1)}, u32[]{:S(2)}, u32[]{:S(2)}) collective-permute-start(bf16[528,256]{1,0:T(8,128)(2,1)S(1)} %broadcast_select_fusion), channel_id=1, source_target_pairs={{0,128},{8,392},{16,144},{24,408},{32,160},{40,424},{48,176},{56,4... | collective-permute-start | bytes 811016 | tf_op jit(solution)/shard_map/ppermute | solution.py:437
  43.9 20.5 %all-to-all-start.1 = ((bf16[8,64,384]{2,1,0:T(8,128)(2,1)}), bf16[8,64,384]{2,1,0:T(8,128)(2,1)}, u32[]{:S(2)}, u32[]{:S(2)}) async-start(bf16[8,64,384]{2,1,0:T(8,128)(2,1)} %get-tuple-element.32), calls=%async_computation.1 | async-start | bytes 786432 | tf_op jit(solution)/shard_map/all_to_all | solution.py:443
  64.4 21.4 %all-to-all-start.2 = ((bf16[8,272,256]{2,1,0:T(8,128)(2,1)}), bf16[8,272,256]{2,1,0:T(8,128)(2,1)S(1)}, u32[]{:S(2)}, u32[]{:S(2)}) async-start(bf16[8,272,256]{2,1,0:T(8,128)(2,1)} %get-tuple-element.33), calls=%async_computation.2 | async-start | bytes 2228224 | tf_op jit(solution)/shard_map/all_to_all | solution.py:474
  69.9 20.6 %collective-permute-start.7 = (bf16[8,64,384]{2,1,0:T(8,128)(2,1)}, bf16[8,64,384]{2,1,0:T(8,128)(2,1)S(1)}, u32[]{:S(2)}, u32[]{:S(2)}) collective-permute-start(bf16[8,64,384]{2,1,0:T(8,128)(2,1)} %all-to-all-done.1), channel_id=1, source_target_pairs={{0,64},{8,72},{16,80},{24,88},{32,96},{40,104},{48,112},{56,120},{... | collective-permute-start | bytes 1179656 | tf_op jit(solution)/shard_map/ppermute | solution.py:476
  87.0 30.6 %all-to-all-start.3 = ((bf16[8,256,256]{2,1,0:T(8,128)(2,1)}), bf16[8,256,256]{2,1,0:T(8,128)(2,1)S(1)}, u32[]{:S(2)}, u32[]{:S(2)}) async-start(bf16[8,256,256]{2,1,0:T(8,128)(2,1)} %merge.1), calls=%async_computation.3 | async-start | bytes 2097152 | tf_op jit(solution)/shard_map/all_to_all | solution.py:489
  91.8 4.7 %collective-permute-start.8 = (bf16[8,2,64,384]{3,2,0,1:T(8,128)(2,1)S(1)}, bf16[8,2,64,384]{3,2,0,1:T(8,128)(2,1)S(1)}, u32[]{:S(2)}, u32[]{:S(2)}) collective-permute-start(bf16[8,2,64,384]{3,2,0,1:T(8,128)(2,1)S(1)} %pad_maximum_fusion.1), channel_id=1, source_target_pairs={{0,8},{8,0},{16,24},{24,16},{32,40},{40,32},{48,56},{56,48},{64,72... | collective-permute-start | bytes 2359304 | tf_op jit(solution)/shard_map/ppermute | solution.py:478

commit v5 on v4

--- a/solution.py
+++ b/solution.py
@@ -426,8 +426,9 @@
     )(where, far_blocks.T, far_count[None, :], radial_width.T, w_out)
 
     count = ROW * ROW
-    f1 = along_column(kv, 1)
-    b1 = along_column(kv, -1)
+    later, table = lax.optimization_barrier((kv, table))
+    f1 = along_column(later, 1)
+    b1 = along_column(later, -1)
     q_all = lax.all_to_all(q_mine, "seq", 0, 0, axis_index_groups=row_peers())
     f2 = along_column(kv, 2)
     b2 = along_column(kv, -2)

time: 120 us -> 119 us (level)
  waiting for transfers between devices: 43.3 us -> 39.4 us
  starting transfers between devices: 55.1 us -> 56.6 us
    all_to_all x1, waiting for transfers between devices: 2.16 us -> 0.01 us  [shards(): q_all = lax.all_to_all(q_mine, 'seq', 0, 0, axis_index_groups=row_peers())]
  transfers between devices with their start and end apart: 13 -> 13, of which waited for: 5 -> 4; matrix products, arithmetic and copies ran while one was open for 2% -> 2% of each run, Pallas kernels for 11% -> 11%
where the time goes in v5:
time: 119 us; the launch traced here: 117 us
  starting transfers between devices  56.6 us (48%)
  waiting for transfers between devices  39.4 us (33%)
  Pallas kernels  16.4 us (14%)
  other arithmetic  2.22 us (2%)
  matrix products  1.42 us (1%)
    ppermute x6, starting transfers between devices, along_column(): lax.ppermute(block, 'seq', [(g, (g + ROW * distance) % count) for g in ra...  26.4 us
    all_to_all x1, waiting for transfers between devices, shards(): attention = lax.all_to_all(merged, 'head', 0, 0)  20.6 us
    all_to_all x1, waiting for transfers between devices, shards(): part = lax.all_to_all(part, 'seq', 0, 0, axis_index_groups=row_peers())  12.7 us
    all_to_all x1, starting transfers between devices, shards(): quarter = lax.all_to_all(quarter, 'head', 0, 0)  6.83 us
    all_to_all x1, starting transfers between devices, shards(): part = lax.all_to_all(part, 'seq', 0, 0, axis_index_groups=row_peers())  6.55 us
    all_to_all x1, starting transfers between devices, shards(): q_all = lax.all_to_all(q_mine, 'seq', 0, 0, axis_index_groups=row_peers())  5.26 us
    pallas_call x1, Pallas kernels, shards(): pl.pallas_call(early_kernel, out_shape=(jax.ShapeDtypeStruct((ROW, width,...  4.75 us
    pallas_call x1, Pallas kernels, shards(): pl.pallas_call(late_kernel, out_shape=(jax.ShapeDtypeStruct((ROW, width +...  4.65 us
  transfers between devices with their start and end apart: 13, of which 4 were waited for; matrix products, arithmetic and copies ran while one was open for 2% of the time, Pallas kernels for 11%

profile of v5, /device:TPU:1, one launch (start us, length us, event | category | flops | bytes accessed | tf_op | source)
XLA Modules:
  0.0 117.1 jit_solution(8856217749589903570)
XLA Ops:
  0.0 3.1 %messages.1 = (bf16[528,256]{1,0:T(8,128)(2,1)}, bf16[8,256,256]{2,1,0:T(8,128)(2,1)}) custom-call(bf16[256,256]{1,0:T(8,128)(2,1)} %k_in.1, bf16[256,256]{1,0:T(8,128)(2,1)} %v_in.1, bf16[256,256]{1,0:T(8,128)(2,1)} %q_in.1, bf16[4,256]{1,0:T(4,128)(2,1)} %tk_in.1, bf16[4,256]{1,0:T(4,128)(2,1)} %tv_in.1), custom_call_target="tpu_custom_call" | custom-call | tf_op jit(solution)/shard_map/messages/pallas_call | solution.py:394
  3.1 6.6 %collective-permute-start = (bf16[528,256]{1,0:T(8,128)(2,1)}, bf16[528,256]{1,0:T(8,128)(2,1)S(1)}, u32[]{:S(2)}, u32[]{:S(2)}) collective-permute-start(bf16[528,256]{1,0:T(8,128)(2,1)} %get-tuple-element.30.own), channel_id=1, source_target_pairs={{0,128},{8,136},{16,144},{24,152},{32,160},{40,168},{48,176},{56,1... | collective-permute-start | bytes 811016 | tf_op jit(solution)/shard_map/ppermute | solution.py:37
  9.7 6.8 %collective-permute-start.1 = (bf16[528,256]{1,0:T(8,128)(2,1)}, bf16[528,256]{1,0:T(8,128)(2,1)S(1)}, u32[]{:S(2)}, u32[]{:S(2)}) collective-permute-start(bf16[528,256]{1,0:T(8,128)(2,1)} %get-tuple-element.30.own), channel_id=1, source_target_pairs={{0,384},{8,392},{16,400},{24,408},{32,416},{40,424},{48,432},{56,4... | collective-permute-start | bytes 811016 | tf_op jit(solution)/shard_map/ppermute | solution.py:37
  16.5 5.3 %all-to-all-start = ((bf16[8,256,256]{2,1,0:T(8,128)(2,1)}), bf16[8,256,256]{2,1,0:T(8,128)(2,1)S(1)}, u32[]{:S(2)}, u32[]{:S(2)}) async-start(bf16[8,256,256]{2,1,0:T(8,128)(2,1)} %get-tuple-element.28), calls=%async_computation | async-start | bytes 2097152 | tf_op jit(solution)/shard_map/all_to_all | solution.py:432
  22.4 0.7 pad_add_fusion.where_ref
  23.1 2.7 %lists.1 = (s32[16,128]{1,0:T(8,128)}, bf16[8,64,384]{2,1,0:T(8,128)(2,1)}) custom-call(s32[3]{0:T(128)} %pad_add_fusion.where_ref, s32[29,128]{1,0:T(8,128)} %bitcast.19, s32[1,128]{1,0:T(1,128)} %bitcast.21, s32[5,64]{1,0:T(8,128)} %bitcast.20, bf16[256,3072]{1,0:T(8,128)(2,1)} %w_in.1), custom_call_target="tpu_custom_call" | custom-call | flops 40000000000 | bytes 100000 | tf_op jit(solution)/shard_map/lists/pallas_call | solution.py:410
  25.8 0.0 copy-start.1
  25.8 3.1 %collective-permute-start.2 = (bf16[528,256]{1,0:T(8,128)(2,1)S(1)}, bf16[528,256]{1,0:T(8,128)(2,1)S(1)}, u32[]{:S(2)}, u32[]{:S(2)}) collective-permute-start(bf16[528,256]{1,0:T(8,128)(2,1)S(1)} %copy-done), channel_id=1, source_target_pairs={{0,64},{8,72},{16,80},{24,88},{32,96},{40,104},{48,112},{56,120},{... | collective-permute-start | bytes 811016 | tf_op jit(solution)/shard_map/ppermute | solution.py:37
  28.9 3.4 %collective-permute-start.3 = (bf16[528,256]{1,0:T(8,128)(2,1)S(1)}, bf16[528,256]{1,0:T(8,128)(2,1)S(1)}, u32[]{:S(2)}, u32[]{:S(2)}) collective-permute-start(bf16[528,256]{1,0:T(8,128)(2,1)S(1)} %copy-done), channel_id=1, source_target_pairs={{0,448},{8,456},{16,464},{24,472},{32,480},{40,488},{48,496},{56,5... | collective-permute-start | bytes 811016 | tf_op jit(solution)/shard_map/ppermute | solution.py:37
  32.3 0.0 collective-permute-done.1.b2
  32.3 1.9 %collective-permute-start.4 = (bf16[528,256]{1,0:T(8,128)(2,1)S(1)}, bf16[528,256]{1,0:T(8,128)(2,1)S(1)}, u32[]{:S(2)}, u32[]{:S(2)}) collective-permute-start(bf16[528,256]{1,0:T(8,128)(2,1)S(1)} %collective-permute-done.f2), channel_id=1, source_target_pairs={{0,64},{8,72},{16,80},{24,88},{32,96},{40,104},{48,112},{56,120},{... | collective-permute-start | bytes 811016 | tf_op jit(solution)/shard_map/ppermute | solution.py:37
  34.3 4.6 %collective-permute-start.5 = (bf16[528,256]{1,0:T(8,128)(2,1)S(1)}, bf16[528,256]{1,0:T(8,128)(2,1)S(1)}, u32[]{:S(2)}, u32[]{:S(2)}) collective-permute-start(bf16[528,256]{1,0:T(8,128)(2,1)S(1)} %collective-permute-done.1.b2), channel_id=1, source_target_pairs={{0,448},{8,456},{16,464},{24,472},{32,480},{40,488},{48,496},{56,5... | collective-permute-start | bytes 811016 | tf_op jit(solution)/shard_map/ppermute | solution.py:37
  38.9 2.1 %collective-permute-start.6 = (bf16[528,256]{1,0:T(8,128)(2,1)S(1)}, bf16[528,256]{1,0:T(8,128)(2,1)S(1)}, u32[]{:S(2)}, u32[]{:S(2)}) collective-permute-start(bf16[528,256]{1,0:T(8,128)(2,1)S(1)} %broadcast_select_fusion), channel_id=1, source_target_pairs={{0,128},{8,392},{16,144},{24,408},{32,160},{40,424},{48,176},{56,4... | collective-permute-start | bytes 811016 | tf_op jit(solution)/shard_map/ppermute | solution.py:438
  41.1 6.8 %all-to-all-start.1 = ((bf16[8,64,384]{2,1,0:T(8,128)(2,1)}), bf16[8,64,384]{2,1,0:T(8,128)(2,1)}, u32[]{:S(2)}, u32[]{:S(2)}) async-start(bf16[8,64,384]{2,1,0:T(8,128)(2,1)} %get-tuple-element.36), calls=%async_computation.1 | async-start | bytes 786432 | tf_op jit(solution)/shard_map/all_to_all | solution.py:444
  47.9 0.0 collective-permute-done.2.f1
  47.9 4.7 %attend_early.1 = (f32[8,256,256]{2,1,0:T(8,128)S(1)}, f32[8,8,256]{2,1,0:T(8,128)S(1)}) custom-call(s32[16,128]{1,0:T(8,128)S(1)} %copy-done.1, bf16[8,256,256]{2,1,0:T(8,128)(2,1)S(1)} %all-to-all-done.q_ref, bf16[528,256]{1,0:T(8,128)(2,1)S(1)} %copy-done, bf16[528,256]{1,0:T(8,128)(2,1)S(1)} %collective-permute-done.2.f1, ...), custom_call_target="tpu_custom_call" | custom-call | flops 6000000000 | bytes 5000000 | tf_op jit(solution)/shard_map/attend_early/pallas_call | solution.py:446
  52.7 4.7 %attend_late.1 = (bf16[8,272,256]{2,1,0:T(8,128)(2,1)}, f32[8,256,256]{2,1,0:T(8,128)S(1)}, f32[8,8,256]{2,1,0:T(8,128)S(1)}) custom-call(s32[16,128]{1,0:T(8,128)S(1)} %copy-done.1, bf16[8,256,256]{2,1,0:T(8,128)(2,1)S(1)} %all-to-all-done.q_ref, bf16[528,256]{1,0:T(8,128)(2,1)S(1)} %copy-done, ...), custom_call_target="tpu_custom_call", output_to_operand_aliasing={{1}: (10, {}), {2}: (11, {})} | custom-call | flops 4000000000 | bytes 5000000 | tf_op jit(solution)/shard_map/attend_late/pallas_call | solution.py:459
  57.4 4.2 %all-to-all-done.1 = bf16[8,64,384]{2,1,0:T(8,128)(2,1)} async-done(((bf16[8,64,384]{2,1,0:T(8,128)(2,1)}), bf16[8,64,384]{2,1,0:T(8,128)(2,1)}, u32[]{:S(2)}, u32[]{:S(2)}) %all-to-all-start.1) | async-done | bytes 393248 | tf_op jit(solution)/shard_map/all_to_all | solution.py:444
  61.5 6.6 %all-to-all-start.2 = ((bf16[8,272,256]{2,1,0:T(8,128)(2,1)}), bf16[8,272,256]{2,1,0:T(8,128)(2,1)S(1)}, u32[]{:S(2)}, u32[]{:S(2)}) async-start(bf16[8,272,256]{2,1,0:T(8,128)(2,1)} %get-tuple-element.37), calls=%async_computation.2 | async-start | bytes 2228224 | tf_op jit(solution)/shard_map/all_to_all | solution.py:475
  68.1 3.1 %collective-permute-start.7 = (bf16[8,64,384]{2,1,0:T(8,128)(2,1)}, bf16[8,64,384]{2,1,0:T(8,128)(2,1)S(1)}, u32[]{:S(2)}, u32[]{:S(2)}) collective-permute-start(bf16[8,64,384]{2,1,0:T(8,128)(2,1)} %all-to-all-done.1), channel_id=1, source_target_pairs={{0,64},{8,72},{16,80},{24,88},{32,96},{40,104},{48,112},{56,120},{... | collective-permute-start | bytes 1179656 | tf_op jit(solution)/shard_map/ppermute | solution.py:477
  71.1 12.7 %all-to-all-done.2.part_ref = bf16[8,272,256]{2,1,0:T(8,128)(2,1)S(1)} async-done(((bf16[8,272,256]{2,1,0:T(8,128)(2,1)}), bf16[8,272,256]{2,1,0:T(8,128)(2,1)S(1)}, u32[]{:S(2)}, u32[]{:S(2)}) %all-to-all-start.2) | async-done | bytes 1114144 | tf_op jit(solution)/shard_map/all_to_all | solution.py:475
  83.9 1.2 %merge.1 = bf16[8,256,256]{2,1,0:T(8,128)(2,1)} custom-call(bf16[8,272,256]{2,1,0:T(8,128)(2,1)S(1)} %all-to-all-done.2.part_ref), custom_call_target="tpu_custom_call" | custom-call | tf_op jit(solution)/shard_map/merge/pallas_call | solution.py:482
  85.1 3.6 %all-to-all-start.3 = ((bf16[8,256,256]{2,1,0:T(8,128)(2,1)}), bf16[8,256,256]{2,1,0:T(8,128)(2,1)S(1)}, u32[]{:S(2)}, u32[]{:S(2)}) async-start(bf16[8,256,256]{2,1,0:T(8,128)(2,1)} %merge.1), calls=%async_computation.3 | async-start | bytes 2097152 | tf_op jit(solution)/shard_map/all_to_all | solution.py:490
  88.7 1.1 select_bitcast_fusion.3
  89.8 0.1 pad_maximum_fusion.1
  89.9 2.8 %collective-permute-start.8 = (bf16[8,2,64,384]{3,2,0,1:T(8,128)(2,1)S(1)}, bf16[8,2,64,384]{3,2,0,1:T(8,128)(2,1)S(1)}, u32[]{:S(2)}, u32[]{:S(2)}) collective-permute-start(bf16[8,2,64,384]{3,2,0,1:T(8,128)(2,1)S(1)} %pad_maximum_fusion.1), channel_id=1, source_target_pairs={{0,8},{8,0},{16,24},{24,16},{32,40},{40,32},{48,56},{56,48},{64,72... | collective-permute-start | bytes 2359304 | tf_op jit(solution)/shard_map/ppermute | solution.py:479
  92.7 1.9 %collective-permute-done.8 = bf16[8,2,64,384]{3,2,0,1:T(8,128)(2,1)S(1)} collective-permute-done((bf16[8,2,64,384]{3,2,0,1:T(8,128)(2,1)S(1)}, bf16[8,2,64,384]{3,2,0,1:T(8,128)(2,1)S(1)}, u32[]{:S(2)}, u32[]{:S(2)}) %collective-permute-start.8) | collective-permute-done | bytes 786464 | tf_op jit(solution)/shard_map/ppermute | solution.py:479
  94.6 0.2 select_bitcast_fusion.1
  94.8 0.2 pad_maximum_fusion
  94.9 0.2 copy.13
  95.1 20.6 %all-to-all-done.3 = bf16[8,256,256]{2,1,0:T(8,128)(2,1)S(1)} async-done(((bf16[8,256,256]{2,1,0:T(8,128)(2,1)}), bf16[8,256,256]{2,1,0:T(8,128)(2,1)S(1)}, u32[]{:S(2)}, u32[]{:S(2)}) %all-to-all-start.3) | async-done | bytes 1048608 | tf_op jit(solution)/shard_map/all_to_all | solution.py:490
  115.7 1.4 %convolution_convert_fusion = bf16[256,384]{1,0:T(8,128)(2,1)} fusion(bf16[2048,256]{1,0:T(8,128)(2,1)S(1)} %bitcast.18, bf16[2048,384]{1,0:T(8,128)(2,1)S(1)} %bitcast.17), kind=kOutput, calls=%fused_computation.1 | convolution fusion | flops 402751488 | bytes 2818048 | tf_op jit(solution)/shard_map/dot_general | solution.py:491
  (11 shorter events, 0.1 us)
Async XLA Ops:
  3.1 29.2 %collective-permute-start = (bf16[528,256]{1,0:T(8,128)(2,1)}, bf16[528,256]{1,0:T(8,128)(2,1)S(1)}, u32[]{:S(2)}, u32[]{:S(2)}) collective-permute-start(bf16[528,256]{1,0:T(8,128)(2,1)} %get-tuple-element.30.own), channel_id=1, source_target_pairs={{0,128},{8,136},{16,144},{24,152},{32,160},{40,168},{48,176},{56,1... | collective-permute-start | bytes 811016 | tf_op jit(solution)/shard_map/ppermute | solution.py:37
  9.7 22.6 %collective-permute-start.1 = (bf16[528,256]{1,0:T(8,128)(2,1)}, bf16[528,256]{1,0:T(8,128)(2,1)S(1)}, u32[]{:S(2)}, u32[]{:S(2)}) collective-permute-start(bf16[528,256]{1,0:T(8,128)(2,1)} %get-tuple-element.30.own), channel_id=1, source_target_pairs={{0,384},{8,392},{16,400},{24,408},{32,416},{40,424},{48,432},{56,4... | collective-permute-start | bytes 811016 | tf_op jit(solution)/shard_map/ppermute | solution.py:37
  16.5 24.6 %all-to-all-start = ((bf16[8,256,256]{2,1,0:T(8,128)(2,1)}), bf16[8,256,256]{2,1,0:T(8,128)(2,1)S(1)}, u32[]{:S(2)}, u32[]{:S(2)}) async-start(bf16[8,256,256]{2,1,0:T(8,128)(2,1)} %get-tuple-element.28), calls=%async_computation | async-start | bytes 2097152 | tf_op jit(solution)/shard_map/all_to_all | solution.py:432
  23.1 2.7 %copy-start = (bf16[528,256]{1,0:T(8,128)(2,1)S(1)}, bf16[528,256]{1,0:T(8,128)(2,1)}, u32[]{:S(2)}) copy-start(bf16[528,256]{1,0:T(8,128)(2,1)} %get-tuple-element.30.own) | copy-start | bytes 811012
  25.8 22.1 %copy-start.1 = (s32[16,128]{1,0:T(8,128)S(1)}, s32[16,128]{1,0:T(8,128)}, u32[]{:S(2)}) copy-start(s32[16,128]{1,0:T(8,128)} %get-tuple-element.26.table) | copy-start | bytes 24580
  25.8 22.1 %collective-permute-start.2 = (bf16[528,256]{1,0:T(8,128)(2,1)S(1)}, bf16[528,256]{1,0:T(8,128)(2,1)S(1)}, u32[]{:S(2)}, u32[]{:S(2)}) collective-permute-start(bf16[528,256]{1,0:T(8,128)(2,1)S(1)} %copy-done), channel_id=1, source_target_pairs={{0,64},{8,72},{16,80},{24,88},{32,96},{40,104},{48,112},{56,120},{... | collective-permute-start | bytes 811016 | tf_op jit(solution)/shard_map/ppermute | solution.py:37
  28.9 19.0 %collective-permute-start.3 = (bf16[528,256]{1,0:T(8,128)(2,1)S(1)}, bf16[528,256]{1,0:T(8,128)(2,1)S(1)}, u32[]{:S(2)}, u32[]{:S(2)}) collective-permute-start(bf16[528,256]{1,0:T(8,128)(2,1)S(1)} %copy-done), channel_id=1, source_target_pairs={{0,448},{8,456},{16,464},{24,472},{32,480},{40,488},{48,496},{56,5... | collective-permute-start | bytes 811016 | tf_op jit(solution)/shard_map/ppermute | solution.py:37
  32.3 20.3 %collective-permute-start.4 = (bf16[528,256]{1,0:T(8,128)(2,1)S(1)}, bf16[528,256]{1,0:T(8,128)(2,1)S(1)}, u32[]{:S(2)}, u32[]{:S(2)}) collective-permute-start(bf16[528,256]{1,0:T(8,128)(2,1)S(1)} %collective-permute-done.f2), channel_id=1, source_target_pairs={{0,64},{8,72},{16,80},{24,88},{32,96},{40,104},{48,112},{56,120},{... | collective-permute-start | bytes 811016 | tf_op jit(solution)/shard_map/ppermute | solution.py:37
  34.3 18.4 %collective-permute-start.5 = (bf16[528,256]{1,0:T(8,128)(2,1)S(1)}, bf16[528,256]{1,0:T(8,128)(2,1)S(1)}, u32[]{:S(2)}, u32[]{:S(2)}) collective-permute-start(bf16[528,256]{1,0:T(8,128)(2,1)S(1)} %collective-permute-done.1.b2), channel_id=1, source_target_pairs={{0,448},{8,456},{16,464},{24,472},{32,480},{40,488},{48,496},{56,5... | collective-permute-start | bytes 811016 | tf_op jit(solution)/shard_map/ppermute | solution.py:37
  38.9 13.8 %collective-permute-start.6 = (bf16[528,256]{1,0:T(8,128)(2,1)S(1)}, bf16[528,256]{1,0:T(8,128)(2,1)S(1)}, u32[]{:S(2)}, u32[]{:S(2)}) collective-permute-start(bf16[528,256]{1,0:T(8,128)(2,1)S(1)} %broadcast_select_fusion), channel_id=1, source_target_pairs={{0,128},{8,392},{16,144},{24,408},{32,160},{40,424},{48,176},{56,4... | collective-permute-start | bytes 811016 | tf_op jit(solution)/shard_map/ppermute | solution.py:438
  41.1 20.5 %all-to-all-start.1 = ((bf16[8,64,384]{2,1,0:T(8,128)(2,1)}), bf16[8,64,384]{2,1,0:T(8,128)(2,1)}, u32[]{:S(2)}, u32[]{:S(2)}) async-start(bf16[8,64,384]{2,1,0:T(8,128)(2,1)} %get-tuple-element.36), calls=%async_computation.1 | async-start | bytes 786432 | tf_op jit(solution)/shard_map/all_to_all | solution.py:444
  61.5 22.4 %all-to-all-start.2 = ((bf16[8,272,256]{2,1,0:T(8,128)(2,1)}), bf16[8,272,256]{2,1,0:T(8,128)(2,1)S(1)}, u32[]{:S(2)}, u32[]{:S(2)}) async-start(bf16[8,272,256]{2,1,0:T(8,128)(2,1)} %get-tuple-element.37), calls=%async_computation.2 | async-start | bytes 2228224 | tf_op jit(solution)/shard_map/all_to_all | solution.py:475
  68.1 20.6 %collective-permute-start.7 = (bf16[8,64,384]{2,1,0:T(8,128)(2,1)}, bf16[8,64,384]{2,1,0:T(8,128)(2,1)S(1)}, u32[]{:S(2)}, u32[]{:S(2)}) collective-permute-start(bf16[8,64,384]{2,1,0:T(8,128)(2,1)} %all-to-all-done.1), channel_id=1, source_target_pairs={{0,64},{8,72},{16,80},{24,88},{32,96},{40,104},{48,112},{56,120},{... | collective-permute-start | bytes 1179656 | tf_op jit(solution)/shard_map/ppermute | solution.py:477
  85.1 30.6 %all-to-all-start.3 = ((bf16[8,256,256]{2,1,0:T(8,128)(2,1)}), bf16[8,256,256]{2,1,0:T(8,128)(2,1)S(1)}, u32[]{:S(2)}, u32[]{:S(2)}) async-start(bf16[8,256,256]{2,1,0:T(8,128)(2,1)} %merge.1), calls=%async_computation.3 | async-start | bytes 2097152 | tf_op jit(solution)/shard_map/all_to_all | solution.py:490
  89.9 4.7 %collective-permute-start.8 = (bf16[8,2,64,384]{3,2,0,1:T(8,128)(2,1)S(1)}, bf16[8,2,64,384]{3,2,0,1:T(8,128)(2,1)S(1)}, u32[]{:S(2)}, u32[]{:S(2)}) collective-permute-start(bf16[8,2,64,384]{3,2,0,1:T(8,128)(2,1)S(1)} %pad_maximum_fusion.1), channel_id=1, source_target_pairs={{0,8},{8,0},{16,24},{24,16},{32,40},{40,32},{48,56},{56,48},{64,72... | collective-permute-start | bytes 2359304 | tf_op jit(solution)/shard_map/ppermute | solution.py:479

commit v6 on v5

--- a/solution.py
+++ b/solution.py
@@ -436,9 +436,7 @@
     f3 = along_column(f2, 1)
     b3 = along_column(b2, -1)
     far4 = lax.ppermute(
-        jnp.where(own % 2 == 0, f2, b2),
-        "seq",
-        [(g, (g + (2 * ROW if g % 2 == 0 else -2 * ROW)) % count) for g in range(count)],
+        later, "seq", [(g, (g + (4 * ROW if g % 2 == 0 else -4 * ROW)) % count) for g in range(count)]
     )
     quarter, q_all = lax.optimization_barrier((quarter, q_all))
     quarter = lax.all_to_all(quarter, "head", 0, 0)

time: 119 us -> 122 us (1.025)
  starting transfers between devices: 56.6 us -> 60.2 us
    ppermute x1, starting transfers between devices: 2.15 us -> 5.73 us  [shards(): lax.ppermute(later, 'seq', [(g, (g + (4 * ROW if g % 2 == 0 else -4 * ROW...]
    all_to_all x1, waiting for transfers between devices: 4.16 us -> 2.41 us  [shards(): quarter = lax.all_to_all(quarter, 'head', 0, 0)]
where the time goes in v6:
time: 122 us; the launch traced here: 121 us
  starting transfers between devices  60.2 us (49%)
  waiting for transfers between devices  38.6 us (32%)
  Pallas kernels  16.4 us (13%)
  other arithmetic  2.19 us (2%)
  matrix products  1.42 us (1%)
    ppermute x6, starting transfers between devices, along_column(): lax.ppermute(block, 'seq', [(g, (g + ROW * distance) % count) for g in ra...  26.4 us
    all_to_all x1, waiting for transfers between devices, shards(): attention = lax.all_to_all(merged, 'head', 0, 0)  20.4 us
    all_to_all x1, waiting for transfers between devices, shards(): part = lax.all_to_all(part, 'seq', 0, 0, axis_index_groups=row_peers())  13.9 us
    all_to_all x1, starting transfers between devices, shards(): part = lax.all_to_all(part, 'seq', 0, 0, axis_index_groups=row_peers())  7.61 us
    all_to_all x1, starting transfers between devices, shards(): quarter = lax.all_to_all(quarter, 'head', 0, 0)  6.83 us
    ppermute x1, starting transfers between devices, shards(): lax.ppermute(later, 'seq', [(g, (g + (4 * ROW if g % 2 == 0 else -4 * ROW...  5.73 us
    all_to_all x1, starting transfers between devices, shards(): q_all = lax.all_to_all(q_mine, 'seq', 0, 0, axis_index_groups=row_peers())  5.26 us
    pallas_call x1, Pallas kernels, shards(): pl.pallas_call(early_kernel, out_shape=(jax.ShapeDtypeStruct((ROW, width,...  4.76 us
  transfers between devices with their start and end apart: 13, of which 4 were waited for; matrix products, arithmetic and copies ran while one was open for 2% of the time, Pallas kernels for 11%

profile of v6, /device:TPU:1, one launch (start us, length us, event | category | flops | bytes accessed | tf_op | source)
XLA Modules:
  0.0 120.6 jit_solution(4283353373116049590)
XLA Ops:
  0.0 3.1 %messages.1 = (bf16[528,256]{1,0:T(8,128)(2,1)}, bf16[8,256,256]{2,1,0:T(8,128)(2,1)}) custom-call(bf16[256,256]{1,0:T(8,128)(2,1)} %k_in.1, bf16[256,256]{1,0:T(8,128)(2,1)} %v_in.1, bf16[256,256]{1,0:T(8,128)(2,1)} %q_in.1, bf16[4,256]{1,0:T(4,128)(2,1)} %tk_in.1, bf16[4,256]{1,0:T(4,128)(2,1)} %tv_in.1), custom_call_target="tpu_custom_call" | custom-call | tf_op jit(solution)/shard_map/messages/pallas_call | solution.py:394
  3.1 6.6 %collective-permute-start = (bf16[528,256]{1,0:T(8,128)(2,1)}, bf16[528,256]{1,0:T(8,128)(2,1)S(1)}, u32[]{:S(2)}, u32[]{:S(2)}) collective-permute-start(bf16[528,256]{1,0:T(8,128)(2,1)} %get-tuple-element.30.own), channel_id=1, source_target_pairs={{0,128},{8,136},{16,144},{24,152},{32,160},{40,168},{48,176},{56,1... | collective-permute-start | bytes 811016 | tf_op jit(solution)/shard_map/ppermute | solution.py:37
  9.7 6.8 %collective-permute-start.1 = (bf16[528,256]{1,0:T(8,128)(2,1)}, bf16[528,256]{1,0:T(8,128)(2,1)S(1)}, u32[]{:S(2)}, u32[]{:S(2)}) collective-permute-start(bf16[528,256]{1,0:T(8,128)(2,1)} %get-tuple-element.30.own), channel_id=1, source_target_pairs={{0,384},{8,392},{16,400},{24,408},{32,416},{40,424},{48,432},{56,4... | collective-permute-start | bytes 811016 | tf_op jit(solution)/shard_map/ppermute | solution.py:37
  16.5 5.3 %all-to-all-start = ((bf16[8,256,256]{2,1,0:T(8,128)(2,1)}), bf16[8,256,256]{2,1,0:T(8,128)(2,1)S(1)}, u32[]{:S(2)}, u32[]{:S(2)}) async-start(bf16[8,256,256]{2,1,0:T(8,128)(2,1)} %get-tuple-element.28), calls=%async_computation | async-start | bytes 2097152 | tf_op jit(solution)/shard_map/all_to_all | solution.py:432
  22.4 0.7 pad_add_fusion.where_ref
  23.1 2.7 %lists.1 = (s32[16,128]{1,0:T(8,128)}, bf16[8,64,384]{2,1,0:T(8,128)(2,1)}) custom-call(s32[3]{0:T(128)} %pad_add_fusion.where_ref, s32[29,128]{1,0:T(8,128)} %bitcast.19, s32[1,128]{1,0:T(1,128)} %bitcast.21, s32[5,64]{1,0:T(8,128)} %bitcast.20, bf16[256,3072]{1,0:T(8,128)(2,1)} %w_in.1), custom_call_target="tpu_custom_call" | custom-call | flops 40000000000 | bytes 100000 | tf_op jit(solution)/shard_map/lists/pallas_call | solution.py:410
  25.8 3.1 %collective-permute-start.2 = (bf16[528,256]{1,0:T(8,128)(2,1)S(1)}, bf16[528,256]{1,0:T(8,128)(2,1)S(1)}, u32[]{:S(2)}, u32[]{:S(2)}) collective-permute-start(bf16[528,256]{1,0:T(8,128)(2,1)S(1)} %copy-done), channel_id=1, source_target_pairs={{0,64},{8,72},{16,80},{24,88},{32,96},{40,104},{48,112},{56,120},{... | collective-permute-start | bytes 811016 | tf_op jit(solution)/shard_map/ppermute | solution.py:37
  28.9 3.4 %collective-permute-start.3 = (bf16[528,256]{1,0:T(8,128)(2,1)S(1)}, bf16[528,256]{1,0:T(8,128)(2,1)S(1)}, u32[]{:S(2)}, u32[]{:S(2)}) collective-permute-start(bf16[528,256]{1,0:T(8,128)(2,1)S(1)} %copy-done), channel_id=1, source_target_pairs={{0,448},{8,456},{16,464},{24,472},{32,480},{40,488},{48,496},{56,5... | collective-permute-start | bytes 811016 | tf_op jit(solution)/shard_map/ppermute | solution.py:37
  32.3 5.7 %collective-permute-start.6 = (bf16[528,256]{1,0:T(8,128)(2,1)S(1)}, bf16[528,256]{1,0:T(8,128)(2,1)S(1)}, u32[]{:S(2)}, u32[]{:S(2)}) collective-permute-start(bf16[528,256]{1,0:T(8,128)(2,1)S(1)} %copy-done), channel_id=1, source_target_pairs={{0,256},{8,264},{16,272},{24,280},{32,288},{40,296},{48,304},{56,3... | collective-permute-start | bytes 811016 | tf_op jit(solution)/shard_map/ppermute | solution.py:438
  38.0 0.0 collective-permute-done.f2
  38.1 1.9 %collective-permute-start.4 = (bf16[528,256]{1,0:T(8,128)(2,1)S(1)}, bf16[528,256]{1,0:T(8,128)(2,1)S(1)}, u32[]{:S(2)}, u32[]{:S(2)}) collective-permute-start(bf16[528,256]{1,0:T(8,128)(2,1)S(1)} %collective-permute-done.f2), channel_id=1, source_target_pairs={{0,64},{8,72},{16,80},{24,88},{32,96},{40,104},{48,112},{56,120},{... | collective-permute-start | bytes 811016 | tf_op jit(solution)/shard_map/ppermute | solution.py:37
  40.0 4.6 %collective-permute-start.5 = (bf16[528,256]{1,0:T(8,128)(2,1)S(1)}, bf16[528,256]{1,0:T(8,128)(2,1)S(1)}, u32[]{:S(2)}, u32[]{:S(2)}) collective-permute-start(bf16[528,256]{1,0:T(8,128)(2,1)S(1)} %collective-permute-done.1.b2), channel_id=1, source_target_pairs={{0,448},{8,456},{16,464},{24,472},{32,480},{40,488},{48,496},{56,5... | collective-permute-start | bytes 811016 | tf_op jit(solution)/shard_map/ppermute | solution.py:37
  44.6 6.8 %all-to-all-start.1 = ((bf16[8,64,384]{2,1,0:T(8,128)(2,1)}), bf16[8,64,384]{2,1,0:T(8,128)(2,1)}, u32[]{:S(2)}, u32[]{:S(2)}) async-start(bf16[8,64,384]{2,1,0:T(8,128)(2,1)} %get-tuple-element.36), calls=%async_computation.1 | async-start | bytes 786432 | tf_op jit(solution)/shard_map/all_to_all | solution.py:442
  51.4 0.0 copy-start.1
  51.4 0.7 copy-done.1
  52.1 4.8 %attend_early.1 = (f32[8,256,256]{2,1,0:T(8,128)S(1)}, f32[8,8,256]{2,1,0:T(8,128)S(1)}) custom-call(s32[16,128]{1,0:T(8,128)S(1)} %copy-done.1, bf16[8,256,256]{2,1,0:T(8,128)(2,1)S(1)} %all-to-all-done.q_ref, bf16[528,256]{1,0:T(8,128)(2,1)S(1)} %copy-done, bf16[528,256]{1,0:T(8,128)(2,1)S(1)} %collective-permute-done.2.f1, ...), custom_call_target="tpu_custom_call" | custom-call | flops 6000000000 | bytes 5000000 | tf_op jit(solution)/shard_map/attend_early/pallas_call | solution.py:444
  56.9 4.6 %attend_late.1 = (bf16[8,272,256]{2,1,0:T(8,128)(2,1)}, f32[8,256,256]{2,1,0:T(8,128)S(1)}, f32[8,8,256]{2,1,0:T(8,128)S(1)}) custom-call(s32[16,128]{1,0:T(8,128)S(1)} %copy-done.1, bf16[8,256,256]{2,1,0:T(8,128)(2,1)S(1)} %all-to-all-done.q_ref, bf16[528,256]{1,0:T(8,128)(2,1)S(1)} %copy-done, ...), custom_call_target="tpu_custom_call", output_to_operand_aliasing={{1}: (10, {}), {2}: (11, {})} | custom-call | flops 4000000000 | bytes 5000000 | tf_op jit(solution)/shard_map/attend_late/pallas_call | solution.py:457
  61.6 2.4 %all-to-all-done.1 = bf16[8,64,384]{2,1,0:T(8,128)(2,1)} async-done(((bf16[8,64,384]{2,1,0:T(8,128)(2,1)}), bf16[8,64,384]{2,1,0:T(8,128)(2,1)}, u32[]{:S(2)}, u32[]{:S(2)}) %all-to-all-start.1) | async-done | bytes 393248 | tf_op jit(solution)/shard_map/all_to_all | solution.py:442
  64.0 7.6 %all-to-all-start.2 = ((bf16[8,272,256]{2,1,0:T(8,128)(2,1)}), bf16[8,272,256]{2,1,0:T(8,128)(2,1)S(1)}, u32[]{:S(2)}, u32[]{:S(2)}) async-start(bf16[8,272,256]{2,1,0:T(8,128)(2,1)} %get-tuple-element.37), calls=%async_computation.2 | async-start | bytes 2228224 | tf_op jit(solution)/shard_map/all_to_all | solution.py:473
  71.6 1.9 %collective-permute-start.7 = (bf16[8,64,384]{2,1,0:T(8,128)(2,1)}, bf16[8,64,384]{2,1,0:T(8,128)(2,1)S(1)}, u32[]{:S(2)}, u32[]{:S(2)}) collective-permute-start(bf16[8,64,384]{2,1,0:T(8,128)(2,1)} %all-to-all-done.1), channel_id=1, source_target_pairs={{0,64},{8,72},{16,80},{24,88},{32,96},{40,104},{48,112},{56,120},{... | collective-permute-start | bytes 1179656 | tf_op jit(solution)/shard_map/ppermute | solution.py:475
  73.5 13.9 %all-to-all-done.2.part_ref = bf16[8,272,256]{2,1,0:T(8,128)(2,1)S(1)} async-done(((bf16[8,272,256]{2,1,0:T(8,128)(2,1)}), bf16[8,272,256]{2,1,0:T(8,128)(2,1)S(1)}, u32[]{:S(2)}, u32[]{:S(2)}) %all-to-all-start.2) | async-done | bytes 1114144 | tf_op jit(solution)/shard_map/all_to_all | solution.py:473
  87.4 1.2 %merge.1 = bf16[8,256,256]{2,1,0:T(8,128)(2,1)} custom-call(bf16[8,272,256]{2,1,0:T(8,128)(2,1)S(1)} %all-to-all-done.2.part_ref), custom_call_target="tpu_custom_call" | custom-call | tf_op jit(solution)/shard_map/merge/pallas_call | solution.py:480
  88.6 3.6 %all-to-all-start.3 = ((bf16[8,256,256]{2,1,0:T(8,128)(2,1)}), bf16[8,256,256]{2,1,0:T(8,128)(2,1)S(1)}, u32[]{:S(2)}, u32[]{:S(2)}) async-start(bf16[8,256,256]{2,1,0:T(8,128)(2,1)} %merge.1), calls=%async_computation.3 | async-start | bytes 2097152 | tf_op jit(solution)/shard_map/all_to_all | solution.py:488
  92.2 1.1 select_bitcast_fusion.3
  93.3 0.1 pad_maximum_fusion.1
  93.4 2.9 %collective-permute-start.8 = (bf16[8,2,64,384]{3,2,0,1:T(8,128)(2,1)S(1)}, bf16[8,2,64,384]{3,2,0,1:T(8,128)(2,1)S(1)}, u32[]{:S(2)}, u32[]{:S(2)}) collective-permute-start(bf16[8,2,64,384]{3,2,0,1:T(8,128)(2,1)S(1)} %pad_maximum_fusion.1), channel_id=1, source_target_pairs={{0,8},{8,0},{16,24},{24,16},{32,40},{40,32},{48,56},{56,48},{64,72... | collective-permute-start | bytes 2359304 | tf_op jit(solution)/shard_map/ppermute | solution.py:477
  96.3 1.9 %collective-permute-done.8 = bf16[8,2,64,384]{3,2,0,1:T(8,128)(2,1)S(1)} collective-permute-done((bf16[8,2,64,384]{3,2,0,1:T(8,128)(2,1)S(1)}, bf16[8,2,64,384]{3,2,0,1:T(8,128)(2,1)S(1)}, u32[]{:S(2)}, u32[]{:S(2)}) %collective-permute-start.8) | collective-permute-done | bytes 786464 | tf_op jit(solution)/shard_map/ppermute | solution.py:477
  98.2 0.2 select_bitcast_fusion.1
  98.4 0.2 pad_maximum_fusion
  98.6 0.2 copy.13
  98.7 20.4 %all-to-all-done.3 = bf16[8,256,256]{2,1,0:T(8,128)(2,1)S(1)} async-done(((bf16[8,256,256]{2,1,0:T(8,128)(2,1)}), bf16[8,256,256]{2,1,0:T(8,128)(2,1)S(1)}, u32[]{:S(2)}, u32[]{:S(2)}) %all-to-all-start.3) | async-done | bytes 1048608 | tf_op jit(solution)/shard_map/all_to_all | solution.py:488
  119.2 1.4 %convolution_convert_fusion = bf16[256,384]{1,0:T(8,128)(2,1)} fusion(bf16[2048,256]{1,0:T(8,128)(2,1)S(1)} %bitcast.18, bf16[2048,384]{1,0:T(8,128)(2,1)S(1)} %bitcast.17), kind=kOutput, calls=%fused_computation.1 | convolution fusion | flops 402751488 | bytes 2818048 | tf_op jit(solution)/shard_map/dot_general | solution.py:489
  (10 shorter events, 0.0 us)
Async XLA Ops:
  3.1 35.0 %collective-permute-start = (bf16[528,256]{1,0:T(8,128)(2,1)}, bf16[528,256]{1,0:T(8,128)(2,1)S(1)}, u32[]{:S(2)}, u32[]{:S(2)}) collective-permute-start(bf16[528,256]{1,0:T(8,128)(2,1)} %get-tuple-element.30.own), channel_id=1, source_target_pairs={{0,128},{8,136},{16,144},{24,152},{32,160},{40,168},{48,176},{56,1... | collective-permute-start | bytes 811016 | tf_op jit(solution)/shard_map/ppermute | solution.py:37
  9.7 28.3 %collective-permute-start.1 = (bf16[528,256]{1,0:T(8,128)(2,1)}, bf16[528,256]{1,0:T(8,128)(2,1)S(1)}, u32[]{:S(2)}, u32[]{:S(2)}) collective-permute-start(bf16[528,256]{1,0:T(8,128)(2,1)} %get-tuple-element.30.own), channel_id=1, source_target_pairs={{0,384},{8,392},{16,400},{24,408},{32,416},{40,424},{48,432},{56,4... | collective-permute-start | bytes 811016 | tf_op jit(solution)/shard_map/ppermute | solution.py:37
  16.5 28.1 %all-to-all-start = ((bf16[8,256,256]{2,1,0:T(8,128)(2,1)}), bf16[8,256,256]{2,1,0:T(8,128)(2,1)S(1)}, u32[]{:S(2)}, u32[]{:S(2)}) async-start(bf16[8,256,256]{2,1,0:T(8,128)(2,1)} %get-tuple-element.28), calls=%async_computation | async-start | bytes 2097152 | tf_op jit(solution)/shard_map/all_to_all | solution.py:432
  23.1 2.7 %copy-start = (bf16[528,256]{1,0:T(8,128)(2,1)S(1)}, bf16[528,256]{1,0:T(8,128)(2,1)}, u32[]{:S(2)}) copy-start(bf16[528,256]{1,0:T(8,128)(2,1)} %get-tuple-element.30.own) | copy-start | bytes 811012
  25.8 25.6 %collective-permute-start.2 = (bf16[528,256]{1,0:T(8,128)(2,1)S(1)}, bf16[528,256]{1,0:T(8,128)(2,1)S(1)}, u32[]{:S(2)}, u32[]{:S(2)}) collective-permute-start(bf16[528,256]{1,0:T(8,128)(2,1)S(1)} %copy-done), channel_id=1, source_target_pairs={{0,64},{8,72},{16,80},{24,88},{32,96},{40,104},{48,112},{56,120},{... | collective-permute-start | bytes 811016 | tf_op jit(solution)/shard_map/ppermute | solution.py:37
  28.9 22.5 %collective-permute-start.3 = (bf16[528,256]{1,0:T(8,128)(2,1)S(1)}, bf16[528,256]{1,0:T(8,128)(2,1)S(1)}, u32[]{:S(2)}, u32[]{:S(2)}) collective-permute-start(bf16[528,256]{1,0:T(8,128)(2,1)S(1)} %copy-done), channel_id=1, source_target_pairs={{0,448},{8,456},{16,464},{24,472},{32,480},{40,488},{48,496},{56,5... | collective-permute-start | bytes 811016 | tf_op jit(solution)/shard_map/ppermute | solution.py:37
  32.3 24.6 %collective-permute-start.6 = (bf16[528,256]{1,0:T(8,128)(2,1)S(1)}, bf16[528,256]{1,0:T(8,128)(2,1)S(1)}, u32[]{:S(2)}, u32[]{:S(2)}) collective-permute-start(bf16[528,256]{1,0:T(8,128)(2,1)S(1)} %copy-done), channel_id=1, source_target_pairs={{0,256},{8,264},{16,272},{24,280},{32,288},{40,296},{48,304},{56,3... | collective-permute-start | bytes 811016 | tf_op jit(solution)/shard_map/ppermute | solution.py:438
  38.1 18.8 %collective-permute-start.4 = (bf16[528,256]{1,0:T(8,128)(2,1)S(1)}, bf16[528,256]{1,0:T(8,128)(2,1)S(1)}, u32[]{:S(2)}, u32[]{:S(2)}) collective-permute-start(bf16[528,256]{1,0:T(8,128)(2,1)S(1)} %collective-permute-done.f2), channel_id=1, source_target_pairs={{0,64},{8,72},{16,80},{24,88},{32,96},{40,104},{48,112},{56,120},{... | collective-permute-start | bytes 811016 | tf_op jit(solution)/shard_map/ppermute | solution.py:37
  40.0 16.9 %collective-permute-start.5 = (bf16[528,256]{1,0:T(8,128)(2,1)S(1)}, bf16[528,256]{1,0:T(8,128)(2,1)S(1)}, u32[]{:S(2)}, u32[]{:S(2)}) collective-permute-start(bf16[528,256]{1,0:T(8,128)(2,1)S(1)} %collective-permute-done.1.b2), channel_id=1, source_target_pairs={{0,448},{8,456},{16,464},{24,472},{32,480},{40,488},{48,496},{56,5... | collective-permute-start | bytes 811016 | tf_op jit(solution)/shard_map/ppermute | solution.py:37
  44.6 19.4 %all-to-all-start.1 = ((bf16[8,64,384]{2,1,0:T(8,128)(2,1)}), bf16[8,64,384]{2,1,0:T(8,128)(2,1)}, u32[]{:S(2)}, u32[]{:S(2)}) async-start(bf16[8,64,384]{2,1,0:T(8,128)(2,1)} %get-tuple-element.36), calls=%async_computation.1 | async-start | bytes 786432 | tf_op jit(solution)/shard_map/all_to_all | solution.py:442
  51.4 0.7 copy-start.1
  64.0 23.4 %all-to-all-start.2 = ((bf16[8,272,256]{2,1,0:T(8,128)(2,1)}), bf16[8,272,256]{2,1,0:T(8,128)(2,1)S(1)}, u32[]{:S(2)}, u32[]{:S(2)}) async-start(bf16[8,272,256]{2,1,0:T(8,128)(2,1)} %get-tuple-element.37), calls=%async_computation.2 | async-start | bytes 2228224 | tf_op jit(solution)/shard_map/all_to_all | solution.py:473
  71.6 20.6 %collective-permute-start.7 = (bf16[8,64,384]{2,1,0:T(8,128)(2,1)}, bf16[8,64,384]{2,1,0:T(8,128)(2,1)S(1)}, u32[]{:S(2)}, u32[]{:S(2)}) collective-permute-start(bf16[8,64,384]{2,1,0:T(8,128)(2,1)} %all-to-all-done.1), channel_id=1, source_target_pairs={{0,64},{8,72},{16,80},{24,88},{32,96},{40,104},{48,112},{56,120},{... | collective-permute-start | bytes 1179656 | tf_op jit(solution)/shard_map/ppermute | solution.py:475
  88.6 30.5 %all-to-all-start.3 = ((bf16[8,256,256]{2,1,0:T(8,128)(2,1)}), bf16[8,256,256]{2,1,0:T(8,128)(2,1)S(1)}, u32[]{:S(2)}, u32[]{:S(2)}) async-start(bf16[8,256,256]{2,1,0:T(8,128)(2,1)} %merge.1), calls=%async_computation.3 | async-start | bytes 2097152 | tf_op jit(solution)/shard_map/all_to_all | solution.py:488
  93.4 4.8 %collective-permute-start.8 = (bf16[8,2,64,384]{3,2,0,1:T(8,128)(2,1)S(1)}, bf16[8,2,64,384]{3,2,0,1:T(8,128)(2,1)S(1)}, u32[]{:S(2)}, u32[]{:S(2)}) collective-permute-start(bf16[8,2,64,384]{3,2,0,1:T(8,128)(2,1)S(1)} %pad_maximum_fusion.1), channel_id=1, source_target_pairs={{0,8},{8,0},{16,24},{24,16},{32,40},{40,32},{48,56},{56,48},{64,72... | collective-permute-start | bytes 2359304 | tf_op jit(solution)/shard_map/ppermute | solution.py:477

commit v7 on v5

--- a/solution.py
+++ b/solution.py
@@ -251,7 +251,7 @@
 def early_kernel(table, q_ref, own, f1, b1, f2, b2, acc, stat, kv, units, sems):
     waits = start_all([(x, kv.at[i]) for i, x in enumerate((own, f1, b1, f2, b2))], sems)
     count = list_units(table, 0, len(EARLY), units)
-    for wait in waits:
+    for wait in waits[:3]:
         wait()
     offset = lax.broadcasted_iota(jnp.int32, (2 * BLK, 2 * BLK), 0) - lax.broadcasted_iota(
         jnp.int32, (2 * BLK, 2 * BLK), 1
@@ -285,6 +285,8 @@
         g = (r + NEAR - step) & (ROW - 1)
         acc[g, :, :] = jnp.zeros((2 * HD, 2 * BLK), jnp.float32)
         stat[g, :, :] = jnp.where((row == 0) | (row == 2), FLOOR, 0.0)
+    for wait in waits[3:]:
+        wait()
     walk_units(units, count, q_ref, kv, acc, stat)
 
 
@@ -297,9 +299,11 @@
         pairs.append((x.at[4 * BLK :], tiles.at[i]))
     waits = start_all(pairs, sems)
     count = list_units(table, len(EARLY), len(LATE), units)
-    for wait in waits:
+    for wait in waits[3:]:
         wait()
     set_text(tiles, table, bias, text_k, text_v)
+    for wait in waits[:3]:
+        wait()
     walk_units(units, count, q_ref, kv, acc, stat)
 
     def some_groups(step, _):

time: 119 us -> 119 us (level)
  no operation moved by 1% of the time
where the time goes in v7:
time: 119 us; the launch traced here: 117 us
  starting transfers between devices  56.6 us (48%)
  waiting for transfers between devices  40 us (34%)
  Pallas kernels  15.7 us (13%)
  other arithmetic  2.22 us (2%)
  matrix products  1.42 us (1%)
    ppermute x6, starting transfers between devices, along_column(): lax.ppermute(block, 'seq', [(g, (g + ROW * distance) % count) for g in ra...  26.4 us
    all_to_all x1, waiting for transfers between devices, shards(): attention = lax.all_to_all(merged, 'head', 0, 0)  20.6 us
    all_to_all x1, waiting for transfers between devices, shards(): part = lax.all_to_all(part, 'seq', 0, 0, axis_index_groups=row_peers())  12.7 us
    all_to_all x1, starting transfers between devices, shards(): quarter = lax.all_to_all(quarter, 'head', 0, 0)  6.83 us
    all_to_all x1, starting transfers between devices, shards(): part = lax.all_to_all(part, 'seq', 0, 0, axis_index_groups=row_peers())  6.55 us
    all_to_all x1, starting transfers between devices, shards(): q_all = lax.all_to_all(q_mine, 'seq', 0, 0, axis_index_groups=row_peers())  5.26 us
    all_to_all x1, waiting for transfers between devices, shards(): quarter = lax.all_to_all(quarter, 'head', 0, 0)  4.84 us
    pallas_call x1, Pallas kernels, shards(): pl.pallas_call(late_kernel, out_shape=(jax.ShapeDtypeStruct((ROW, width +...  4.64 us
  transfers between devices with their start and end apart: 13, of which 4 were waited for; matrix products, arithmetic and copies ran while one was open for 2% of the time, Pallas kernels for 11%

profile of v7, /device:TPU:1, one launch (start us, length us, event | category | flops | bytes accessed | tf_op | source)
XLA Modules:
  0.0 117.1 jit_solution(8373232379944593579)
XLA Ops:
  0.0 3.1 %messages.1 = (bf16[528,256]{1,0:T(8,128)(2,1)}, bf16[8,256,256]{2,1,0:T(8,128)(2,1)}) custom-call(bf16[256,256]{1,0:T(8,128)(2,1)} %k_in.1, bf16[256,256]{1,0:T(8,128)(2,1)} %v_in.1, bf16[256,256]{1,0:T(8,128)(2,1)} %q_in.1, bf16[4,256]{1,0:T(4,128)(2,1)} %tk_in.1, bf16[4,256]{1,0:T(4,128)(2,1)} %tv_in.1), custom_call_target="tpu_custom_call" | custom-call | tf_op jit(solution)/shard_map/messages/pallas_call | solution.py:398
  3.1 6.6 %collective-permute-start = (bf16[528,256]{1,0:T(8,128)(2,1)}, bf16[528,256]{1,0:T(8,128)(2,1)S(1)}, u32[]{:S(2)}, u32[]{:S(2)}) collective-permute-start(bf16[528,256]{1,0:T(8,128)(2,1)} %get-tuple-element.30.own), channel_id=1, source_target_pairs={{0,128},{8,136},{16,144},{24,152},{32,160},{40,168},{48,176},{56,1... | collective-permute-start | bytes 811016 | tf_op jit(solution)/shard_map/ppermute | solution.py:37
  9.7 6.8 %collective-permute-start.1 = (bf16[528,256]{1,0:T(8,128)(2,1)}, bf16[528,256]{1,0:T(8,128)(2,1)S(1)}, u32[]{:S(2)}, u32[]{:S(2)}) collective-permute-start(bf16[528,256]{1,0:T(8,128)(2,1)} %get-tuple-element.30.own), channel_id=1, source_target_pairs={{0,384},{8,392},{16,400},{24,408},{32,416},{40,424},{48,432},{56,4... | collective-permute-start | bytes 811016 | tf_op jit(solution)/shard_map/ppermute | solution.py:37
  16.5 5.3 %all-to-all-start = ((bf16[8,256,256]{2,1,0:T(8,128)(2,1)}), bf16[8,256,256]{2,1,0:T(8,128)(2,1)S(1)}, u32[]{:S(2)}, u32[]{:S(2)}) async-start(bf16[8,256,256]{2,1,0:T(8,128)(2,1)} %get-tuple-element.28), calls=%async_computation | async-start | bytes 2097152 | tf_op jit(solution)/shard_map/all_to_all | solution.py:436
  22.4 0.7 pad_add_fusion.where_ref
  23.1 2.7 %lists.1 = (s32[16,128]{1,0:T(8,128)}, bf16[8,64,384]{2,1,0:T(8,128)(2,1)}) custom-call(s32[3]{0:T(128)} %pad_add_fusion.where_ref, s32[29,128]{1,0:T(8,128)} %bitcast.19, s32[1,128]{1,0:T(1,128)} %bitcast.21, s32[5,64]{1,0:T(8,128)} %bitcast.20, bf16[256,3072]{1,0:T(8,128)(2,1)} %w_in.1), custom_call_target="tpu_custom_call" | custom-call | flops 40000000000 | bytes 100000 | tf_op jit(solution)/shard_map/lists/pallas_call | solution.py:414
  25.8 0.0 copy-start.1
  25.8 3.1 %collective-permute-start.2 = (bf16[528,256]{1,0:T(8,128)(2,1)S(1)}, bf16[528,256]{1,0:T(8,128)(2,1)S(1)}, u32[]{:S(2)}, u32[]{:S(2)}) collective-permute-start(bf16[528,256]{1,0:T(8,128)(2,1)S(1)} %copy-done), channel_id=1, source_target_pairs={{0,64},{8,72},{16,80},{24,88},{32,96},{40,104},{48,112},{56,120},{... | collective-permute-start | bytes 811016 | tf_op jit(solution)/shard_map/ppermute | solution.py:37
  28.9 3.4 %collective-permute-start.3 = (bf16[528,256]{1,0:T(8,128)(2,1)S(1)}, bf16[528,256]{1,0:T(8,128)(2,1)S(1)}, u32[]{:S(2)}, u32[]{:S(2)}) collective-permute-start(bf16[528,256]{1,0:T(8,128)(2,1)S(1)} %copy-done), channel_id=1, source_target_pairs={{0,448},{8,456},{16,464},{24,472},{32,480},{40,488},{48,496},{56,5... | collective-permute-start | bytes 811016 | tf_op jit(solution)/shard_map/ppermute | solution.py:37
  32.3 0.0 collective-permute-done.f2
  32.3 1.9 %collective-permute-start.4 = (bf16[528,256]{1,0:T(8,128)(2,1)S(1)}, bf16[528,256]{1,0:T(8,128)(2,1)S(1)}, u32[]{:S(2)}, u32[]{:S(2)}) collective-permute-start(bf16[528,256]{1,0:T(8,128)(2,1)S(1)} %collective-permute-done.f2), channel_id=1, source_target_pairs={{0,64},{8,72},{16,80},{24,88},{32,96},{40,104},{48,112},{56,120},{... | collective-permute-start | bytes 811016 | tf_op jit(solution)/shard_map/ppermute | solution.py:37
  34.3 4.6 %collective-permute-start.5 = (bf16[528,256]{1,0:T(8,128)(2,1)S(1)}, bf16[528,256]{1,0:T(8,128)(2,1)S(1)}, u32[]{:S(2)}, u32[]{:S(2)}) collective-permute-start(bf16[528,256]{1,0:T(8,128)(2,1)S(1)} %collective-permute-done.1.b2), channel_id=1, source_target_pairs={{0,448},{8,456},{16,464},{24,472},{32,480},{40,488},{48,496},{56,5... | collective-permute-start | bytes 811016 | tf_op jit(solution)/shard_map/ppermute | solution.py:37
  38.9 2.1 %collective-permute-start.6 = (bf16[528,256]{1,0:T(8,128)(2,1)S(1)}, bf16[528,256]{1,0:T(8,128)(2,1)S(1)}, u32[]{:S(2)}, u32[]{:S(2)}) collective-permute-start(bf16[528,256]{1,0:T(8,128)(2,1)S(1)} %broadcast_select_fusion), channel_id=1, source_target_pairs={{0,128},{8,392},{16,144},{24,408},{32,160},{40,424},{48,176},{56,4... | collective-permute-start | bytes 811016 | tf_op jit(solution)/shard_map/ppermute | solution.py:442
  41.1 6.8 %all-to-all-start.1 = ((bf16[8,64,384]{2,1,0:T(8,128)(2,1)}), bf16[8,64,384]{2,1,0:T(8,128)(2,1)}, u32[]{:S(2)}, u32[]{:S(2)}) async-start(bf16[8,64,384]{2,1,0:T(8,128)(2,1)} %get-tuple-element.36), calls=%async_computation.1 | async-start | bytes 786432 | tf_op jit(solution)/shard_map/all_to_all | solution.py:448
  47.9 0.0 collective-permute-done.2.f1
  47.9 4.1 %attend_early.1 = (f32[8,256,256]{2,1,0:T(8,128)S(1)}, f32[8,8,256]{2,1,0:T(8,128)S(1)}) custom-call(s32[16,128]{1,0:T(8,128)S(1)} %copy-done.1, bf16[8,256,256]{2,1,0:T(8,128)(2,1)S(1)} %all-to-all-done.q_ref, bf16[528,256]{1,0:T(8,128)(2,1)S(1)} %copy-done, bf16[528,256]{1,0:T(8,128)(2,1)S(1)} %collective-permute-done.2.f1, ...), custom_call_target="tpu_custom_call" | custom-call | flops 6000000000 | bytes 5000000 | tf_op jit(solution)/shard_map/attend_early/pallas_call | solution.py:450
  52.0 4.6 %attend_late.1 = (bf16[8,272,256]{2,1,0:T(8,128)(2,1)}, f32[8,256,256]{2,1,0:T(8,128)S(1)}, f32[8,8,256]{2,1,0:T(8,128)S(1)}) custom-call(s32[16,128]{1,0:T(8,128)S(1)} %copy-done.1, bf16[8,256,256]{2,1,0:T(8,128)(2,1)S(1)} %all-to-all-done.q_ref, bf16[528,256]{1,0:T(8,128)(2,1)S(1)} %copy-done, ...), custom_call_target="tpu_custom_call", output_to_operand_aliasing={{1}: (10, {}), {2}: (11, {})} | custom-call | flops 4000000000 | bytes 5000000 | tf_op jit(solution)/shard_map/attend_late/pallas_call | solution.py:463
  56.7 4.8 %all-to-all-done.1 = bf16[8,64,384]{2,1,0:T(8,128)(2,1)} async-done(((bf16[8,64,384]{2,1,0:T(8,128)(2,1)}), bf16[8,64,384]{2,1,0:T(8,128)(2,1)}, u32[]{:S(2)}, u32[]{:S(2)}) %all-to-all-start.1) | async-done | bytes 393248 | tf_op jit(solution)/shard_map/all_to_all | solution.py:448
  61.5 6.6 %all-to-all-start.2 = ((bf16[8,272,256]{2,1,0:T(8,128)(2,1)}), bf16[8,272,256]{2,1,0:T(8,128)(2,1)S(1)}, u32[]{:S(2)}, u32[]{:S(2)}) async-start(bf16[8,272,256]{2,1,0:T(8,128)(2,1)} %get-tuple-element.37), calls=%async_computation.2 | async-start | bytes 2228224 | tf_op jit(solution)/shard_map/all_to_all | solution.py:479
  68.1 3.1 %collective-permute-start.7 = (bf16[8,64,384]{2,1,0:T(8,128)(2,1)}, bf16[8,64,384]{2,1,0:T(8,128)(2,1)S(1)}, u32[]{:S(2)}, u32[]{:S(2)}) collective-permute-start(bf16[8,64,384]{2,1,0:T(8,128)(2,1)} %all-to-all-done.1), channel_id=1, source_target_pairs={{0,64},{8,72},{16,80},{24,88},{32,96},{40,104},{48,112},{56,120},{... | collective-permute-start | bytes 1179656 | tf_op jit(solution)/shard_map/ppermute | solution.py:481
  71.1 12.7 %all-to-all-done.2.part_ref = bf16[8,272,256]{2,1,0:T(8,128)(2,1)S(1)} async-done(((bf16[8,272,256]{2,1,0:T(8,128)(2,1)}), bf16[8,272,256]{2,1,0:T(8,128)(2,1)S(1)}, u32[]{:S(2)}, u32[]{:S(2)}) %all-to-all-start.2) | async-done | bytes 1114144 | tf_op jit(solution)/shard_map/all_to_all | solution.py:479
  83.9 1.2 %merge.1 = bf16[8,256,256]{2,1,0:T(8,128)(2,1)} custom-call(bf16[8,272,256]{2,1,0:T(8,128)(2,1)S(1)} %all-to-all-done.2.part_ref), custom_call_target="tpu_custom_call" | custom-call | tf_op jit(solution)/shard_map/merge/pallas_call | solution.py:486
  85.1 3.6 %all-to-all-start.3 = ((bf16[8,256,256]{2,1,0:T(8,128)(2,1)}), bf16[8,256,256]{2,1,0:T(8,128)(2,1)S(1)}, u32[]{:S(2)}, u32[]{:S(2)}) async-start(bf16[8,256,256]{2,1,0:T(8,128)(2,1)} %merge.1), calls=%async_computation.3 | async-start | bytes 2097152 | tf_op jit(solution)/shard_map/all_to_all | solution.py:494
  88.7 1.1 select_bitcast_fusion.3
  89.8 0.1 pad_maximum_fusion.1
  89.9 2.8 %collective-permute-start.8 = (bf16[8,2,64,384]{3,2,0,1:T(8,128)(2,1)S(1)}, bf16[8,2,64,384]{3,2,0,1:T(8,128)(2,1)S(1)}, u32[]{:S(2)}, u32[]{:S(2)}) collective-permute-start(bf16[8,2,64,384]{3,2,0,1:T(8,128)(2,1)S(1)} %pad_maximum_fusion.1), channel_id=1, source_target_pairs={{0,8},{8,0},{16,24},{24,16},{32,40},{40,32},{48,56},{56,48},{64,72... | collective-permute-start | bytes 2359304 | tf_op jit(solution)/shard_map/ppermute | solution.py:483
  92.7 1.9 %collective-permute-done.8 = bf16[8,2,64,384]{3,2,0,1:T(8,128)(2,1)S(1)} collective-permute-done((bf16[8,2,64,384]{3,2,0,1:T(8,128)(2,1)S(1)}, bf16[8,2,64,384]{3,2,0,1:T(8,128)(2,1)S(1)}, u32[]{:S(2)}, u32[]{:S(2)}) %collective-permute-start.8) | collective-permute-done | bytes 786464 | tf_op jit(solution)/shard_map/ppermute | solution.py:483
  94.6 0.2 select_bitcast_fusion.1
  94.8 0.2 pad_maximum_fusion
  94.9 0.2 copy.13
  95.1 20.6 %all-to-all-done.3 = bf16[8,256,256]{2,1,0:T(8,128)(2,1)S(1)} async-done(((bf16[8,256,256]{2,1,0:T(8,128)(2,1)}), bf16[8,256,256]{2,1,0:T(8,128)(2,1)S(1)}, u32[]{:S(2)}, u32[]{:S(2)}) %all-to-all-start.3) | async-done | bytes 1048608 | tf_op jit(solution)/shard_map/all_to_all | solution.py:494
  115.7 1.4 %convolution_convert_fusion = bf16[256,384]{1,0:T(8,128)(2,1)} fusion(bf16[2048,256]{1,0:T(8,128)(2,1)S(1)} %bitcast.18, bf16[2048,384]{1,0:T(8,128)(2,1)S(1)} %bitcast.17), kind=kOutput, calls=%fused_computation.1 | convolution fusion | flops 402751488 | bytes 2818048 | tf_op jit(solution)/shard_map/dot_general | solution.py:495
  (11 shorter events, 0.1 us)
Async XLA Ops:
  3.1 29.2 %collective-permute-start = (bf16[528,256]{1,0:T(8,128)(2,1)}, bf16[528,256]{1,0:T(8,128)(2,1)S(1)}, u32[]{:S(2)}, u32[]{:S(2)}) collective-permute-start(bf16[528,256]{1,0:T(8,128)(2,1)} %get-tuple-element.30.own), channel_id=1, source_target_pairs={{0,128},{8,136},{16,144},{24,152},{32,160},{40,168},{48,176},{56,1... | collective-permute-start | bytes 811016 | tf_op jit(solution)/shard_map/ppermute | solution.py:37
  9.7 22.6 %collective-permute-start.1 = (bf16[528,256]{1,0:T(8,128)(2,1)}, bf16[528,256]{1,0:T(8,128)(2,1)S(1)}, u32[]{:S(2)}, u32[]{:S(2)}) collective-permute-start(bf16[528,256]{1,0:T(8,128)(2,1)} %get-tuple-element.30.own), channel_id=1, source_target_pairs={{0,384},{8,392},{16,400},{24,408},{32,416},{40,424},{48,432},{56,4... | collective-permute-start | bytes 811016 | tf_op jit(solution)/shard_map/ppermute | solution.py:37
  16.5 24.6 %all-to-all-start = ((bf16[8,256,256]{2,1,0:T(8,128)(2,1)}), bf16[8,256,256]{2,1,0:T(8,128)(2,1)S(1)}, u32[]{:S(2)}, u32[]{:S(2)}) async-start(bf16[8,256,256]{2,1,0:T(8,128)(2,1)} %get-tuple-element.28), calls=%async_computation | async-start | bytes 2097152 | tf_op jit(solution)/shard_map/all_to_all | solution.py:436
  23.1 2.7 %copy-start = (bf16[528,256]{1,0:T(8,128)(2,1)S(1)}, bf16[528,256]{1,0:T(8,128)(2,1)}, u32[]{:S(2)}) copy-start(bf16[528,256]{1,0:T(8,128)(2,1)} %get-tuple-element.30.own) | copy-start | bytes 811012
  25.8 22.1 %copy-start.1 = (s32[16,128]{1,0:T(8,128)S(1)}, s32[16,128]{1,0:T(8,128)}, u32[]{:S(2)}) copy-start(s32[16,128]{1,0:T(8,128)} %get-tuple-element.26.table) | copy-start | bytes 24580
  25.8 22.1 %collective-permute-start.2 = (bf16[528,256]{1,0:T(8,128)(2,1)S(1)}, bf16[528,256]{1,0:T(8,128)(2,1)S(1)}, u32[]{:S(2)}, u32[]{:S(2)}) collective-permute-start(bf16[528,256]{1,0:T(8,128)(2,1)S(1)} %copy-done), channel_id=1, source_target_pairs={{0,64},{8,72},{16,80},{24,88},{32,96},{40,104},{48,112},{56,120},{... | collective-permute-start | bytes 811016 | tf_op jit(solution)/shard_map/ppermute | solution.py:37
  28.9 19.0 %collective-permute-start.3 = (bf16[528,256]{1,0:T(8,128)(2,1)S(1)}, bf16[528,256]{1,0:T(8,128)(2,1)S(1)}, u32[]{:S(2)}, u32[]{:S(2)}) collective-permute-start(bf16[528,256]{1,0:T(8,128)(2,1)S(1)} %copy-done), channel_id=1, source_target_pairs={{0,448},{8,456},{16,464},{24,472},{32,480},{40,488},{48,496},{56,5... | collective-permute-start | bytes 811016 | tf_op jit(solution)/shard_map/ppermute | solution.py:37
  32.3 19.7 %collective-permute-start.4 = (bf16[528,256]{1,0:T(8,128)(2,1)S(1)}, bf16[528,256]{1,0:T(8,128)(2,1)S(1)}, u32[]{:S(2)}, u32[]{:S(2)}) collective-permute-start(bf16[528,256]{1,0:T(8,128)(2,1)S(1)} %collective-permute-done.f2), channel_id=1, source_target_pairs={{0,64},{8,72},{16,80},{24,88},{32,96},{40,104},{48,112},{56,120},{... | collective-permute-start | bytes 811016 | tf_op jit(solution)/shard_map/ppermute | solution.py:37
  34.3 17.8 %collective-permute-start.5 = (bf16[528,256]{1,0:T(8,128)(2,1)S(1)}, bf16[528,256]{1,0:T(8,128)(2,1)S(1)}, u32[]{:S(2)}, u32[]{:S(2)}) collective-permute-start(bf16[528,256]{1,0:T(8,128)(2,1)S(1)} %collective-permute-done.1.b2), channel_id=1, source_target_pairs={{0,448},{8,456},{16,464},{24,472},{32,480},{40,488},{48,496},{56,5... | collective-permute-start | bytes 811016 | tf_op jit(solution)/shard_map/ppermute | solution.py:37
  38.9 13.1 %collective-permute-start.6 = (bf16[528,256]{1,0:T(8,128)(2,1)S(1)}, bf16[528,256]{1,0:T(8,128)(2,1)S(1)}, u32[]{:S(2)}, u32[]{:S(2)}) collective-permute-start(bf16[528,256]{1,0:T(8,128)(2,1)S(1)} %broadcast_select_fusion), channel_id=1, source_target_pairs={{0,128},{8,392},{16,144},{24,408},{32,160},{40,424},{48,176},{56,4... | collective-permute-start | bytes 811016 | tf_op jit(solution)/shard_map/ppermute | solution.py:442
  41.1 20.5 %all-to-all-start.1 = ((bf16[8,64,384]{2,1,0:T(8,128)(2,1)}), bf16[8,64,384]{2,1,0:T(8,128)(2,1)}, u32[]{:S(2)}, u32[]{:S(2)}) async-start(bf16[8,64,384]{2,1,0:T(8,128)(2,1)} %get-tuple-element.36), calls=%async_computation.1 | async-start | bytes 786432 | tf_op jit(solution)/shard_map/all_to_all | solution.py:448
  61.5 22.4 %all-to-all-start.2 = ((bf16[8,272,256]{2,1,0:T(8,128)(2,1)}), bf16[8,272,256]{2,1,0:T(8,128)(2,1)S(1)}, u32[]{:S(2)}, u32[]{:S(2)}) async-start(bf16[8,272,256]{2,1,0:T(8,128)(2,1)} %get-tuple-element.37), calls=%async_computation.2 | async-start | bytes 2228224 | tf_op jit(solution)/shard_map/all_to_all | solution.py:479
  68.1 20.6 %collective-permute-start.7 = (bf16[8,64,384]{2,1,0:T(8,128)(2,1)}, bf16[8,64,384]{2,1,0:T(8,128)(2,1)S(1)}, u32[]{:S(2)}, u32[]{:S(2)}) collective-permute-start(bf16[8,64,384]{2,1,0:T(8,128)(2,1)} %all-to-all-done.1), channel_id=1, source_target_pairs={{0,64},{8,72},{16,80},{24,88},{32,96},{40,104},{48,112},{56,120},{... | collective-permute-start | bytes 1179656 | tf_op jit(solution)/shard_map/ppermute | solution.py:481
  85.1 30.6 %all-to-all-start.3 = ((bf16[8,256,256]{2,1,0:T(8,128)(2,1)}), bf16[8,256,256]{2,1,0:T(8,128)(2,1)S(1)}, u32[]{:S(2)}, u32[]{:S(2)}) async-start(bf16[8,256,256]{2,1,0:T(8,128)(2,1)} %merge.1), calls=%async_computation.3 | async-start | bytes 2097152 | tf_op jit(solution)/shard_map/all_to_all | solution.py:494
  89.9 4.7 %collective-permute-start.8 = (bf16[8,2,64,384]{3,2,0,1:T(8,128)(2,1)S(1)}, bf16[8,2,64,384]{3,2,0,1:T(8,128)(2,1)S(1)}, u32[]{:S(2)}, u32[]{:S(2)}) collective-permute-start(bf16[8,2,64,384]{3,2,0,1:T(8,128)(2,1)S(1)} %pad_maximum_fusion.1), channel_id=1, source_target_pairs={{0,8},{8,0},{16,24},{24,16},{32,40},{40,32},{48,56},{56,48},{64,72... | collective-permute-start | bytes 2359304 | tf_op jit(solution)/shard_map/ppermute | solution.py:483
